TPU v7x, 32 devices: a whole 2x2x4 slice. The times are simulated.
32 devices in a mesh: chan: 4 (over z), win: 8 (over y, x, core).
Axes of the slice: x: 2, y: 2, z: 4, core: 2. Of those that a mesh axis runs over, the one named last changes fastest.
Arguments:
- spectra: bfloat16 [2, 128, 128, 384], P(None, 'win', 'chan'), may hold values from -6 to 6
- valid: int32 [128, 128], P('win', 'chan'), may hold values 0 or 1
- source_block: int32 [4], replicated, may hold values from 0 to 3, as said below
Outputs:
- linear_stack: float32 [128, 128, 1024], P('win', 'chan')
- phase_weighted: float32 [128, 128, 1024], P('win', 'chan')
Inputs may be any that keep to these rules, and one draw needn't show every extreme that they name: The entries of source_block are distinct group numbers; group g holds the channels g * 32 up to g * 32 + 31.
All inputs are finite; a program needn't handle non-finite values. No bound on the sum of `valid` on one device may be relied on, other than what follows from the above.
Results may differ from a plain program's by a relative error of at most 0.00032.
Values may be sent and summed in bfloat16 or wider, within the bound.
No kernel may reach another device: no remote copies, remote signals or barrier semaphores. Data moves between devices by JAX's collectives and lax.ppermute only.
A program may use at most 128 MiB of HBM per device.

v0:
```python
import math

import jax
import jax.numpy as jnp
from jax import lax
from jax.sharding import PartitionSpec as P

LAGS = 1024
SRC_W = 128


lowest_bin = 60
window_samples = 15000
amp_eps = 1e-05
phase_floor = 0.5


def from_root(block, axis, source):
    block = jnp.where(lax.axis_index(axis) == source, block, jnp.zeros_like(block))
    return lax.psum(block, axis)


def prepare(spectra, valid):
    real_part = spectra[0].astype(jnp.float32)
    imag_part = spectra[1].astype(jnp.float32)
    power = real_part * real_part + imag_part * imag_part
    scale_amp = jnp.sqrt(jnp.mean(power, axis=-1, keepdims=True) + amp_eps)
    weight = valid.astype(jnp.float32)[:, :, None]
    paired = jnp.stack([real_part, imag_part])
    white = (paired * (weight / scale_amp)).astype(jnp.bfloat16)
    unit = (paired * (weight / jnp.maximum(jnp.sqrt(power), phase_floor))).astype(jnp.bfloat16)
    return (white, unit)


def lag_table(freq, lags):
    bins = lowest_bin + jnp.arange(freq, dtype=jnp.int32)
    shifts = jnp.arange(lags, dtype=jnp.int32) - lags // 2
    phase = jnp.mod(bins[:, None] * shifts[None, :], window_samples)
    theta = phase.astype(jnp.float32) * (2.0 * math.pi / window_samples)
    return jnp.concatenate([jnp.cos(theta), jnp.sin(theta)], axis=0)


def cross(source, receiver):
    turned = jnp.stack([receiver[1], -receiver[0]])
    real_sum = jnp.einsum("kwsf,kwrf->srf", source, receiver, preferred_element_type=jnp.float32)
    imag_sum = jnp.einsum("kwsf,kwrf->srf", source, turned, preferred_element_type=jnp.float32)
    return (real_sum, imag_sum)


def finish(rows, counts, table, windows, freq):
    den = jnp.maximum(counts, 1.0)[:, :, None]
    mean_re = rows[:, 0] / den
    mean_im = rows[:, 1] / den
    coher = (rows[:, 2] * rows[:, 2] + rows[:, 3] * rows[:, 3]) / (den * den)
    linear_part = jnp.concatenate([mean_re, -mean_im], axis=-1)
    weighted = linear_part * jnp.concatenate([coher, coher], axis=-1)
    both = jnp.stack([linear_part, weighted])
    shape = both.shape
    lagged = jnp.dot(
        both.reshape(-1, shape[-1]),
        table,
        precision=lax.Precision.HIGHEST,
        preferred_element_type=jnp.float32,
    ).reshape(shape[0], shape[1], shape[2], -1)
    factor = math.sqrt(windows / freq)
    return (lagged[0] * factor, lagged[1] * (factor * windows))


def body(spectra, valid, source_block):
    win_dev = spectra.shape[1]
    freq = spectra.shape[3]
    win_count = lax.axis_size("win")
    recv_mask = valid.astype(jnp.bfloat16)
    white, unit = prepare(spectra, valid)

    def fetch(carry, owner):
        got = (
            from_root(white, "chan", owner),
            from_root(unit, "chan", owner),
            from_root(recv_mask, "chan", owner),
        )
        return (carry, got)

    unused, fetched = lax.scan(fetch, jnp.zeros((), jnp.int32), source_block)
    src_white = jnp.moveaxis(fetched[0], 0, 2).reshape(2, win_dev, SRC_W, freq)
    src_unit = jnp.moveaxis(fetched[1], 0, 2).reshape(2, win_dev, SRC_W, freq)
    src_mask = jnp.moveaxis(fetched[2], 0, 1).reshape(win_dev, SRC_W)
    lin_re, lin_im = cross(src_white, white)
    pha_re, pha_im = cross(src_unit, unit)
    rows = lax.psum_scatter(
        jnp.stack([lin_re, lin_im, pha_re, pha_im], axis=1), "win", scatter_dimension=0, tiled=True
    )
    pair_total = jnp.einsum("ws,wr->sr", src_mask, recv_mask, preferred_element_type=jnp.float32)
    counts = lax.psum_scatter(pair_total, "win", scatter_dimension=0, tiled=True)
    table = lag_table(freq, LAGS)
    return finish(rows, counts, table, win_dev * win_count, freq)


def solution(mesh):
    placed = (P(None, "win", "chan", None), P("win", "chan"), P())
    return jax.shard_map(
        body,
        mesh=mesh,
        in_specs=placed,
        out_specs=(P("win", "chan", None), P("win", "chan", None)),
        check_vma=False,
    )
```

profile of v0, /device:TPU:1, one launch (start us, length us, event | category | flops | bytes accessed | tf_op | source)
XLA Modules:
  0.0 574.5 jit_solution(15630373680759741384)
XLA Ops:
  8.8 2.2 slice_convert_fusion.1
  11.0 1.6 fusion.18
  12.7 1.4 multiply_convert_fusion.1
  14.0 302.9 %while.14 = (s32[]{:T(128)}, bf16[4,2,16,32,384]{4,3,0,2,1:T(8,128)(2,1)}, bf16[4,2,16,32,384]{4,3,0,2,1:T(8,128)(2,1)}, bf16[4,16,32]{2,1,0:T(8,128)(2,1)S(1)},...) while((s32[]{:T(128)}, ...), condition=%wide.region_5.6_spmd, body=%wide.region_1.5_spmd.sunk | while | flops 1573894 | bytes 15741141 | solution.py:84
  17.3 10.9 %psum.22 = bf16[1,16,32]{2,1,0:T(8,128)(2,1)S(1)} all-reduce(bf16[1,16,32]{2,1,0:T(8,128)(2,1)S(1)} %select_bitcast_fusion.8), channel_id=1, replica_groups=mesh['chan'=4,'win'=8] {'chan'}, use_global_device_ids=true, to_apply=%region_4.4 | all-reduce | flops 512 | bytes 2048 | tf_op jit(solution)/shard_map/while/body/eval_jaxpr/psum | solution.py:20
  28.2 60.3 %all-reduce.5.cloned.1.call-done = (bf16[1,2,16,32,384]{4,3,2,1,0:T(8,128)(2,1)}, bf16[1,2,16,32,384]{4,3,2,1,0:T(8,128)(2,1)}) async-done(((bf16[1,2,16,32,384]{4,3,2,1,0:T(8,128)(2,1)}, bf16[1,2,16,32,384]{4,3,2,1,0:T(8,128)(2,1)}), (bf16[1,2,16,32,384]{4,3,2,1,0:T(8,128)(2,1)}, bf16[1,2,16,32,384]{4,3,2,1,0:T(8,128)(2,1)})) %all-reduce.5.cloned.1.call-update) | async-done | bytes 1572880 | tf_op jit(solution)/shard_map/while/body/eval_jaxpr/psum | solution.py:20
  88.5 2.8 bitcast_dynamic-update-slice_fusion.3
  94.5 9.1 %psum.22 = bf16[1,16,32]{2,1,0:T(8,128)(2,1)S(1)} all-reduce(bf16[1,16,32]{2,1,0:T(8,128)(2,1)S(1)} %select_bitcast_fusion.8), channel_id=1, replica_groups=mesh['chan'=4,'win'=8] {'chan'}, use_global_device_ids=true, to_apply=%region_4.4 | all-reduce | flops 512 | bytes 2048 | tf_op jit(solution)/shard_map/while/body/eval_jaxpr/psum | solution.py:20
  103.6 60.2 %all-reduce.5.cloned.1.call-done = (bf16[1,2,16,32,384]{4,3,2,1,0:T(8,128)(2,1)}, bf16[1,2,16,32,384]{4,3,2,1,0:T(8,128)(2,1)}) async-done(((bf16[1,2,16,32,384]{4,3,2,1,0:T(8,128)(2,1)}, bf16[1,2,16,32,384]{4,3,2,1,0:T(8,128)(2,1)}), (bf16[1,2,16,32,384]{4,3,2,1,0:T(8,128)(2,1)}, bf16[1,2,16,32,384]{4,3,2,1,0:T(8,128)(2,1)})) %all-reduce.5.cloned.1.call-update) | async-done | bytes 1572880 | tf_op jit(solution)/shard_map/while/body/eval_jaxpr/psum | solution.py:20
  163.8 2.7 bitcast_dynamic-update-slice_fusion.3
  169.8 9.1 %psum.22 = bf16[1,16,32]{2,1,0:T(8,128)(2,1)S(1)} all-reduce(bf16[1,16,32]{2,1,0:T(8,128)(2,1)S(1)} %select_bitcast_fusion.8), channel_id=1, replica_groups=mesh['chan'=4,'win'=8] {'chan'}, use_global_device_ids=true, to_apply=%region_4.4 | all-reduce | flops 512 | bytes 2048 | tf_op jit(solution)/shard_map/while/body/eval_jaxpr/psum | solution.py:20
  178.9 60.2 %all-reduce.5.cloned.1.call-done = (bf16[1,2,16,32,384]{4,3,2,1,0:T(8,128)(2,1)}, bf16[1,2,16,32,384]{4,3,2,1,0:T(8,128)(2,1)}) async-done(((bf16[1,2,16,32,384]{4,3,2,1,0:T(8,128)(2,1)}, bf16[1,2,16,32,384]{4,3,2,1,0:T(8,128)(2,1)}), (bf16[1,2,16,32,384]{4,3,2,1,0:T(8,128)(2,1)}, bf16[1,2,16,32,384]{4,3,2,1,0:T(8,128)(2,1)})) %all-reduce.5.cloned.1.call-update) | async-done | bytes 1572880 | tf_op jit(solution)/shard_map/while/body/eval_jaxpr/psum | solution.py:20
  239.1 2.8 bitcast_dynamic-update-slice_fusion.3
  245.1 9.1 %psum.22 = bf16[1,16,32]{2,1,0:T(8,128)(2,1)S(1)} all-reduce(bf16[1,16,32]{2,1,0:T(8,128)(2,1)S(1)} %select_bitcast_fusion.8), channel_id=1, replica_groups=mesh['chan'=4,'win'=8] {'chan'}, use_global_device_ids=true, to_apply=%region_4.4 | all-reduce | flops 512 | bytes 2048 | tf_op jit(solution)/shard_map/while/body/eval_jaxpr/psum | solution.py:20
  254.3 59.9 %all-reduce.5.cloned.1.call-done = (bf16[1,2,16,32,384]{4,3,2,1,0:T(8,128)(2,1)}, bf16[1,2,16,32,384]{4,3,2,1,0:T(8,128)(2,1)}) async-done(((bf16[1,2,16,32,384]{4,3,2,1,0:T(8,128)(2,1)}, bf16[1,2,16,32,384]{4,3,2,1,0:T(8,128)(2,1)}), (bf16[1,2,16,32,384]{4,3,2,1,0:T(8,128)(2,1)}, bf16[1,2,16,32,384]{4,3,2,1,0:T(8,128)(2,1)})) %all-reduce.5.cloned.1.call-update) | async-done | bytes 1572880 | tf_op jit(solution)/shard_map/while/body/eval_jaxpr/psum | solution.py:20
  314.2 2.8 bitcast_dynamic-update-slice_fusion.3
  318.8 5.1 copy.31
  323.9 5.1 copy.26
  329.1 5.2 copy.28
  334.2 4.1 copy.27
  338.3 2.0 pad_maximum_fusion.4
  340.3 5.9 %copy.33 = bf16[2,16,32,384]{2,1,0,3:T(8,128)(2,1)} copy(bf16[2,16,32,384]{3,2,1,0:T(8,128)(2,1)} %pad_maximum_fusion.4) | data formatting | bytes 1572864 | tf_op jit(solution)/shard_map/stack | solution.py:44
  346.2 5.0 copy.32
  351.3 4.2 convolution_bitcast_fusion
  357.9 1.2 convolution_bitcast_fusion.2
  361.0 8.9 %pad_maximum_fusion = f32[128,4,32,384]{0,2,3,1:T(8,128)} fusion(f32[128,1,32,384]{0,2,3,1:T(8,128)S(1)} %convolution_bitcast_fusion, f32[128,1,32,384]{0,2,3,1:T(8,128)S(1)} %convolution_bitcast_fusion.1, f32[128,1,32,384]{0,2,3,1:T(8,128)S(1)} %convolution_bitcast_fusion.2, f32[128,1,32,384]{0,2,3,1:T(8,128)S(1)} %convolution_bitcast_fusion.3), kind=kLoop, calls=%fused_computation.6 | loop fusion | flops 18874368 | bytes 50331648 | tf_op jit(solution)/shard_map/stack | solution.py:91
  369.8 24.9 %copy.35 = f32[128,4,32,384]{3,2,1,0:T(8,128)} copy(f32[128,4,32,384]{0,2,3,1:T(8,128)} %pad_maximum_fusion) | data formatting | bytes 50331648 | tf_op jit(solution)/shard_map/stack | solution.py:91
  394.8 6.4 %fusion.9 = (f32[384,1024]{1,0:T(8,128)S(1)}, f32[384,1024]{1,0:T(8,128)S(1)}) fusion(s32[1024]{0:T(1024)S(1)} %iota_add_fusion, s32[384]{0:T(512)S(1)} %iota_add_fusion.1), kind=kLoop, calls=%fused_computation.28 | loop fusion | flops 3538944 | bytes 3151360 | tf_op jit(solution)/shard_map/cos | solution.py:40
  401.9 149.8 %reduce-scatter.3.cloned.1.call-done = f32[16,4,32,384]{3,2,1,0:T(8,128)} async-done(((f32[128,4,32,384]{3,2,1,0:T(8,128)}), f32[16,4,32,384]{3,2,1,0:T(8,128)}) %reduce-scatter.3.cloned.1.call-update) | async-done | bytes 3145744 | tf_op jit(solution)/shard_map/reduce_scatter | solution.py:90
  551.7 2.1 fusion.17
  554.5 10.4 %fusion = f32[1024,1024]{1,0:T(8,128)S(1)} fusion(f32[1024,768]{1,0:T(8,128)S(1)} %bitcast.100, f32[384,1024]{1,0:T(8,128)S(1)} %get-tuple-element.105, f32[384,1024]{1,0:T(8,128)S(1)} %get-tuple-element.104), kind=kOutput, calls=%fused_computation.8 | convolution fusion | flops 9664462848 | bytes 10485760 | tf_op jit(solution)/shard_map/dot_general | solution.py:59
  564.9 2.5 slice_multiply_fusion
  (63 shorter events, 18.6 us)
Async XLA Ops:
  8.0 4.6 copy-start.4
  11.0 3.0 copy-start.5
  14.0 74.5 %all-reduce.5.cloned.1.call-start = ((), (), s32[]{:S(2)}) async-start(), calls=%async_computation.4 | async-start | bytes 3145728 | tf_op jit(solution)/shard_map/while/body/eval_jaxpr/psum | solution.py:20
  91.3 72.6 %all-reduce.5.cloned.1.call-start = ((), (), s32[]{:S(2)}) async-start(), calls=%async_computation.4 | async-start | bytes 3145728 | tf_op jit(solution)/shard_map/while/body/eval_jaxpr/psum | solution.py:20
  166.6 72.5 %all-reduce.5.cloned.1.call-start = ((), (), s32[]{:S(2)}) async-start(), calls=%async_computation.4 | async-start | bytes 3145728 | tf_op jit(solution)/shard_map/while/body/eval_jaxpr/psum | solution.py:20
  241.9 72.2 %all-reduce.5.cloned.1.call-start = ((), (), s32[]{:S(2)}) async-start(), calls=%async_computation.4 | async-start | bytes 3145728 | tf_op jit(solution)/shard_map/while/body/eval_jaxpr/psum | solution.py:20
  316.9 84.3 %reduce-scatter.5.cloned.1.call-start = ((), (), s32[]{:S(2)}) async-start(), calls=%async_computation.3 | async-start | bytes 73728 | tf_op jit(solution)/shard_map/reduce_scatter | solution.py:94
  317.9 233.8 %reduce-scatter.3.cloned.1.call-start = ((), (), s32[]{:S(2)}) async-start(), calls=%async_computation.2 | async-start | bytes 28311552 | tf_op jit(solution)/shard_map/reduce_scatter | solution.py:90
  351.2 4.2 copy-start
  351.2 4.7 copy-start.2
  356.0 1.9 copy-start.3
  357.9 1.9 copy-start.1
Sparse Core Ops, SparseCore 0:
  18.0 70.4 all-reduce.4
  95.2 68.5 all-reduce.4
  170.5 68.5 all-reduce.4
  245.6 68.5 all-reduce.4
Sparse Core Ops, SparseCore 1:
  320.4 32.9 reduce-scatter.4
  394.9 156.8 reduce-scatter.2
where the time goes:
time: 576 us; the launch traced here: 574 us
  waiting for transfers between devices  391 us (68%)
  local copies, waits for them, and re-layouts  70.7 us (12%)
  blocking collectives  38.3 us (7%)
  other arithmetic  37.8 us (7%)
  matrix products  19 us (3%)
  between operations  15.3 us (3%)
    psum x4, waiting for transfers between devices, from_root(): return lax.psum(block, axis)  241 us
    reduce_scatter x1, waiting for transfers between devices, body(): lax.psum_scatter(jnp.stack([lin_re, lin_im, pha_re, pha_im], axis=1), 'wi...  150 us
    psum x4, blocking collectives, from_root(): return lax.psum(block, axis)  38.3 us
    another operation x1, local copies, waits for them, and re-layouts, body(): jnp.stack([lin_re, lin_im, pha_re, pha_im], axis=1)  24.9 us
  transfers between devices with their start and end apart: 6, of which 5 were waited for; matrix products, arithmetic and copies ran while one was open for 14% of the time, Pallas kernels for 0%

commit v1 on v0

v1 whole, which is shorter than its diff:
```python
import functools
import math

import jax
import jax.numpy as jnp
import ml_dtypes
import numpy as np
from jax import lax
from jax.experimental import pallas as pl
from jax.experimental.pallas import tpu as pltpu
from jax.sharding import PartitionSpec as P

LAGS = 1024
SRC_W = 128

lowest_bin = 60
window_samples = 15000
amp_eps = 1e-05
phase_floor = 0.5

PACK = 4
CHUNKS = (1.0,)
VMEM = 60 * 1024 * 1024


def chunk_sizes(slots):
    edges = [0]
    total = 0.0
    for share in CHUNKS:
        total += share
        edges.append(round(slots * total))
    return [edges[i + 1] - edges[i] for i in range(len(CHUNKS))]


def pack_kernel(sizes, devs, spectra_ref, valid_ref, *rest):
    outs, (wide, turned) = rest[: len(sizes)], rest[len(sizes) :]
    kinds, windows, chans, freq = spectra_ref.shape
    span = freq // PACK
    slots = span // devs
    real_part = spectra_ref[0].astype(jnp.float32)
    imag_part = spectra_ref[1].astype(jnp.float32)
    for i in range(freq // 128):
        cut = slice(i * 128, (i + 1) * 128)
        wide[i, pl.ds(0, windows * chans), :] = real_part[:, :, cut].reshape(windows * chans, 128)
        wide[i, pl.ds(windows * chans, windows * chans), :] = imag_part[:, :, cut].reshape(windows * chans, 128)
    total = jnp.sum(real_part * real_part + imag_part * imag_part, axis=-1, keepdims=True)
    lane = lax.broadcasted_iota(jnp.int32, (chans, 128), 1)
    energy = jnp.zeros((chans, 128), jnp.float32)
    for w in range(windows):
        energy = jnp.where(lane % windows == w, total[w], energy)
    scale = valid_ref[...] / jnp.sqrt(energy * (1.0 / freq) + amp_eps)
    high = scale.astype(jnp.bfloat16).astype(jnp.float32)
    middle = (scale - high).astype(jnp.bfloat16).astype(jnp.float32)
    low = scale - high - middle
    part = lane // windows
    split = jnp.where(part == 0, high, jnp.where(part == 1, middle, jnp.where(part == 2, low, 0.0)))
    for c in range(chans):
        rows = []
        for k in range(kinds):
            rows_at = pl.ds(k * windows * chans + c, windows, stride=chans)
            line = jnp.concatenate([wide[i, rows_at, :] for i in range(freq // 128)], axis=1)
            for b in range(PACK):
                moved = line if b == 0 else pltpu.roll(line, freq - b * span, 1)
                rows.append(moved[:, :128])
        flipped = jnp.concatenate(rows, axis=0).T
        turned[pl.ds(c, span, stride=chans), :] = flipped[:span]
    for d in range(devs):
        start = d * slots
        for i, out in enumerate(outs):
            block = turned[pl.ds(start * chans, sizes[i] * chans), :]
            out[d, : sizes[i]] = block.astype(jnp.bfloat16).reshape(sizes[i], chans, 128)
            if i == 0:
                out[d, sizes[0]] = split.astype(jnp.bfloat16)
            start += sizes[i]


def swap_blocks(arrays, width):
    arrays = list(arrays)
    lane = lax.broadcasted_iota(jnp.int32, arrays[0].shape, 1)
    bit = 1
    while bit < len(arrays):
        upper = (lane // (width * bit)) % 2 == 1
        for i in range(len(arrays)):
            if i & bit == 0:
                a, c = arrays[i], arrays[i | bit]
                arrays[i] = jnp.where(upper, pltpu.roll(c, width * bit, 1), a)
                arrays[i | bit] = jnp.where(upper, c, pltpu.roll(a, 128 - width * bit, 1))
        bit *= 2
    return arrays


def cross_kernel(groups, own_first, pos_ref, *rest):
    blocks = rest[:groups]
    rest = rest[groups:]
    own = blocks[0]
    if not own_first:
        own, rest = rest[0], rest[1:]
    scales = rest[:groups]
    rest = rest[groups:]
    own_scale = scales[0]
    if not own_first:
        own_scale, rest = rest[0], rest[1:]
    out, factor, cap, src_white, src_unit, recv_white, recv_unit, inv = rest
    devs, chans = own_scale.shape[0], own_scale.shape[2]
    width = 128 // 8
    parts = devs // 8
    half = parts * 128
    slots = out.shape[1] // PACK
    rows_out = out.shape[2]
    per_group = chans // rows_out
    sets = groups if own_first else groups + 1

    def opened(ref, q, part):
        return swap_blocks([ref[part * 8 + d, q].astype(jnp.float32) for d in range(8)], width)

    scale_refs = list(scales) if own_first else list(scales) + [own_scale]
    for g, ref in enumerate(scale_refs):
        for part in range(parts):
            got = opened(ref, 0, part)
            value = got[0] + got[1] + got[2]
            factor[pl.ds(g * chans, chans), pl.ds(part * 128, 128)] = value
            cap[pl.ds(g * chans, chans), pl.ds(part * 128, 128)] = jnp.where(value > 0, 1.0 / phase_floor, 0.0)
    masks = jnp.where(cap[...] > 0, 1.0, 0.0).astype(jnp.bfloat16)
    mine = 0 if own_first else groups * chans
    recv = jnp.concatenate([masks[mine : mine + chans]] * 4, axis=0)
    counts = lax.dot_general(
        masks[: groups * chans], recv, (((1,), (1,)), ((), ())), preferred_element_type=jnp.float32
    )
    inv[...] = 1.0 / jnp.maximum(counts, 1.0)
    data_refs = list(blocks) if own_first else list(blocks) + [own]

    def step(q, carry):
        for g, ref in enumerate(data_refs):
            rows = pl.ds(g * chans, chans)
            for part in range(parts):
                got = opened(ref, q, part)
                scale = factor[rows, pl.ds(part * 128, 128)]
                limit = cap[rows, pl.ds(part * 128, 128)]
                lo = pl.ds(part * 128, 128)
                hi = pl.ds(half + part * 128, 128)
                for b in range(PACK):
                    real_part, imag_part = got[b], got[PACK + b]
                    power = real_part * real_part + imag_part * imag_part
                    phase = jnp.minimum(lax.rsqrt(power), limit)
                    white_re = (real_part * scale).astype(jnp.bfloat16)
                    white_im = (imag_part * scale).astype(jnp.bfloat16)
                    unit_re = (real_part * phase).astype(jnp.bfloat16)
                    unit_im = (imag_part * phase).astype(jnp.bfloat16)
                    if g < groups:
                        src_white[b, rows, lo] = white_re
                        src_white[b, rows, hi] = white_im
                        src_unit[b, rows, lo] = unit_re
                        src_unit[b, rows, hi] = unit_im
                    if g == (0 if own_first else groups):
                        for t in range(4):
                            at = pl.ds(t * chans, chans)
                            recv_white[b, at, lo] = white_im if t % 2 else white_re
                            recv_white[b, at, hi] = -white_re if t % 2 else white_im
                        for t in range(8):
                            at = pl.ds(t * chans, chans)
                            odd = (t + t // 4) % 2
                            recv_unit[b, at, lo] = unit_im if odd else unit_re
                            recv_unit[b, at, hi] = -unit_re if odd else unit_im
        scaled = inv[...]
        lane = lax.broadcasted_iota(jnp.int32, scaled.shape, 1)
        for b in range(PACK):
            lin = lax.dot_general(
                src_white[b], recv_white[b], (((1,), (1,)), ((), ())), preferred_element_type=jnp.float32
            )
            pha = lax.dot_general(
                src_unit[b], recv_unit[b], (((1,), (1,)), ((), ())), preferred_element_type=jnp.float32
            )
            mean = lin * scaled
            one = pha[:, :128] * scaled
            two = pha[:, 128:] * scaled
            coher = one * one + two * two
            both = jnp.where(lane < 2 * chans, mean, mean * coher)
            for g in range(groups):
                for h in range(per_group):
                    at = g * chans + h * rows_out
                    out[pos_ref[g] * per_group + h, q * PACK + b] = both[at : at + rows_out]
        return carry

    lax.fori_loop(0, slots, step, 0)


def lag_kernel(pieces, tile, rows_out, windows, freq, *rest):
    refs, (table_high, table_low, linear, weighted) = rest[:pieces], rest[pieces:]
    chans = linear.shape[1]
    first = pl.program_id(0) * tile
    lin_rows, pw_rows = [], []
    factor = math.sqrt(windows / freq)
    for i in range(tile):
        got = []
        for ref in refs:
            got.append(ref[pl.ds(first + i, ref.shape[0] // rows_out, stride=rows_out), :])
        flipped = (jnp.concatenate(got, axis=0) if pieces > 1 else got[0]).T
        lin_rows.append(jnp.concatenate([flipped[:chans], flipped[chans : 2 * chans]], axis=1))
        pw_rows.append(jnp.concatenate([flipped[2 * chans : 3 * chans], flipped[3 * chans :]], axis=1))
    for rows, out, gain in ((lin_rows, linear, factor), (pw_rows, weighted, factor * windows)):
        value = jnp.concatenate(rows, axis=0) * gain
        high = value.astype(jnp.bfloat16)
        low = (value - high.astype(jnp.float32)).astype(jnp.bfloat16)
        total = jnp.dot(high, table_high[...], preferred_element_type=jnp.float32)
        total += jnp.dot(high, table_low[...], preferred_element_type=jnp.float32)
        total += jnp.dot(low, table_high[...], preferred_element_type=jnp.float32)
        out[...] = total.reshape(tile, chans, LAGS)


def lag_table(freq, devs, sizes):
    slots = freq // PACK // devs
    order = []
    start = 0
    for size in sizes:
        for d in range(devs):
            for q in range(start, start + size):
                for b in range(PACK):
                    order.append(b * (freq // PACK) + d * slots + q)
        start += size
    bins = lowest_bin + np.asarray(order, np.int64)
    shifts = np.arange(LAGS, dtype=np.int64) - LAGS // 2
    theta = np.mod(bins[:, None] * shifts[None, :], window_samples) * (2.0 * math.pi / window_samples)
    table = np.concatenate([np.cos(theta), -np.sin(theta)], axis=0).astype(np.float32)
    high = table.astype(ml_dtypes.bfloat16)
    low = (table - high.astype(np.float32)).astype(ml_dtypes.bfloat16)
    return high, low


def body(spectra, valid, source_block):
    kinds, win_dev, chans, freq = spectra.shape
    devs = lax.axis_size("win")
    stations = lax.axis_size("chan")
    groups = source_block.shape[0]
    slots = freq // PACK // devs
    sizes = chunk_sizes(slots)
    rows_out = SRC_W // devs
    windows = win_dev * devs
    own_first = stations == groups
    params = pltpu.CompilerParams(vmem_limit_bytes=VMEM)

    mask = jnp.tile(valid.astype(jnp.float32).T, (1, 128 // win_dev))
    packed = pl.pallas_call(
        functools.partial(pack_kernel, sizes, devs),
        out_shape=[
            jax.ShapeDtypeStruct((devs, n + (i == 0), chans, 128), jnp.bfloat16) for i, n in enumerate(sizes)
        ],
        scratch_shapes=[
            pltpu.VMEM((freq // 128, kinds * win_dev * chans, 128), jnp.float32),
            pltpu.VMEM((freq // PACK * chans, 128), jnp.float32),
        ],
        compiler_params=params,
        name="pack",
    )(spectra, mask)

    me = lax.axis_index("chan")
    if own_first:
        held = lax.rem(me - jnp.arange(groups, dtype=jnp.int32) + stations, stations)
        pos = jnp.argmax(source_block[None, :] == held[:, None], axis=1).astype(jnp.int32)
    else:
        pos = jnp.arange(groups, dtype=jnp.int32)

    ring = [(i, (i + 1) % stations) for i in range(stations)]
    scale_blocks = None
    pieces = []
    for i, n in enumerate(sizes):
        mine = lax.all_to_all(packed[i], "win", 0, 0, tiled=True)
        if own_first:
            got = [mine]
            for hop in range(groups - 1):
                got.append(lax.ppermute(got[-1], "chan", ring))
        else:
            every = lax.all_gather(mine, "chan")
            got = [lax.dynamic_index_in_dim(every, source_block[g], 0, False) for g in range(groups)]
            got.append(mine)
        if i == 0:
            scale_blocks = got
        rows = groups * chans if own_first else (groups + 1) * chans
        half = win_dev * devs
        last = sizes[0]
        whole = pl.BlockSpec((devs, n + (i == 0), chans, 128), lambda s: (0, 0, 0, 0))
        tail = pl.BlockSpec((devs, 1, chans, 128), lambda s: (0, last, 0, 0))
        out = pl.pallas_call(
            functools.partial(cross_kernel, groups, own_first),
            grid=(1,),
            in_specs=[pl.BlockSpec(memory_space=pltpu.SMEM)] + [whole] * len(got) + [tail] * len(got),
            out_specs=pl.BlockSpec((devs, n * PACK, rows_out, 128), lambda s: (0, 0, 0, 0)),
            out_shape=jax.ShapeDtypeStruct((devs, n * PACK, rows_out, 128), jnp.float32),
            scratch_shapes=[
                pltpu.VMEM((rows, half), jnp.float32),
                pltpu.VMEM((rows, half), jnp.float32),
                pltpu.VMEM((PACK, groups * chans, 2 * half), jnp.bfloat16),
                pltpu.VMEM((PACK, groups * chans, 2 * half), jnp.bfloat16),
                pltpu.VMEM((PACK, 4 * chans, 2 * half), jnp.bfloat16),
                pltpu.VMEM((PACK, 8 * chans, 2 * half), jnp.bfloat16),
                pltpu.VMEM((groups * chans, 128), jnp.float32),
            ],
            compiler_params=params,
            name="cross",
        )(pos, *got, *scale_blocks)
        back = lax.all_to_all(out, "win", 0, 0, tiled=True)
        pieces.append(back.reshape(devs * n * PACK * rows_out, 128))

    high, low = lag_table(freq, devs, sizes)
    tile = 4
    full = lambda shape: pl.BlockSpec(shape, lambda s: (0, 0))
    return pl.pallas_call(
        functools.partial(lag_kernel, len(pieces), tile, rows_out, windows, freq),
        grid=(rows_out // tile,),
        in_specs=[full(p.shape) for p in pieces] + [full(high.shape), full(low.shape)],
        out_specs=[pl.BlockSpec((tile, chans, LAGS), lambda s: (s, 0, 0))] * 2,
        out_shape=[jax.ShapeDtypeStruct((rows_out, chans, LAGS), jnp.float32)] * 2,
        compiler_params=params,
        name="lag",
    )(*pieces, jnp.asarray(high), jnp.asarray(low))


def solution(mesh):
    placed = (P(None, "win", "chan", None), P("win", "chan"), P())
    return jax.shard_map(
        body,
        mesh=mesh,
        in_specs=placed,
        out_specs=(P("win", "chan", None), P("win", "chan", None)),
        check_vma=False,
    )
```

time: 576 us -> 157 us (0.27)
  waiting for transfers between devices: 391 us -> 60 us
  local copies, waits for them, and re-layouts: 70.7 us -> 1.62 us
  other arithmetic: 37.8 us -> 1.53 us
  Pallas kernels: 0 us -> 28.7 us
  blocking collectives: 38.3 us -> 62.1 us
  matrix products: 19 us -> 0 us
  between operations: 15.3 us -> 0.66 us
    psum x4 -> x0, waiting for transfers between devices: 241 us -> none  [from_root(): return lax.psum(block, axis)]
    reduce_scatter x2 -> x0, waiting for transfers between devices: 150 us -> none  [the longest x1 150 us: body(): lax.psum_scatter(jnp.stack([lin_re, lin_im, pha_re, pha_im], axis=1), 'wi...]
    all_to_all x0 -> x2, blocking collectives: none -> 62.1 us  [the longest x1 44.3 us: body(): back = lax.all_to_all(out, 'win', 0, 0, tiled=True)]
    ppermute x0 -> x3, waiting for transfers between devices: none -> 60 us  [body(): got.append(lax.ppermute(got[-1], 'chan', ring))]
    psum x4 -> x0, blocking collectives: 38.3 us -> none  [from_root(): return lax.psum(block, axis)]
    another operation x3 -> x2, local copies, waits for them, and re-layouts: 36 us -> 0.69 us  [body(): mask = jnp.tile(valid.astype(jnp.float32).T, (1, 128 // win_dev))]
    pallas_call x0 -> x3, Pallas kernels: none -> 28.7 us  [the longest x1 13.4 us: body(): pl.pallas_call(functools.partial(cross_kernel, groups, own_first), grid=(...]
    dot_general x6 -> x0, matrix products: 19 us -> none  [the longest x1 10.4 us: finish(): jnp.dot(both.reshape(-1, shape[-1]), table, precision=lax.Precision.HIGHE...]
  transfers between devices with their start and end apart: 6 -> 3, of which waited for: 5 -> 3; matrix products, arithmetic and copies ran while one was open for 14% -> 1% of each run, Pallas kernels for 0% -> 0%
where the time goes in v1:
time: 157 us; the launch traced here: 156 us
  blocking collectives  62.1 us (40%)
  waiting for transfers between devices  60 us (38%)
  Pallas kernels  28.7 us (18%)
  local copies, waits for them, and re-layouts  1.62 us (1%)
    ppermute x3, waiting for transfers between devices, body(): got.append(lax.ppermute(got[-1], 'chan', ring))  60 us
    all_to_all x1, blocking collectives, body(): back = lax.all_to_all(out, 'win', 0, 0, tiled=True)  44.3 us
    all_to_all x1, blocking collectives, body(): mine = lax.all_to_all(packed[i], 'win', 0, 0, tiled=True)  17.7 us
    pallas_call x1, Pallas kernels, body(): pl.pallas_call(functools.partial(cross_kernel, groups, own_first), grid=(...  13.4 us
    pallas_call x1, Pallas kernels, body(): pl.pallas_call(functools.partial(lag_kernel, len(pieces), tile, rows_out,...  10.7 us
    pallas_call x1, Pallas kernels, body(): pl.pallas_call(functools.partial(pack_kernel, sizes, devs), out_shape=[ja...  4.55 us
  transfers between devices with their start and end apart: 3, of which 3 were waited for; matrix products, arithmetic and copies ran while one was open for 1% of the time, Pallas kernels for 0%

profile of v1, /device:TPU:1, one launch (start us, length us, event | category | flops | bytes accessed | tf_op | source)
XLA Modules:
  0.0 155.8 jit_solution(5971654132738123775)
XLA Ops:
  0.6 0.0 copy-start.4
  0.6 0.7 convert_bitcast_fusion
  1.4 0.7 copy.9.valid_ref
  2.0 4.5 %pack.1 = bf16[8,13,32,128]{3,2,1,0:T(8,128)(2,1)} custom-call(bf16[2,16,32,384]{3,2,1,0:T(8,128)(2,1)} %spectra_ref.1, f32[32,128]{1,0:T(8,128)} %copy.9.valid_ref), custom_call_target="tpu_custom_call" | custom-call | tf_op jit(solution)/shard_map/pack/pallas_call | solution.py:242
  6.6 17.7 %all_to_all.10.rest_0_.rest_4_ = bf16[8,13,32,128]{3,2,1,0:T(8,128)(2,1)S(1)} all-to-all(bf16[8,13,32,128]{3,2,1,0:T(8,128)(2,1)} %pack.1), channel_id=1, replica_groups=mesh['chan'=4,'win'=8] {'win'}, dimensions={0} | all-to-all | bytes 1703936 | tf_op jit(solution)/shard_map/all_to_all | solution.py:266
  24.3 0.0 copy-start
  24.3 1.3 collective-permute-start
  25.6 20.4 %collective-permute-done.rest_1_.rest_5_ = bf16[8,13,32,128]{3,2,1,0:T(8,128)(2,1)S(1)} collective-permute-done((bf16[8,13,32,128]{3,2,1,0:T(8,128)(2,1)S(1)}, bf16[8,13,32,128]{3,2,1,0:T(8,128)(2,1)S(1)}, u32[]{:S(2)}, u32[]{:S(2)}) %collective-permute-start) | collective-permute-done | bytes 852000 | tf_op jit(solution)/shard_map/ppermute | solution.py:270
  46.0 0.0 copy-start.1
  46.0 0.0 collective-permute-start.1
  46.0 20.7 %collective-permute-done.1.rest_2_.rest_6_ = bf16[8,13,32,128]{3,2,1,0:T(8,128)(2,1)S(1)} collective-permute-done((bf16[8,13,32,128]{3,2,1,0:T(8,128)(2,1)S(1)}, bf16[8,13,32,128]{3,2,1,0:T(8,128)(2,1)S(1)}, u32[]{:S(2)}, u32[]{:S(2)}) %collective-permute-start.1) | collective-permute-done | bytes 852000 | tf_op jit(solution)/shard_map/ppermute | solution.py:270
  66.7 0.0 copy-start.2
  66.7 0.0 collective-permute-start.2
  66.7 0.0 copy-done.4
  66.7 0.8 iota_reduce_fusion
  67.5 18.9 %collective-permute-done.2.rest_3_.rest_7_ = bf16[8,13,32,128]{3,2,1,0:T(8,128)(2,1)S(1)} collective-permute-done((bf16[8,13,32,128]{3,2,1,0:T(8,128)(2,1)S(1)}, bf16[8,13,32,128]{3,2,1,0:T(8,128)(2,1)S(1)}, u32[]{:S(2)}, u32[]{:S(2)}) %collective-permute-start.2) | collective-permute-done | bytes 852000 | tf_op jit(solution)/shard_map/ppermute | solution.py:270
  86.4 0.0 copy-start.3
  86.4 0.0 copy-done
  86.4 0.0 copy-done.1
  86.4 0.0 copy-done.2
  86.4 0.9 copy-done.3
  87.3 13.4 %cross.1 = f32[8,48,16,128]{3,2,1,0:T(8,128)} custom-call(s32[4]{0:T(128)} %get-tuple-element.3.pos_ref, bf16[8,13,32,128]{3,2,1,0:T(8,128)(2,1)} %copy-done, bf16[8,13,32,128]{3,2,1,0:T(8,128)(2,1)} %copy-done.1, bf16[8,13,32,128]{3,2,1,0:T(8,128)(2,1)} %copy-done.2, bf16[8,13,32,128]{3,2,1,0:T(8,128)(2,1)} %copy-done.3, bf16[8,13,32,128]{3,2,1,0:T(8,128)(2,1)} %copy-done, ...), custom_call_target="tpu_custom_call" | custom-call | tf_op jit(solution)/shard_map/cross/pallas_call | solution.py:282
  100.8 44.3 %all_to_all.11 = f32[8,48,16,128]{3,2,1,0:T(8,128)} all-to-all(f32[8,48,16,128]{3,2,1,0:T(8,128)} %cross.1), channel_id=1, replica_groups=mesh['chan'=4,'win'=8] {'win'}, dimensions={0} | all-to-all | bytes 6291456 | tf_op jit(solution)/shard_map/all_to_all | solution.py:300
  145.1 10.7 %lag.1 = (f32[16,32,1024]{2,1,0:T(8,128)}, f32[16,32,1024]{2,1,0:T(8,128)}) custom-call(f32[6144,128]{1,0:T(8,128)} %bitcast.4, bf16[768,1024]{1,0:T(8,128)(2,1)} %constant.20.clone.rest_1_, bf16[768,1024]{1,0:T(8,128)(2,1)} %constant.21.clone.rest_2_), custom_call_target="tpu_custom_call" | custom-call | tf_op jit(solution)/shard_map/lag/pallas_call | solution.py:306
  (2 shorter events, 0.0 us)
Async XLA Ops:
  0.6 66.1 %copy-start.4 = (s32[4]{0:T(128)S(1)}, s32[4]{0:T(128)}, u32[]{:S(2)}) copy-start(s32[4]{0:T(128)} %param.7) | copy-start | bytes 52
  24.3 62.1 %copy-start = (bf16[8,13,32,128]{3,2,1,0:T(8,128)(2,1)}, bf16[8,13,32,128]{3,2,1,0:T(8,128)(2,1)S(1)}, u32[]{:S(2)}) copy-start(bf16[8,13,32,128]{3,2,1,0:T(8,128)(2,1)S(1)} %all_to_all.10.rest_0_.rest_4_) | copy-start | bytes 2555908
  24.3 21.7 %collective-permute-start = (bf16[8,13,32,128]{3,2,1,0:T(8,128)(2,1)S(1)}, bf16[8,13,32,128]{3,2,1,0:T(8,128)(2,1)S(1)}, u32[]{:S(2)}, u32[]{:S(2)}) collective-permute-start(bf16[8,13,32,128]{3,2,1,0:T(8,128)(2,1)S(1)} %all_to_all.10.rest_0_.rest_4_), channel_id=1, source_target_pairs={{0,8},{8,16},{16,24},{24,0},{1,9},{9,17},{17,25},{25,1},{2,10},{10... | collective-permute-start | bytes 2555912 | tf_op jit(solution)/shard_map/ppermute | solution.py:270
  46.0 40.4 %copy-start.1 = (bf16[8,13,32,128]{3,2,1,0:T(8,128)(2,1)}, bf16[8,13,32,128]{3,2,1,0:T(8,128)(2,1)S(1)}, u32[]{:S(2)}) copy-start(bf16[8,13,32,128]{3,2,1,0:T(8,128)(2,1)S(1)} %collective-permute-done.rest_1_.rest_5_) | copy-start | bytes 2555908
  46.0 20.7 %collective-permute-start.1 = (bf16[8,13,32,128]{3,2,1,0:T(8,128)(2,1)S(1)}, bf16[8,13,32,128]{3,2,1,0:T(8,128)(2,1)S(1)}, u32[]{:S(2)}, u32[]{:S(2)}) collective-permute-start(bf16[8,13,32,128]{3,2,1,0:T(8,128)(2,1)S(1)} %collective-permute-done.rest_1_.rest_5_), channel_id=1, source_target_pairs={{0,8},{8,16},{16,24},{24,0},{1,9},{9,17},{17,25},{25,1},{2,10},{10... | collective-permute-start | bytes 2555912 | tf_op jit(solution)/shard_map/ppermute | solution.py:270
  66.7 19.8 %copy-start.2 = (bf16[8,13,32,128]{3,2,1,0:T(8,128)(2,1)}, bf16[8,13,32,128]{3,2,1,0:T(8,128)(2,1)S(1)}, u32[]{:S(2)}) copy-start(bf16[8,13,32,128]{3,2,1,0:T(8,128)(2,1)S(1)} %collective-permute-done.1.rest_2_.rest_6_) | copy-start | bytes 2555908
  66.7 19.8 %collective-permute-start.2 = (bf16[8,13,32,128]{3,2,1,0:T(8,128)(2,1)S(1)}, bf16[8,13,32,128]{3,2,1,0:T(8,128)(2,1)S(1)}, u32[]{:S(2)}, u32[]{:S(2)}) collective-permute-start(bf16[8,13,32,128]{3,2,1,0:T(8,128)(2,1)S(1)} %collective-permute-done.1.rest_2_.rest_6_), channel_id=1, source_target_pairs={{0,8},{8,16},{16,24},{24,0},{1,9},{9,17},{17,25},{25,1},{2,10},{10... | collective-permute-start | bytes 2555912 | tf_op jit(solution)/shard_map/ppermute | solution.py:270
  86.4 0.9 copy-start.3

commit v2 on v1

--- a/solution.py
+++ b/solution.py
@@ -18,9 +18,18 @@
 amp_eps = 1e-05
 phase_floor = 0.5
 
+ROWS = 3
 PACK = 4
-CHUNKS = (1.0,)
+CHUNKS = (1 / 2, 1 / 2)
+W_IN = 1
+W_Z = 1
+W_X = 1
+W_O = 0
 VMEM = 60 * 1024 * 1024
+
+
+def cost(micros):
+    return pl.CostEstimate(flops=0, bytes_accessed=int(micros * 3.0e6), transcendentals=0)
 
 
 def chunk_sizes(slots):
@@ -44,11 +53,12 @@
         wide[i, pl.ds(0, windows * chans), :] = real_part[:, :, cut].reshape(windows * chans, 128)
         wide[i, pl.ds(windows * chans, windows * chans), :] = imag_part[:, :, cut].reshape(windows * chans, 128)
     total = jnp.sum(real_part * real_part + imag_part * imag_part, axis=-1, keepdims=True)
+    mask = jnp.concatenate([valid_ref[...].astype(jnp.float32)] * (128 // windows), axis=0).T
     lane = lax.broadcasted_iota(jnp.int32, (chans, 128), 1)
     energy = jnp.zeros((chans, 128), jnp.float32)
     for w in range(windows):
         energy = jnp.where(lane % windows == w, total[w], energy)
-    scale = valid_ref[...] / jnp.sqrt(energy * (1.0 / freq) + amp_eps)
+    scale = mask / jnp.sqrt(energy * (1.0 / freq) + amp_eps)
     high = scale.astype(jnp.bfloat16).astype(jnp.float32)
     middle = (scale - high).astype(jnp.bfloat16).astype(jnp.float32)
     low = scale - high - middle
@@ -89,7 +99,7 @@
     return arrays
 
 
-def cross_kernel(groups, own_first, pos_ref, *rest):
+def cross_kernel(groups, own_first, rows_ref, *rest):
     blocks = rest[:groups]
     rest = rest[groups:]
     own = blocks[0]
@@ -100,15 +110,14 @@
     own_scale = scales[0]
     if not own_first:
         own_scale, rest = rest[0], rest[1:]
-    out, factor, cap, src_white, src_unit, recv_white, recv_unit, inv = rest
     devs, chans = own_scale.shape[0], own_scale.shape[2]
+    outs, rest = rest[:devs], rest[devs:]
+    factor, cap, src_white, src_unit, recv_white, recv_unit, inv, packed = rest
     width = 128 // 8
     parts = devs // 8
     half = parts * 128
-    slots = out.shape[1] // PACK
-    rows_out = out.shape[2]
-    per_group = chans // rows_out
-    sets = groups if own_first else groups + 1
+    slots = outs[0].shape[0] // ROWS
+    rows_out = outs[0].shape[1]
 
     def opened(ref, q, part):
         return swap_blocks([ref[part * 8 + d, q].astype(jnp.float32) for d in range(8)], width)
@@ -163,6 +172,7 @@
                             recv_unit[b, at, hi] = -unit_re if odd else unit_im
         scaled = inv[...]
         lane = lax.broadcasted_iota(jnp.int32, scaled.shape, 1)
+        means, cohers = [], []
         for b in range(PACK):
             lin = lax.dot_general(
                 src_white[b], recv_white[b], (((1,), (1,)), ((), ())), preferred_element_type=jnp.float32
@@ -170,60 +180,107 @@
             pha = lax.dot_general(
                 src_unit[b], recv_unit[b], (((1,), (1,)), ((), ())), preferred_element_type=jnp.float32
             )
-            mean = lin * scaled
+            means.append(lin * scaled)
             one = pha[:, :128] * scaled
             two = pha[:, 128:] * scaled
-            coher = one * one + two * two
-            both = jnp.where(lane < 2 * chans, mean, mean * coher)
-            for g in range(groups):
-                for h in range(per_group):
-                    at = g * chans + h * rows_out
-                    out[pos_ref[g] * per_group + h, q * PACK + b] = both[at : at + rows_out]
+            cohers.append(one * one + two * two)
+        packed[0] = jnp.where(lane < 2 * chans, means[0], means[1])
+        packed[1] = jnp.where(lane < 2 * chans, means[2], means[3])
+        low = jnp.where(lane < chans, cohers[0], cohers[1])
+        high = jnp.where(lane < 3 * chans, cohers[2], cohers[3])
+        packed[2] = jnp.where(lane < 2 * chans, low, high)
+        for m, out in enumerate(outs):
+            at = pl.ds(pl.multiple_of(rows_ref[m], rows_out), rows_out)
+            for t in range(ROWS):
+                out[q * ROWS + t] = packed[t, at, :]
         return carry
 
-    lax.fori_loop(0, slots, step, 0)
-
-
-def lag_kernel(pieces, tile, rows_out, windows, freq, *rest):
-    refs, (table_high, table_low, linear, weighted) = rest[:pieces], rest[pieces:]
+    lax.fori_loop(0, slots, step, 0, unroll=2)
+
+
+def lag_kernel(slots, devs, rows_out, windows, freq, pieces, first, me_ref, *rest):
+    refs, rest = rest[:pieces], rest[pieces:]
+    table_high, table_low, rest = rest[0], rest[1], rest[2:]
+    if not first:
+        linear_before, weighted_before, rest = rest[0], rest[1], rest[2:]
+    linear, weighted, staged, left_high, left_low = rest
     chans = linear.shape[1]
-    first = pl.program_id(0) * tile
-    lin_rows, pw_rows = [], []
+    side = 128 // 2
+    room = side // devs
     factor = math.sqrt(windows / freq)
-    for i in range(tile):
-        got = []
-        for ref in refs:
-            got.append(ref[pl.ds(first + i, ref.shape[0] // rows_out, stride=rows_out), :])
-        flipped = (jnp.concatenate(got, axis=0) if pieces > 1 else got[0]).T
-        lin_rows.append(jnp.concatenate([flipped[:chans], flipped[chans : 2 * chans]], axis=1))
-        pw_rows.append(jnp.concatenate([flipped[2 * chans : 3 * chans], flipped[3 * chans :]], axis=1))
-    for rows, out, gain in ((lin_rows, linear, factor), (pw_rows, weighted, factor * windows)):
-        value = jnp.concatenate(rows, axis=0) * gain
-        high = value.astype(jnp.bfloat16)
-        low = (value - high.astype(jnp.float32)).astype(jnp.bfloat16)
-        total = jnp.dot(high, table_high[...], preferred_element_type=jnp.float32)
-        total += jnp.dot(high, table_low[...], preferred_element_type=jnp.float32)
-        total += jnp.dot(low, table_high[...], preferred_element_type=jnp.float32)
-        out[...] = total.reshape(tile, chans, LAGS)
-
-
-def lag_table(freq, devs, sizes):
-    slots = freq // PACK // devs
-    order = []
-    start = 0
-    for size in sizes:
-        for d in range(devs):
-            for q in range(start, start + size):
-                for b in range(PACK):
-                    order.append(b * (freq // PACK) + d * slots + q)
-        start += size
-    bins = lowest_bin + np.asarray(order, np.int64)
+
+    @pl.when(pl.program_id(0) == 0)
+    def fill():
+        def store(rows, value):
+            high = value.astype(jnp.bfloat16)
+            left_high[rows, :] = high
+            left_low[rows, :] = (value - high.astype(jnp.float32)).astype(jnp.bfloat16)
+
+        pad = jnp.zeros((max(room - slots, 1), 128), jnp.float32)
+        lane = lax.broadcasted_iota(jnp.int32, (chans, 128), 1)
+        for s in range(rows_out):
+            for m in range(devs):
+                at = pl.multiple_of((me_ref[0] ^ m) * room, room)
+                for t, places in enumerate(((0,), (1,), (2, 3))):
+                    block = refs[m][pl.ds(t * rows_out + s, slots, stride=ROWS * rows_out), :]
+                    block = jnp.concatenate([block, pad], axis=0) if room > slots else block
+                    for place in places:
+                        staged[pl.ds(place * side + at, room), :] = block
+            means = staged[: 2 * side].T * factor
+            coher = staged[2 * side :].T * windows
+            blocks = [coher[b * chans : (b + 1) * chans] for b in range(PACK)]
+            weights = [jnp.where(lane < side, blocks[0], blocks[2]), jnp.where(lane < side, blocks[1], blocks[3])]
+            parts = [means[i * chans : (i + 1) * chans] for i in range(4)]
+            plain = [parts[0], parts[2], parts[1], parts[3]]
+            store(pl.ds(s * chans, chans), jnp.concatenate(plain, axis=1))
+            scaled = [part * weights[i % 2] for i, part in enumerate(plain)]
+            store(pl.ds((rows_out + s) * chans, chans), jnp.concatenate(scaled, axis=1))
+
+    total = jnp.dot(left_high[...], table_high[...], preferred_element_type=jnp.float32)
+    total += jnp.dot(left_high[...], table_low[...], preferred_element_type=jnp.float32)
+    total += jnp.dot(left_low[...], table_high[...], preferred_element_type=jnp.float32)
+    half = rows_out * chans
+    for out, share, before in (
+        (linear, total[:half], None if first else linear_before),
+        (weighted, total[half:], None if first else weighted_before),
+    ):
+        share = share.reshape(out.shape)
+        out[...] = share if first else share + before[...]
+
+
+def lag_table(freq, devs, start, count):
+    span = freq // PACK
+    slots = span // devs
+    room = 128 // 2 // devs
     shifts = np.arange(LAGS, dtype=np.int64) - LAGS // 2
+    bins = lowest_bin + np.arange(freq, dtype=np.int64)
     theta = np.mod(bins[:, None] * shifts[None, :], window_samples) * (2.0 * math.pi / window_samples)
-    table = np.concatenate([np.cos(theta), -np.sin(theta)], axis=0).astype(np.float32)
+    table = np.zeros((2, 2, 2, devs, room, LAGS), np.float32)
+    for kind, values in enumerate((np.cos(theta), -np.sin(theta))):
+        values = values.reshape(PACK, devs, slots, LAGS)[:, :, start : start + count]
+        for b in range(PACK):
+            table[kind, b % 2, b // 2, :, :count] = values[b]
+    table = table.reshape(-1, LAGS)
     high = table.astype(ml_dtypes.bfloat16)
     low = (table - high.astype(np.float32)).astype(ml_dtypes.bfloat16)
     return high, low
+
+
+def join_kernel(*refs):
+    pass
+
+
+def join(token, arrays):
+    anywhere = pl.BlockSpec(memory_space=pl.ANY)
+    return pl.pallas_call(
+        join_kernel,
+        in_specs=[anywhere] * (1 + len(arrays)),
+        out_specs=anywhere,
+        out_shape=jax.ShapeDtypeStruct(token.shape, token.dtype),
+        input_output_aliases={0: 0},
+        cost_estimate=cost(0.1),
+        name="join",
+    )(token, *arrays)
 
 
 def body(spectra, valid, source_block):
@@ -235,10 +292,9 @@
     sizes = chunk_sizes(slots)
     rows_out = SRC_W // devs
     windows = win_dev * devs
-    own_first = stations == groups
+    own_first = stations == groups == 4
     params = pltpu.CompilerParams(vmem_limit_bytes=VMEM)
 
-    mask = jnp.tile(valid.astype(jnp.float32).T, (1, 128 // win_dev))
     packed = pl.pallas_call(
         functools.partial(pack_kernel, sizes, devs),
         out_shape=[
@@ -249,8 +305,9 @@
             pltpu.VMEM((freq // PACK * chans, 128), jnp.float32),
         ],
         compiler_params=params,
+        cost_estimate=cost(5),
         name="pack",
-    )(spectra, mask)
+    )(spectra, valid)
 
     me = lax.axis_index("chan")
     if own_first:
@@ -259,32 +316,29 @@
     else:
         pos = jnp.arange(groups, dtype=jnp.int32)
 
+    me_win = lax.axis_index("win")
+    per_group = chans // rows_out
+    target = me_win ^ jnp.arange(devs, dtype=jnp.int32)
+    holder = jnp.argmax(pos[None, :] == (target // per_group)[:, None], axis=1).astype(jnp.int32)
+    row_table = holder * chans + target % per_group * rows_out
+
     ring = [(i, (i + 1) % stations) for i in range(stations)]
-    scale_blocks = None
-    pieces = []
-    for i, n in enumerate(sizes):
-        mine = lax.all_to_all(packed[i], "win", 0, 0, tiled=True)
-        if own_first:
-            got = [mine]
-            for hop in range(groups - 1):
-                got.append(lax.ppermute(got[-1], "chan", ring))
-        else:
-            every = lax.all_gather(mine, "chan")
-            got = [lax.dynamic_index_in_dim(every, source_block[g], 0, False) for g in range(groups)]
-            got.append(mine)
-        if i == 0:
-            scale_blocks = got
+    count = len(sizes)
+
+    def cross_call(i, token, got, heads):
+        n = sizes[i]
         rows = groups * chans if own_first else (groups + 1) * chans
         half = win_dev * devs
         last = sizes[0]
         whole = pl.BlockSpec((devs, n + (i == 0), chans, 128), lambda s: (0, 0, 0, 0))
         tail = pl.BlockSpec((devs, 1, chans, 128), lambda s: (0, last, 0, 0))
-        out = pl.pallas_call(
+        shape = (n * ROWS, rows_out, 128)
+        return pl.pallas_call(
             functools.partial(cross_kernel, groups, own_first),
             grid=(1,),
             in_specs=[pl.BlockSpec(memory_space=pltpu.SMEM)] + [whole] * len(got) + [tail] * len(got),
-            out_specs=pl.BlockSpec((devs, n * PACK, rows_out, 128), lambda s: (0, 0, 0, 0)),
-            out_shape=jax.ShapeDtypeStruct((devs, n * PACK, rows_out, 128), jnp.float32),
+            out_specs=[pl.BlockSpec(shape, lambda s: (0, 0, 0))] * devs,
+            out_shape=[jax.ShapeDtypeStruct(shape, jnp.float32)] * devs,
             scratch_shapes=[
                 pltpu.VMEM((rows, half), jnp.float32),
                 pltpu.VMEM((rows, half), jnp.float32),
@@ -293,25 +347,91 @@
                 pltpu.VMEM((PACK, 4 * chans, 2 * half), jnp.bfloat16),
                 pltpu.VMEM((PACK, 8 * chans, 2 * half), jnp.bfloat16),
                 pltpu.VMEM((groups * chans, 128), jnp.float32),
+                pltpu.VMEM((ROWS, groups * chans, 128), jnp.float32),
             ],
             compiler_params=params,
+            cost_estimate=cost(2 + n),
             name="cross",
-        )(pos, *got, *scale_blocks)
-        back = lax.all_to_all(out, "win", 0, 0, tiled=True)
-        pieces.append(back.reshape(devs * n * PACK * rows_out, 128))
-
-    high, low = lag_table(freq, devs, sizes)
-    tile = 4
-    full = lambda shape: pl.BlockSpec(shape, lambda s: (0, 0))
-    return pl.pallas_call(
-        functools.partial(lag_kernel, len(pieces), tile, rows_out, windows, freq),
-        grid=(rows_out // tile,),
-        in_specs=[full(p.shape) for p in pieces] + [full(high.shape), full(low.shape)],
-        out_specs=[pl.BlockSpec((tile, chans, LAGS), lambda s: (s, 0, 0))] * 2,
-        out_shape=[jax.ShapeDtypeStruct((rows_out, chans, LAGS), jnp.float32)] * 2,
-        compiler_params=params,
-        name="lag",
-    )(*pieces, jnp.asarray(high), jnp.asarray(low))
+        )(token, *got, *heads)
+
+    def send_back(outs):
+        back = [outs[0]]
+        for m in range(1, devs):
+            back.append(lax.ppermute(outs[m], "win", [(d, d ^ m) for d in range(devs)]))
+        return back
+
+    backs = [None] * count
+    if own_first:
+        back_ring = [(i, (i - 1) % stations) for i in range(stations)]
+        held = {}
+        crossed = {}
+
+        def enter(i, after):
+            block = join(packed[i], after) if after else packed[i]
+            held[i] = [lax.all_to_all(block, "win", 0, 0, tiled=True)]
+
+        def spread(i, after):
+            own = join(held[i][0], after) if after else held[i][0]
+            up = lax.ppermute(own, "chan", ring)
+            down = lax.ppermute(own, "chan", back_ring)
+            held[i] = [own, up, lax.ppermute(up, "chan", ring), down]
+
+        def cross_chunk(i, after):
+            token = join(row_table, after) if after else row_table
+            crossed[i] = cross_call(i, token, held[i], held[0])
+            backs[i] = send_back(crossed[i])
+
+        enter(0, [])
+        for i in range(count + 1):
+            if i < count:
+                after = []
+                if i and W_Z:
+                    after.append(held[i - 1][1])
+                if i > 1 and W_X:
+                    after.append(crossed[i - 2][0])
+                spread(i, after)
+                if i + 1 < count:
+                    enter(i + 1, [held[max(i - 1, 0)][0 if i == 0 else 1]] if W_IN else [])
+            if i:
+                cross_chunk(i - 1, [backs[i - 2][-1]] if W_O and i > 1 else [])
+    else:
+        gathered = []
+        for p in packed:
+            mine = lax.all_to_all(p, "win", 0, 0, tiled=True)
+            every = lax.all_gather(mine, "chan")
+            picked = [lax.dynamic_index_in_dim(every, source_block[g], 0, False) for g in range(groups)]
+            gathered.append(picked + [mine])
+        for i in range(count):
+            backs[i] = send_back(cross_call(i, row_table, gathered[i], gathered[0]))
+
+    tile = 256
+    result = []
+    whole_out = jax.ShapeDtypeStruct((rows_out, chans, LAGS), jnp.float32)
+    out_spec = pl.BlockSpec((rows_out, chans, tile), lambda s: (0, 0, s))
+    start = 0
+    for i, n in enumerate(sizes):
+        pieces = [back.reshape(-1, 128) for back in backs[i]]
+        high, low = lag_table(freq, devs, start, n)
+        table_spec = pl.BlockSpec((high.shape[0], tile), lambda s: (0, s))
+        result = pl.pallas_call(
+            functools.partial(lag_kernel, n, devs, rows_out, windows, freq, len(pieces), i == 0),
+            grid=(LAGS // tile,),
+            in_specs=[pl.BlockSpec(memory_space=pltpu.SMEM)] + [pl.BlockSpec(pieces[0].shape, lambda s: (0, 0))] * len(pieces)
+            + [table_spec] * 2
+            + [out_spec] * len(result),
+            out_specs=[out_spec] * 2,
+            out_shape=[whole_out] * 2,
+            scratch_shapes=[
+                pltpu.VMEM((2 * 128, 128), jnp.float32),
+                pltpu.VMEM((2 * rows_out * chans, high.shape[0]), jnp.bfloat16),
+                pltpu.VMEM((2 * rows_out * chans, high.shape[0]), jnp.bfloat16),
+            ],
+            compiler_params=params,
+            cost_estimate=cost(6),
+            name="lag",
+        )(me_win.reshape(1), *pieces, jnp.asarray(high), jnp.asarray(low), *result)
+        start += n
+    return result
 
 
 def solution(mesh):

time: 157 us -> 124 us (0.79)
  blocking collectives: 62.1 us -> 13.4 us
  starting transfers between devices: 1.3 us -> 35.1 us
  waiting for transfers between devices: 60 us -> 34.7 us
  Pallas kernels: 28.7 us -> 34.2 us
    all_to_all x2 -> x1, blocking collectives: 62.1 us -> 13.4 us  [enter(): held[i] = [lax.all_to_all(block, 'win', 0, 0, tiled=True)]]
    ppermute x3 -> x20, waiting for transfers between devices: 60 us -> 28.3 us  [the longest x2 12.9 us: spread(): down = lax.ppermute(own, 'chan', back_ring)]
    ppermute x3 -> x20, starting transfers between devices: 1.3 us -> 30.5 us  [the longest x14 22.6 us: send_back(): back.append(lax.ppermute(outs[m], 'win', [(d, d ^ m) for d in range(devs)]))]
    all_to_all x0 -> x1, waiting for transfers between devices: none -> 6.35 us  [enter(): held[i] = [lax.all_to_all(block, 'win', 0, 0, tiled=True)]]
    pallas_call x2 -> x6, Pallas kernels: 24.2 us -> 29.7 us  [the longest x2 15.8 us: body(): pl.pallas_call(functools.partial(lag_kernel, n, devs, rows_out, windows,...]
    all_to_all x0 -> x1, starting transfers between devices: none -> 4.61 us  [enter(): held[i] = [lax.all_to_all(block, 'win', 0, 0, tiled=True)]]
  transfers between devices with their start and end apart: 3 -> 21, of which waited for: 3 -> 9; matrix products, arithmetic and copies ran while one was open for 1% -> 2% of each run, Pallas kernels for 0% -> 17%
where the time goes in v2:
time: 124 us; the launch traced here: 123 us
  starting transfers between devices  35.1 us (28%)
  waiting for transfers between devices  34.7 us (28%)
  Pallas kernels  34.2 us (28%)
  blocking collectives  13.4 us (11%)
  local copies, waits for them, and re-layouts  2.42 us (2%)
  other arithmetic  2.02 us (2%)
    ppermute x14, starting transfers between devices, send_back(): back.append(lax.ppermute(outs[m], 'win', [(d, d ^ m) for d in range(devs)]))  22.6 us
    pallas_call x2, Pallas kernels, body(): pl.pallas_call(functools.partial(lag_kernel, n, devs, rows_out, windows,...  15.8 us
    pallas_call x2, Pallas kernels, cross_call(): pl.pallas_call(functools.partial(cross_kernel, groups, own_first), grid=(...  13.9 us
    all_to_all x1, blocking collectives, enter(): held[i] = [lax.all_to_all(block, 'win', 0, 0, tiled=True)]  13.4 us
    ppermute x2, waiting for transfers between devices, spread(): down = lax.ppermute(own, 'chan', back_ring)  12.9 us
    ppermute x2, waiting for transfers between devices, spread(): held[i] = [own, up, lax.ppermute(up, 'chan', ring), down]  7.07 us
    all_to_all x1, waiting for transfers between devices, enter(): held[i] = [lax.all_to_all(block, 'win', 0, 0, tiled=True)]  6.35 us
    ppermute x2, starting transfers between devices, spread(): down = lax.ppermute(own, 'chan', back_ring)  5.58 us
  transfers between devices with their start and end apart: 21, of which 9 were waited for; matrix products, arithmetic and copies ran while one was open for 2% of the time, Pallas kernels for 17%

profile of v2, /device:TPU:1, one launch (start us, length us, event | category | flops | bytes accessed | tf_op | source)
XLA Modules:
  0.0 122.6 jit_solution(4899525006022804655)
XLA Ops:
  0.6 4.5 %pack.1 = (bf16[8,7,32,128]{3,2,1,0:T(8,128)(2,1)}, bf16[8,6,32,128]{3,2,1,0:T(8,128)(2,1)}) custom-call(bf16[2,16,32,384]{3,2,1,0:T(8,128)(2,1)} %spectra_ref.1, s32[16,32]{1,0:T(8,128)} %valid_ref.1), custom_call_target="tpu_custom_call" | custom-call | bytes 15000000 | tf_op jit(solution)/shard_map/pack/pallas_call | solution.py:298
  5.1 13.4 %all_to_all.10.refs_1_.rest_4_.rest_0_ = bf16[8,7,32,128]{3,2,1,0:T(8,128)(2,1)S(1)} all-to-all(bf16[8,7,32,128]{3,2,1,0:T(8,128)(2,1)} %get-tuple-element.27), channel_id=1, replica_groups=mesh['chan'=4,'win'=8] {'win'}, dimensions={0} | all-to-all | bytes 917504 | tf_op jit(solution)/shard_map/all_to_all | solution.py:371
  18.5 1.3 %collective-permute-start = (bf16[8,7,32,128]{3,2,1,0:T(8,128)(2,1)S(1)}, bf16[8,7,32,128]{3,2,1,0:T(8,128)(2,1)S(1)}, u32[]{:S(2)}, u32[]{:S(2)}) collective-permute-start(bf16[8,7,32,128]{3,2,1,0:T(8,128)(2,1)S(1)} %all_to_all.10.refs_1_.rest_4_.rest_0_), channel_id=1, source_target_pairs={{0,8},{8,16},{16,24},{24,0},{1,9},{9,17},{17,25},{25,1},{2,10},{10... | collective-permute-start | bytes 1376264 | tf_op jit(solution)/shard_map/ppermute | solution.py:375
  19.8 4.6 %all-to-all-start.1 = ((bf16[8,6,32,128]{3,2,1,0:T(8,128)(2,1)}), bf16[8,6,32,128]{3,2,1,0:T(8,128)(2,1)S(1)}, u32[]{:S(2)}, u32[]{:S(2)}) async-start(bf16[8,6,32,128]{3,2,1,0:T(8,128)(2,1)} %join.2), calls=%async_computation.1 | async-start | bytes 786432 | tf_op jit(solution)/shard_map/all_to_all | solution.py:371
  24.5 6.3 %all-to-all-done.1.refs_0_ = bf16[8,6,32,128]{3,2,1,0:T(8,128)(2,1)S(1)} async-done(((bf16[8,6,32,128]{3,2,1,0:T(8,128)(2,1)}), bf16[8,6,32,128]{3,2,1,0:T(8,128)(2,1)S(1)}, u32[]{:S(2)}, u32[]{:S(2)}) %all-to-all-start.1) | async-done | bytes 393248 | tf_op jit(solution)/shard_map/all_to_all | solution.py:371
  30.8 0.7 collective-permute-done.refs_1_.rest_5_.rest_1_
  31.6 0.8 copy-done.1
  32.3 1.0 collective-permute-start.1
  33.3 0.7 iota_reduce_fusion.1
  34.1 2.3 %collective-permute-start.5 = (bf16[8,7,32,128]{3,2,1,0:T(8,128)(2,1)}, bf16[8,7,32,128]{3,2,1,0:T(8,128)(2,1)S(1)}, u32[]{:S(2)}, u32[]{:S(2)}) collective-permute-start(bf16[8,7,32,128]{3,2,1,0:T(8,128)(2,1)} %copy-done), channel_id=1, source_target_pairs={{0,24},{8,0},{16,8},{24,16},{1,25},{9,1},{17,9},{25,17},{2,26},{10... | collective-permute-start | bytes 1376264 | tf_op jit(solution)/shard_map/ppermute | solution.py:376
  36.3 3.3 %collective-permute-start.3 = (bf16[8,6,32,128]{3,2,1,0:T(8,128)(2,1)}, bf16[8,6,32,128]{3,2,1,0:T(8,128)(2,1)S(1)}, u32[]{:S(2)}, u32[]{:S(2)}) collective-permute-start(bf16[8,6,32,128]{3,2,1,0:T(8,128)(2,1)} %join.3.rest_0_), channel_id=1, source_target_pairs={{0,24},{8,0},{16,8},{24,16},{1,25},{9,1},{17,9},{25,17},{2,26},{10... | collective-permute-start | bytes 1179656 | tf_op jit(solution)/shard_map/ppermute | solution.py:376
  39.7 3.3 %collective-permute-done.1.rest_1_ = bf16[8,6,32,128]{3,2,1,0:T(8,128)(2,1)S(1)} collective-permute-done((bf16[8,6,32,128]{3,2,1,0:T(8,128)(2,1)}, bf16[8,6,32,128]{3,2,1,0:T(8,128)(2,1)S(1)}, u32[]{:S(2)}, u32[]{:S(2)}) %collective-permute-start.1) | collective-permute-done | bytes 393248 | tf_op jit(solution)/shard_map/ppermute | solution.py:375
  43.0 0.8 iota_reduce_fusion
  44.3 12.9 %collective-permute-done.5.rest_7_.rest_3_ = bf16[8,7,32,128]{3,2,1,0:T(8,128)(2,1)S(1)} collective-permute-done((bf16[8,7,32,128]{3,2,1,0:T(8,128)(2,1)}, bf16[8,7,32,128]{3,2,1,0:T(8,128)(2,1)S(1)}, u32[]{:S(2)}, u32[]{:S(2)}) %collective-permute-start.5) | collective-permute-done | bytes 458784 | tf_op jit(solution)/shard_map/ppermute | solution.py:376
  57.2 5.5 %collective-permute-done.4.rest_6_.rest_2_ = bf16[8,7,32,128]{3,2,1,0:T(8,128)(2,1)S(1)} collective-permute-done((bf16[8,7,32,128]{3,2,1,0:T(8,128)(2,1)}, bf16[8,7,32,128]{3,2,1,0:T(8,128)(2,1)S(1)}, u32[]{:S(2)}, u32[]{:S(2)}) %collective-permute-start.4) | collective-permute-done | bytes 458784 | tf_op jit(solution)/shard_map/ppermute | solution.py:377
  62.7 0.8 copy-done.3
  63.5 7.0 %cross.3 = (f32[18,16,128]{2,1,0:T(8,128)}, f32[18,16,128]{2,1,0:T(8,128)}, f32[18,16,128]{2,1,0:T(8,128)}, f32[18,16,128]{2,1,0:T(8,128)}, f32[18,16,128]{2,1,0...) custom-call(s32[8]{0:T(128)} %fusion.1.rows_ref, ...), custom_call_target="tpu_custom_call" | custom-call | bytes 24000000 | tf_op jit(solution)/shard_map/cross/pallas_call | solution.py:336
  70.5 5.5 %collective-permute-start.13 = (f32[18,16,128]{2,1,0:T(8,128)}, f32[18,16,128]{2,1,0:T(8,128)S(1)}, u32[]{:S(2)}, u32[]{:S(2)}) collective-permute-start(f32[18,16,128]{2,1,0:T(8,128)} %get-tuple-element.37), channel_id=1, source_target_pairs={{0,1},{1,0},{2,3},{3,2},{4,5},{5,4},{6,7},{7,6},{8,9},{9,8},{10,11... | collective-permute-start | bytes 442376 | tf_op jit(solution)/shard_map/ppermute | solution.py:360
  76.4 1.3 %collective-permute-start.15 = (f32[18,16,128]{2,1,0:T(8,128)}, f32[18,16,128]{2,1,0:T(8,128)S(1)}, u32[]{:S(2)}, u32[]{:S(2)}) collective-permute-start(f32[18,16,128]{2,1,0:T(8,128)} %get-tuple-element.39), channel_id=1, source_target_pairs={{0,3},{1,2},{2,1},{3,0},{4,7},{5,6},{6,5},{7,4},{8,11},{9,10},{10,... | collective-permute-start | bytes 442376 | tf_op jit(solution)/shard_map/ppermute | solution.py:360
  78.0 1.6 %collective-permute-done.2.rest_2_ = bf16[8,6,32,128]{3,2,1,0:T(8,128)(2,1)S(1)} collective-permute-done((bf16[8,6,32,128]{3,2,1,0:T(8,128)(2,1)S(1)}, bf16[8,6,32,128]{3,2,1,0:T(8,128)(2,1)S(1)}, u32[]{:S(2)}, u32[]{:S(2)}) %collective-permute-start.2) | collective-permute-done | bytes 393248 | tf_op jit(solution)/shard_map/ppermute | solution.py:377
  79.6 3.0 %collective-permute-start.17 = (f32[18,16,128]{2,1,0:T(8,128)}, f32[18,16,128]{2,1,0:T(8,128)S(1)}, u32[]{:S(2)}, u32[]{:S(2)}) collective-permute-start(f32[18,16,128]{2,1,0:T(8,128)} %get-tuple-element.41), channel_id=1, source_target_pairs={{0,5},{1,4},{2,7},{3,6},{4,1},{5,0},{6,3},{7,2},{8,13},{9,12},{10,... | collective-permute-start | bytes 442376 | tf_op jit(solution)/shard_map/ppermute | solution.py:360
  82.6 6.9 %cross.2 = (f32[18,16,128]{2,1,0:T(8,128)}, f32[18,16,128]{2,1,0:T(8,128)}, f32[18,16,128]{2,1,0:T(8,128)}, f32[18,16,128]{2,1,0:T(8,128)}, f32[18,16,128]{2,1,0...) custom-call(s32[8]{0:T(128)} %fusion.1.rows_ref, ...), custom_call_target="tpu_custom_call" | custom-call | bytes 24000000 | tf_op jit(solution)/shard_map/cross/pallas_call | solution.py:336
  89.5 2.8 %collective-permute-start.18 = (f32[18,16,128]{2,1,0:T(8,128)S(1)}, f32[18,16,128]{2,1,0:T(8,128)S(1)}, u32[]{:S(2)}, u32[]{:S(2)}) collective-permute-start(f32[18,16,128]{2,1,0:T(8,128)S(1)} %copy-done.24), channel_id=1, source_target_pairs={{0,6},{1,7},{2,4},{3,5},{4,2},{5,3},{6,0},{7,1},{8,14},{9,15},{10,... | collective-permute-start | bytes 442376 | tf_op jit(solution)/shard_map/ppermute | solution.py:360
  92.9 1.8 %collective-permute-start.7 = (f32[18,16,128]{2,1,0:T(8,128)}, f32[18,16,128]{2,1,0:T(8,128)S(1)}, u32[]{:S(2)}, u32[]{:S(2)}) collective-permute-start(f32[18,16,128]{2,1,0:T(8,128)} %get-tuple-element.30), channel_id=1, source_target_pairs={{0,2},{1,3},{2,0},{3,1},{4,6},{5,7},{6,4},{7,5},{8,10},{9,11},{10,... | collective-permute-start | bytes 442376 | tf_op jit(solution)/shard_map/ppermute | solution.py:360
  95.1 1.1 collective-permute-done.18
  96.2 1.1 collective-permute-start.9
  97.3 2.9 %collective-permute-done.19 = f32[18,16,128]{2,1,0:T(8,128)S(1)} collective-permute-done((f32[18,16,128]{2,1,0:T(8,128)S(1)}, f32[18,16,128]{2,1,0:T(8,128)S(1)}, u32[]{:S(2)}, u32[]{:S(2)}) %collective-permute-start.19) | collective-permute-done | bytes 147488 | tf_op jit(solution)/shard_map/ppermute | solution.py:360
  100.2 0.6 collective-permute-start.10
  100.8 1.4 %collective-permute-start.11 = (f32[18,16,128]{2,1,0:T(8,128)}, f32[18,16,128]{2,1,0:T(8,128)S(1)}, u32[]{:S(2)}, u32[]{:S(2)}) collective-permute-start(f32[18,16,128]{2,1,0:T(8,128)} %get-tuple-element.34), channel_id=1, source_target_pairs={{0,6},{1,7},{2,4},{3,5},{4,2},{5,3},{6,0},{7,1},{8,14},{9,15},{10,... | collective-permute-start | bytes 442376 | tf_op jit(solution)/shard_map/ppermute | solution.py:360
  102.5 3.4 %collective-permute-start.12 = (f32[18,16,128]{2,1,0:T(8,128)}, f32[18,16,128]{2,1,0:T(8,128)S(1)}, u32[]{:S(2)}, u32[]{:S(2)}) collective-permute-start(f32[18,16,128]{2,1,0:T(8,128)} %get-tuple-element.35), channel_id=1, source_target_pairs={{0,7},{1,6},{2,5},{3,4},{4,3},{5,2},{6,1},{7,0},{8,15},{9,14},{10,... | collective-permute-start | bytes 442376 | tf_op jit(solution)/shard_map/ppermute | solution.py:360
  106.0 7.5 %lag.2 = (f32[16,32,1024]{2,1,0:T(8,128)}, f32[16,32,1024]{2,1,0:T(8,128)}) custom-call(s32[1]{0:T(128)} %bitcast.me_ref, f32[288,128]{1,0:T(8,128)} %bitcast.17, f32[288,128]{1,0:T(8,128)} %bitcast.18, f32[288,128]{1,0:T(8,128)} %bitcast.19, f32[288,128]{1,0:T(8,128)} %bitcast.20, f32[288,128]{1,0:T(8,128)} %bitcast.21, f32[288,128]{1,0:T(8,128)} %bitcast.22, ...), custom_call_target="tpu_custom_call" | custom-call | bytes 18000000 | tf_op jit(solution)/shard_map/lag/pallas_call | solution.py:416
  114.3 8.3 %lag.3 = (f32[16,32,1024]{2,1,0:T(8,128)}, f32[16,32,1024]{2,1,0:T(8,128)}) custom-call(s32[1]{0:T(128)} %bitcast.me_ref, f32[288,128]{1,0:T(8,128)} %bitcast.25, f32[288,128]{1,0:T(8,128)} %bitcast.26, f32[288,128]{1,0:T(8,128)} %bitcast.27, f32[288,128]{1,0:T(8,128)} %bitcast.28, f32[288,128]{1,0:T(8,128)} %bitcast.29, f32[288,128]{1,0:T(8,128)} %bitcast.30, ...), custom_call_target="tpu_custom_call" | custom-call | bytes 18000000 | tf_op jit(solution)/shard_map/lag/pallas_call | solution.py:416
  (73 shorter events, 3.3 us)
Async XLA Ops:
  5.1 28.2 %copy-start.22 = (s32[4]{0:T(128)S(1)}, s32[4]{0:T(128)}, u32[]{:S(2)}) copy-start(s32[4]{0:T(128)} %param.9) | copy-start | bytes 52
  18.5 13.0 %collective-permute-start = (bf16[8,7,32,128]{3,2,1,0:T(8,128)(2,1)S(1)}, bf16[8,7,32,128]{3,2,1,0:T(8,128)(2,1)S(1)}, u32[]{:S(2)}, u32[]{:S(2)}) collective-permute-start(bf16[8,7,32,128]{3,2,1,0:T(8,128)(2,1)S(1)} %all_to_all.10.refs_1_.rest_4_.rest_0_), channel_id=1, source_target_pairs={{0,8},{8,16},{16,24},{24,0},{1,9},{9,17},{17,25},{25,1},{2,10},{10... | collective-permute-start | bytes 1376264 | tf_op jit(solution)/shard_map/ppermute | solution.py:375
  19.8 11.0 %all-to-all-start.1 = ((bf16[8,6,32,128]{3,2,1,0:T(8,128)(2,1)}), bf16[8,6,32,128]{3,2,1,0:T(8,128)(2,1)S(1)}, u32[]{:S(2)}, u32[]{:S(2)}) async-start(bf16[8,6,32,128]{3,2,1,0:T(8,128)(2,1)} %join.2), calls=%async_computation.1 | async-start | bytes 786432 | tf_op jit(solution)/shard_map/all_to_all | solution.py:371
  32.3 10.7 %collective-permute-start.1 = (bf16[8,6,32,128]{3,2,1,0:T(8,128)(2,1)}, bf16[8,6,32,128]{3,2,1,0:T(8,128)(2,1)S(1)}, u32[]{:S(2)}, u32[]{:S(2)}) collective-permute-start(bf16[8,6,32,128]{3,2,1,0:T(8,128)(2,1)} %join.3.rest_0_), channel_id=1, source_target_pairs={{0,8},{8,16},{16,24},{24,0},{1,9},{9,17},{17,25},{25,1},{2,10},{10... | collective-permute-start | bytes 1179656 | tf_op jit(solution)/shard_map/ppermute | solution.py:375
  34.1 23.1 %collective-permute-start.5 = (bf16[8,7,32,128]{3,2,1,0:T(8,128)(2,1)}, bf16[8,7,32,128]{3,2,1,0:T(8,128)(2,1)S(1)}, u32[]{:S(2)}, u32[]{:S(2)}) collective-permute-start(bf16[8,7,32,128]{3,2,1,0:T(8,128)(2,1)} %copy-done), channel_id=1, source_target_pairs={{0,24},{8,0},{16,8},{24,16},{1,25},{9,1},{17,9},{25,17},{2,26},{10... | collective-permute-start | bytes 1376264 | tf_op jit(solution)/shard_map/ppermute | solution.py:376
  36.3 26.4 %collective-permute-start.4 = (bf16[8,7,32,128]{3,2,1,0:T(8,128)(2,1)}, bf16[8,7,32,128]{3,2,1,0:T(8,128)(2,1)S(1)}, u32[]{:S(2)}, u32[]{:S(2)}) collective-permute-start(bf16[8,7,32,128]{3,2,1,0:T(8,128)(2,1)} %copy-done.1), channel_id=1, source_target_pairs={{0,8},{8,16},{16,24},{24,0},{1,9},{9,17},{17,25},{25,1},{2,10},{10... | collective-permute-start | bytes 1376264 | tf_op jit(solution)/shard_map/ppermute | solution.py:377
  36.3 41.4 %collective-permute-start.3 = (bf16[8,6,32,128]{3,2,1,0:T(8,128)(2,1)}, bf16[8,6,32,128]{3,2,1,0:T(8,128)(2,1)S(1)}, u32[]{:S(2)}, u32[]{:S(2)}) collective-permute-start(bf16[8,6,32,128]{3,2,1,0:T(8,128)(2,1)} %join.3.rest_0_), channel_id=1, source_target_pairs={{0,24},{8,0},{16,8},{24,16},{1,25},{9,1},{17,9},{25,17},{2,26},{10... | collective-permute-start | bytes 1179656 | tf_op jit(solution)/shard_map/ppermute | solution.py:376
  43.0 39.6 %copy-start.5 = (bf16[8,6,32,128]{3,2,1,0:T(8,128)(2,1)}, bf16[8,6,32,128]{3,2,1,0:T(8,128)(2,1)S(1)}, u32[]{:S(2)}) copy-start(bf16[8,6,32,128]{3,2,1,0:T(8,128)(2,1)S(1)} %collective-permute-done.1.rest_1_) | copy-start | bytes 1179652
  43.0 36.6 %collective-permute-start.2 = (bf16[8,6,32,128]{3,2,1,0:T(8,128)(2,1)S(1)}, bf16[8,6,32,128]{3,2,1,0:T(8,128)(2,1)S(1)}, u32[]{:S(2)}, u32[]{:S(2)}) collective-permute-start(bf16[8,6,32,128]{3,2,1,0:T(8,128)(2,1)S(1)} %collective-permute-done.1.rest_1_), channel_id=1, source_target_pairs={{0,8},{8,16},{16,24},{24,0},{1,9},{9,17},{17,25},{25,1},{2,10},{10... | collective-permute-start | bytes 1179656 | tf_op jit(solution)/shard_map/ppermute | solution.py:377
  70.5 19.0 %copy-start.24 = (f32[18,16,128]{2,1,0:T(8,128)S(1)}, f32[18,16,128]{2,1,0:T(8,128)}, u32[]{:S(2)}) copy-start(f32[18,16,128]{2,1,0:T(8,128)} %get-tuple-element.42) | copy-start | bytes 442372
  70.5 21.9 %copy-start.23 = (f32[18,16,128]{2,1,0:T(8,128)S(1)}, f32[18,16,128]{2,1,0:T(8,128)}, u32[]{:S(2)}) copy-start(f32[18,16,128]{2,1,0:T(8,128)} %get-tuple-element.43) | copy-start | bytes 442372
  70.5 19.0 %collective-permute-start.13 = (f32[18,16,128]{2,1,0:T(8,128)}, f32[18,16,128]{2,1,0:T(8,128)S(1)}, u32[]{:S(2)}, u32[]{:S(2)}) collective-permute-start(f32[18,16,128]{2,1,0:T(8,128)} %get-tuple-element.37), channel_id=1, source_target_pairs={{0,1},{1,0},{2,3},{3,2},{4,5},{5,4},{6,7},{7,6},{8,9},{9,8},{10,11... | collective-permute-start | bytes 442376 | tf_op jit(solution)/shard_map/ppermute | solution.py:360
  76.0 16.4 %collective-permute-start.14 = (f32[18,16,128]{2,1,0:T(8,128)}, f32[18,16,128]{2,1,0:T(8,128)S(1)}, u32[]{:S(2)}, u32[]{:S(2)}) collective-permute-start(f32[18,16,128]{2,1,0:T(8,128)} %get-tuple-element.38), channel_id=1, source_target_pairs={{0,2},{1,3},{2,0},{3,1},{4,6},{5,7},{6,4},{7,5},{8,10},{9,11},{10,... | collective-permute-start | bytes 442376 | tf_op jit(solution)/shard_map/ppermute | solution.py:360
  76.4 16.3 %collective-permute-start.15 = (f32[18,16,128]{2,1,0:T(8,128)}, f32[18,16,128]{2,1,0:T(8,128)S(1)}, u32[]{:S(2)}, u32[]{:S(2)}) collective-permute-start(f32[18,16,128]{2,1,0:T(8,128)} %get-tuple-element.39), channel_id=1, source_target_pairs={{0,3},{1,2},{2,1},{3,0},{4,7},{5,6},{6,5},{7,4},{8,11},{9,10},{10,... | collective-permute-start | bytes 442376 | tf_op jit(solution)/shard_map/ppermute | solution.py:360
  77.7 15.2 %collective-permute-start.16 = (f32[18,16,128]{2,1,0:T(8,128)}, f32[18,16,128]{2,1,0:T(8,128)S(1)}, u32[]{:S(2)}, u32[]{:S(2)}) collective-permute-start(f32[18,16,128]{2,1,0:T(8,128)} %get-tuple-element.40), channel_id=1, source_target_pairs={{0,4},{1,5},{2,6},{3,7},{4,0},{5,1},{6,2},{7,3},{8,12},{9,13},{10,... | collective-permute-start | bytes 442376 | tf_op jit(solution)/shard_map/ppermute | solution.py:360
  79.6 15.2 %collective-permute-start.17 = (f32[18,16,128]{2,1,0:T(8,128)}, f32[18,16,128]{2,1,0:T(8,128)S(1)}, u32[]{:S(2)}, u32[]{:S(2)}) collective-permute-start(f32[18,16,128]{2,1,0:T(8,128)} %get-tuple-element.41), channel_id=1, source_target_pairs={{0,5},{1,4},{2,7},{3,6},{4,1},{5,0},{6,3},{7,2},{8,13},{9,12},{10,... | collective-permute-start | bytes 442376 | tf_op jit(solution)/shard_map/ppermute | solution.py:360
  89.5 16.4 %copy-start.8 = (f32[18,16,128]{2,1,0:T(8,128)}, f32[18,16,128]{2,1,0:T(8,128)S(1)}, u32[]{:S(2)}) copy-start(f32[18,16,128]{2,1,0:T(8,128)S(1)} %collective-permute-done.13) | copy-start | bytes 442372
  89.5 6.7 %collective-permute-start.18 = (f32[18,16,128]{2,1,0:T(8,128)S(1)}, f32[18,16,128]{2,1,0:T(8,128)S(1)}, u32[]{:S(2)}, u32[]{:S(2)}) collective-permute-start(f32[18,16,128]{2,1,0:T(8,128)S(1)} %copy-done.24), channel_id=1, source_target_pairs={{0,6},{1,7},{2,4},{3,5},{4,2},{5,3},{6,0},{7,1},{8,14},{9,15},{10,... | collective-permute-start | bytes 442376 | tf_op jit(solution)/shard_map/ppermute | solution.py:360
  92.4 13.5 %copy-start.9 = (f32[18,16,128]{2,1,0:T(8,128)}, f32[18,16,128]{2,1,0:T(8,128)S(1)}, u32[]{:S(2)}) copy-start(f32[18,16,128]{2,1,0:T(8,128)S(1)} %collective-permute-done.14) | copy-start | bytes 442372
  92.4 7.8 %collective-permute-start.19 = (f32[18,16,128]{2,1,0:T(8,128)S(1)}, f32[18,16,128]{2,1,0:T(8,128)S(1)}, u32[]{:S(2)}, u32[]{:S(2)}) collective-permute-start(f32[18,16,128]{2,1,0:T(8,128)S(1)} %copy-done.23), channel_id=1, source_target_pairs={{0,7},{1,6},{2,5},{3,4},{4,3},{5,2},{6,1},{7,0},{8,15},{9,14},{10,... | collective-permute-start | bytes 442376 | tf_op jit(solution)/shard_map/ppermute | solution.py:360
  92.8 13.1 %copy-start.10 = (f32[18,16,128]{2,1,0:T(8,128)}, f32[18,16,128]{2,1,0:T(8,128)S(1)}, u32[]{:S(2)}) copy-start(f32[18,16,128]{2,1,0:T(8,128)S(1)} %collective-permute-done.15) | copy-start | bytes 442372
  92.8 8.0 %collective-permute-start.6 = (f32[18,16,128]{2,1,0:T(8,128)}, f32[18,16,128]{2,1,0:T(8,128)S(1)}, u32[]{:S(2)}, u32[]{:S(2)}) collective-permute-start(f32[18,16,128]{2,1,0:T(8,128)} %get-tuple-element.29), channel_id=1, source_target_pairs={{0,1},{1,0},{2,3},{3,2},{4,5},{5,4},{6,7},{7,6},{8,9},{9,8},{10,11... | collective-permute-start | bytes 442376 | tf_op jit(solution)/shard_map/ppermute | solution.py:360
  92.9 13.0 %copy-start.11 = (f32[18,16,128]{2,1,0:T(8,128)}, f32[18,16,128]{2,1,0:T(8,128)S(1)}, u32[]{:S(2)}) copy-start(f32[18,16,128]{2,1,0:T(8,128)S(1)} %collective-permute-done.16) | copy-start | bytes 442372
  92.9 9.6 %collective-permute-start.7 = (f32[18,16,128]{2,1,0:T(8,128)}, f32[18,16,128]{2,1,0:T(8,128)S(1)}, u32[]{:S(2)}, u32[]{:S(2)}) collective-permute-start(f32[18,16,128]{2,1,0:T(8,128)} %get-tuple-element.30), channel_id=1, source_target_pairs={{0,2},{1,3},{2,0},{3,1},{4,6},{5,7},{6,4},{7,5},{8,10},{9,11},{10,... | collective-permute-start | bytes 442376 | tf_op jit(solution)/shard_map/ppermute | solution.py:360
  94.7 11.2 %copy-start.12 = (f32[18,16,128]{2,1,0:T(8,128)}, f32[18,16,128]{2,1,0:T(8,128)S(1)}, u32[]{:S(2)}) copy-start(f32[18,16,128]{2,1,0:T(8,128)S(1)} %collective-permute-done.17) | copy-start | bytes 442372
  94.8 18.7 %collective-permute-start.8 = (f32[18,16,128]{2,1,0:T(8,128)}, f32[18,16,128]{2,1,0:T(8,128)S(1)}, u32[]{:S(2)}, u32[]{:S(2)}) collective-permute-start(f32[18,16,128]{2,1,0:T(8,128)} %get-tuple-element.31), channel_id=1, source_target_pairs={{0,3},{1,2},{2,1},{3,0},{4,7},{5,6},{6,5},{7,4},{8,11},{9,10},{10,... | collective-permute-start | bytes 442376 | tf_op jit(solution)/shard_map/ppermute | solution.py:360
  96.2 17.3 %collective-permute-start.9 = (f32[18,16,128]{2,1,0:T(8,128)}, f32[18,16,128]{2,1,0:T(8,128)S(1)}, u32[]{:S(2)}, u32[]{:S(2)}) collective-permute-start(f32[18,16,128]{2,1,0:T(8,128)} %get-tuple-element.32), channel_id=1, source_target_pairs={{0,4},{1,5},{2,6},{3,7},{4,0},{5,1},{6,2},{7,3},{8,12},{9,13},{10,... | collective-permute-start | bytes 442376 | tf_op jit(solution)/shard_map/ppermute | solution.py:360
  100.2 13.3 %collective-permute-start.10 = (f32[18,16,128]{2,1,0:T(8,128)}, f32[18,16,128]{2,1,0:T(8,128)S(1)}, u32[]{:S(2)}, u32[]{:S(2)}) collective-permute-start(f32[18,16,128]{2,1,0:T(8,128)} %get-tuple-element.33), channel_id=1, source_target_pairs={{0,5},{1,4},{2,7},{3,6},{4,1},{5,0},{6,3},{7,2},{8,13},{9,12},{10,... | collective-permute-start | bytes 442376 | tf_op jit(solution)/shard_map/ppermute | solution.py:360
  100.8 12.7 %copy-start.15 = (f32[18,16,128]{2,1,0:T(8,128)}, f32[18,16,128]{2,1,0:T(8,128)S(1)}, u32[]{:S(2)}) copy-start(f32[18,16,128]{2,1,0:T(8,128)S(1)} %collective-permute-done.6) | copy-start | bytes 442372
  100.8 12.7 %collective-permute-start.11 = (f32[18,16,128]{2,1,0:T(8,128)}, f32[18,16,128]{2,1,0:T(8,128)S(1)}, u32[]{:S(2)}, u32[]{:S(2)}) collective-permute-start(f32[18,16,128]{2,1,0:T(8,128)} %get-tuple-element.34), channel_id=1, source_target_pairs={{0,6},{1,7},{2,4},{3,5},{4,2},{5,3},{6,0},{7,1},{8,14},{9,15},{10,... | collective-permute-start | bytes 442376 | tf_op jit(solution)/shard_map/ppermute | solution.py:360
  102.5 11.1 %copy-start.16 = (f32[18,16,128]{2,1,0:T(8,128)}, f32[18,16,128]{2,1,0:T(8,128)S(1)}, u32[]{:S(2)}) copy-start(f32[18,16,128]{2,1,0:T(8,128)S(1)} %collective-permute-done.7) | copy-start | bytes 442372
  102.5 11.1 %collective-permute-start.12 = (f32[18,16,128]{2,1,0:T(8,128)}, f32[18,16,128]{2,1,0:T(8,128)S(1)}, u32[]{:S(2)}, u32[]{:S(2)}) collective-permute-start(f32[18,16,128]{2,1,0:T(8,128)} %get-tuple-element.35), channel_id=1, source_target_pairs={{0,7},{1,6},{2,5},{3,4},{4,3},{5,2},{6,1},{7,0},{8,15},{9,14},{10,... | collective-permute-start | bytes 442376 | tf_op jit(solution)/shard_map/ppermute | solution.py:360
  (14 other events, 36.1 us)

commit v3 on v2

--- a/solution.py
+++ b/solution.py
@@ -386,7 +386,7 @@
             if i < count:
                 after = []
                 if i and W_Z:
-                    after.append(held[i - 1][1])
+                    after.append(held[i - 1][3])
                 if i > 1 and W_X:
                     after.append(crossed[i - 2][0])
                 spread(i, after)

time: 124 us -> 118 us (0.952)
  starting transfers between devices: 35.1 us -> 31.9 us
  waiting for transfers between devices: 34.7 us -> 32 us
    ppermute x2, waiting for transfers between devices: 12.9 us -> 0.01 us  [spread(): down = lax.ppermute(own, 'chan', back_ring)]
    ppermute x2, waiting for transfers between devices: 4.06 us -> 10.6 us  [spread(): up = lax.ppermute(own, 'chan', ring)]
    ppermute x14, starting transfers between devices: 22.6 us -> 17.7 us  [send_back(): back.append(lax.ppermute(outs[m], 'win', [(d, d ^ m) for d in range(devs)]))]
    ppermute x2, waiting for transfers between devices: 7.07 us -> 10.7 us  [spread(): held[i] = [own, up, lax.ppermute(up, 'chan', ring), down]]
    ppermute x2, starting transfers between devices: 0.01 us -> 3.61 us  [spread(): held[i] = [own, up, lax.ppermute(up, 'chan', ring), down]]
    ppermute x2, starting transfers between devices: 2.3 us -> 0.01 us  [spread(): up = lax.ppermute(own, 'chan', ring)]
  transfers between devices with their start and end apart: 21 -> 21, of which waited for: 9 -> 8; matrix products, arithmetic and copies ran while one was open for 2% -> 2% of each run, Pallas kernels for 17% -> 18%
where the time goes in v3:
time: 118 us; the launch traced here: 117 us
  Pallas kernels  34.2 us (29%)
  waiting for transfers between devices  32 us (27%)
  starting transfers between devices  31.9 us (27%)
  blocking collectives  13.4 us (11%)
  local copies, waits for them, and re-layouts  3.12 us (3%)
  other arithmetic  1.93 us (2%)
    ppermute x14, starting transfers between devices, send_back(): back.append(lax.ppermute(outs[m], 'win', [(d, d ^ m) for d in range(devs)]))  17.7 us
    pallas_call x2, Pallas kernels, body(): pl.pallas_call(functools.partial(lag_kernel, n, devs, rows_out, windows,...  15.8 us
    pallas_call x2, Pallas kernels, cross_call(): pl.pallas_call(functools.partial(cross_kernel, groups, own_first), grid=(...  13.9 us
    all_to_all x1, blocking collectives, enter(): held[i] = [lax.all_to_all(block, 'win', 0, 0, tiled=True)]  13.4 us
    ppermute x2, waiting for transfers between devices, spread(): held[i] = [own, up, lax.ppermute(up, 'chan', ring), down]  10.7 us
    ppermute x2, waiting for transfers between devices, spread(): up = lax.ppermute(own, 'chan', ring)  10.6 us
    all_to_all x1, waiting for transfers between devices, enter(): held[i] = [lax.all_to_all(block, 'win', 0, 0, tiled=True)]  6.05 us
    ppermute x2, starting transfers between devices, spread(): down = lax.ppermute(own, 'chan', back_ring)  6.04 us
  transfers between devices with their start and end apart: 21, of which 8 were waited for; matrix products, arithmetic and copies ran while one was open for 2% of the time, Pallas kernels for 18%

profile of v3, /device:TPU:1, one launch (start us, length us, event | category | flops | bytes accessed | tf_op | source)
XLA Modules:
  0.0 117.5 jit_solution(1235004432153977386)
XLA Ops:
  0.6 4.5 %pack.1 = (bf16[8,7,32,128]{3,2,1,0:T(8,128)(2,1)}, bf16[8,6,32,128]{3,2,1,0:T(8,128)(2,1)}) custom-call(bf16[2,16,32,384]{3,2,1,0:T(8,128)(2,1)} %spectra_ref.1, s32[16,32]{1,0:T(8,128)} %valid_ref.1), custom_call_target="tpu_custom_call" | custom-call | bytes 15000000 | tf_op jit(solution)/shard_map/pack/pallas_call | solution.py:298
  5.1 13.4 %all_to_all.10.refs_1_.rest_4_.rest_0_ = bf16[8,7,32,128]{3,2,1,0:T(8,128)(2,1)S(1)} all-to-all(bf16[8,7,32,128]{3,2,1,0:T(8,128)(2,1)} %get-tuple-element.27), channel_id=1, replica_groups=mesh['chan'=4,'win'=8] {'win'}, dimensions={0} | all-to-all | bytes 917504 | tf_op jit(solution)/shard_map/all_to_all | solution.py:371
  18.5 3.3 %collective-permute-start = (bf16[8,7,32,128]{3,2,1,0:T(8,128)(2,1)S(1)}, bf16[8,7,32,128]{3,2,1,0:T(8,128)(2,1)S(1)}, u32[]{:S(2)}, u32[]{:S(2)}) collective-permute-start(bf16[8,7,32,128]{3,2,1,0:T(8,128)(2,1)S(1)} %all_to_all.10.refs_1_.rest_4_.rest_0_), channel_id=1, source_target_pairs={{0,24},{8,0},{16,8},{24,16},{1,25},{9,1},{17,9},{25,17},{2,26},{10... | collective-permute-start | bytes 1376264 | tf_op jit(solution)/shard_map/ppermute | solution.py:376
  21.9 4.6 %all-to-all-start.1 = ((bf16[8,6,32,128]{3,2,1,0:T(8,128)(2,1)}), bf16[8,6,32,128]{3,2,1,0:T(8,128)(2,1)S(1)}, u32[]{:S(2)}, u32[]{:S(2)}) async-start(bf16[8,6,32,128]{3,2,1,0:T(8,128)(2,1)} %join.2), calls=%async_computation.1 | async-start | bytes 786432 | tf_op jit(solution)/shard_map/all_to_all | solution.py:371
  26.5 6.0 %all-to-all-done.1.refs_0_ = bf16[8,6,32,128]{3,2,1,0:T(8,128)(2,1)S(1)} async-done(((bf16[8,6,32,128]{3,2,1,0:T(8,128)(2,1)}), bf16[8,6,32,128]{3,2,1,0:T(8,128)(2,1)S(1)}, u32[]{:S(2)}, u32[]{:S(2)}) %all-to-all-start.1) | async-done | bytes 393248 | tf_op jit(solution)/shard_map/all_to_all | solution.py:371
  32.5 0.7 copy-done.4
  33.3 0.8 copy-done.1
  34.1 0.7 iota_reduce_fusion.1
  34.8 6.6 %collective-permute-done.4.rest_5_.rest_1_ = bf16[8,7,32,128]{3,2,1,0:T(8,128)(2,1)S(1)} collective-permute-done((bf16[8,7,32,128]{3,2,1,0:T(8,128)(2,1)}, bf16[8,7,32,128]{3,2,1,0:T(8,128)(2,1)S(1)}, u32[]{:S(2)}, u32[]{:S(2)}) %collective-permute-start.4) | collective-permute-done | bytes 458784 | tf_op jit(solution)/shard_map/ppermute | solution.py:375
  41.4 1.8 %collective-permute-start.5 = (bf16[8,7,32,128]{3,2,1,0:T(8,128)(2,1)S(1)}, bf16[8,7,32,128]{3,2,1,0:T(8,128)(2,1)S(1)}, u32[]{:S(2)}, u32[]{:S(2)}) collective-permute-start(bf16[8,7,32,128]{3,2,1,0:T(8,128)(2,1)S(1)} %collective-permute-done.4.rest_5_.rest_1_), channel_id=1, source_target_pairs={{0,8},{8,16},{16,24},{24,0},{1,9},{9,17},{17,25},{25,1},{2,10},{10... | collective-permute-start | bytes 1376264 | tf_op jit(solution)/shard_map/ppermute | solution.py:377
  43.3 2.7 %collective-permute-start.3 = (bf16[8,6,32,128]{3,2,1,0:T(8,128)(2,1)}, bf16[8,6,32,128]{3,2,1,0:T(8,128)(2,1)S(1)}, u32[]{:S(2)}, u32[]{:S(2)}) collective-permute-start(bf16[8,6,32,128]{3,2,1,0:T(8,128)(2,1)} %join.3.rest_0_), channel_id=1, source_target_pairs={{0,24},{8,0},{16,8},{24,16},{1,25},{9,1},{17,9},{25,17},{2,26},{10... | collective-permute-start | bytes 1179656 | tf_op jit(solution)/shard_map/ppermute | solution.py:376
  46.0 3.9 %collective-permute-done.1.rest_1_ = bf16[8,6,32,128]{3,2,1,0:T(8,128)(2,1)S(1)} collective-permute-done((bf16[8,6,32,128]{3,2,1,0:T(8,128)(2,1)}, bf16[8,6,32,128]{3,2,1,0:T(8,128)(2,1)S(1)}, u32[]{:S(2)}, u32[]{:S(2)}) %collective-permute-start.1) | collective-permute-done | bytes 393248 | tf_op jit(solution)/shard_map/ppermute | solution.py:375
  49.9 1.8 %collective-permute-start.2 = (bf16[8,6,32,128]{3,2,1,0:T(8,128)(2,1)S(1)}, bf16[8,6,32,128]{3,2,1,0:T(8,128)(2,1)S(1)}, u32[]{:S(2)}, u32[]{:S(2)}) collective-permute-start(bf16[8,6,32,128]{3,2,1,0:T(8,128)(2,1)S(1)} %collective-permute-done.1.rest_1_), channel_id=1, source_target_pairs={{0,8},{8,16},{16,24},{24,0},{1,9},{9,17},{17,25},{25,1},{2,10},{10... | collective-permute-start | bytes 1179656 | tf_op jit(solution)/shard_map/ppermute | solution.py:377
  51.7 0.7 iota_reduce_fusion
  52.9 6.9 %collective-permute-done.5.rest_6_.rest_2_ = bf16[8,7,32,128]{3,2,1,0:T(8,128)(2,1)S(1)} collective-permute-done((bf16[8,7,32,128]{3,2,1,0:T(8,128)(2,1)S(1)}, bf16[8,7,32,128]{3,2,1,0:T(8,128)(2,1)S(1)}, u32[]{:S(2)}, u32[]{:S(2)}) %collective-permute-start.5) | collective-permute-done | bytes 458784 | tf_op jit(solution)/shard_map/ppermute | solution.py:377
  59.7 0.8 copy-done.3
  60.5 7.0 %cross.3 = (f32[18,16,128]{2,1,0:T(8,128)}, f32[18,16,128]{2,1,0:T(8,128)}, f32[18,16,128]{2,1,0:T(8,128)}, f32[18,16,128]{2,1,0:T(8,128)}, f32[18,16,128]{2,1,0...) custom-call(s32[8]{0:T(128)} %fusion.1.rows_ref, ...), custom_call_target="tpu_custom_call" | custom-call | bytes 24000000 | tf_op jit(solution)/shard_map/cross/pallas_call | solution.py:336
  67.6 3.4 %collective-permute-start.13 = (f32[18,16,128]{2,1,0:T(8,128)}, f32[18,16,128]{2,1,0:T(8,128)S(1)}, u32[]{:S(2)}, u32[]{:S(2)}) collective-permute-start(f32[18,16,128]{2,1,0:T(8,128)} %get-tuple-element.37), channel_id=1, source_target_pairs={{0,1},{1,0},{2,3},{3,2},{4,5},{5,4},{6,7},{7,6},{8,9},{9,8},{10,11... | collective-permute-start | bytes 442376 | tf_op jit(solution)/shard_map/ppermute | solution.py:360
  71.3 1.5 %collective-permute-start.15 = (f32[18,16,128]{2,1,0:T(8,128)}, f32[18,16,128]{2,1,0:T(8,128)S(1)}, u32[]{:S(2)}, u32[]{:S(2)}) collective-permute-start(f32[18,16,128]{2,1,0:T(8,128)} %get-tuple-element.39), channel_id=1, source_target_pairs={{0,3},{1,2},{2,1},{3,0},{4,7},{5,6},{6,5},{7,4},{8,11},{9,10},{10,... | collective-permute-start | bytes 442376 | tf_op jit(solution)/shard_map/ppermute | solution.py:360
  72.7 3.9 %collective-permute-done.2.rest_2_ = bf16[8,6,32,128]{3,2,1,0:T(8,128)(2,1)S(1)} collective-permute-done((bf16[8,6,32,128]{3,2,1,0:T(8,128)(2,1)S(1)}, bf16[8,6,32,128]{3,2,1,0:T(8,128)(2,1)S(1)}, u32[]{:S(2)}, u32[]{:S(2)}) %collective-permute-start.2) | collective-permute-done | bytes 393248 | tf_op jit(solution)/shard_map/ppermute | solution.py:377
  76.6 2.1 %collective-permute-start.17 = (f32[18,16,128]{2,1,0:T(8,128)}, f32[18,16,128]{2,1,0:T(8,128)S(1)}, u32[]{:S(2)}, u32[]{:S(2)}) collective-permute-start(f32[18,16,128]{2,1,0:T(8,128)} %get-tuple-element.41), channel_id=1, source_target_pairs={{0,5},{1,4},{2,7},{3,6},{4,1},{5,0},{6,3},{7,2},{8,13},{9,12},{10,... | collective-permute-start | bytes 442376 | tf_op jit(solution)/shard_map/ppermute | solution.py:360
  78.7 6.9 %cross.2 = (f32[18,16,128]{2,1,0:T(8,128)}, f32[18,16,128]{2,1,0:T(8,128)}, f32[18,16,128]{2,1,0:T(8,128)}, f32[18,16,128]{2,1,0:T(8,128)}, f32[18,16,128]{2,1,0...) custom-call(s32[8]{0:T(128)} %fusion.1.rows_ref, ...), custom_call_target="tpu_custom_call" | custom-call | bytes 24000000 | tf_op jit(solution)/shard_map/cross/pallas_call | solution.py:336
  85.6 1.6 %collective-permute-start.18 = (f32[18,16,128]{2,1,0:T(8,128)S(1)}, f32[18,16,128]{2,1,0:T(8,128)S(1)}, u32[]{:S(2)}, u32[]{:S(2)}) collective-permute-start(f32[18,16,128]{2,1,0:T(8,128)S(1)} %copy-done.24), channel_id=1, source_target_pairs={{0,6},{1,7},{2,4},{3,5},{4,2},{5,3},{6,0},{7,1},{8,14},{9,15},{10,... | collective-permute-start | bytes 442376 | tf_op jit(solution)/shard_map/ppermute | solution.py:360
  87.2 1.6 %collective-permute-start.19 = (f32[18,16,128]{2,1,0:T(8,128)S(1)}, f32[18,16,128]{2,1,0:T(8,128)S(1)}, u32[]{:S(2)}, u32[]{:S(2)}) collective-permute-start(f32[18,16,128]{2,1,0:T(8,128)S(1)} %copy-done.23), channel_id=1, source_target_pairs={{0,7},{1,6},{2,5},{3,4},{4,3},{5,2},{6,1},{7,0},{8,15},{9,14},{10,... | collective-permute-start | bytes 442376 | tf_op jit(solution)/shard_map/ppermute | solution.py:360
  88.8 0.7 collective-permute-start.7
  89.6 1.4 %collective-permute-start.8 = (f32[18,16,128]{2,1,0:T(8,128)}, f32[18,16,128]{2,1,0:T(8,128)S(1)}, u32[]{:S(2)}, u32[]{:S(2)}) collective-permute-start(f32[18,16,128]{2,1,0:T(8,128)} %get-tuple-element.31), channel_id=1, source_target_pairs={{0,3},{1,2},{2,1},{3,0},{4,7},{5,6},{6,5},{7,4},{8,11},{9,10},{10,... | collective-permute-start | bytes 442376 | tf_op jit(solution)/shard_map/ppermute | solution.py:360
  91.4 2.1 %collective-permute-start.9 = (f32[18,16,128]{2,1,0:T(8,128)}, f32[18,16,128]{2,1,0:T(8,128)S(1)}, u32[]{:S(2)}, u32[]{:S(2)}) collective-permute-start(f32[18,16,128]{2,1,0:T(8,128)} %get-tuple-element.32), channel_id=1, source_target_pairs={{0,4},{1,5},{2,6},{3,7},{4,0},{5,1},{6,2},{7,3},{8,12},{9,13},{10,... | collective-permute-start | bytes 442376 | tf_op jit(solution)/shard_map/ppermute | solution.py:360
  93.5 2.8 %collective-permute-done.19 = f32[18,16,128]{2,1,0:T(8,128)S(1)} collective-permute-done((f32[18,16,128]{2,1,0:T(8,128)S(1)}, f32[18,16,128]{2,1,0:T(8,128)S(1)}, u32[]{:S(2)}, u32[]{:S(2)}) %collective-permute-start.19) | collective-permute-done | bytes 147488 | tf_op jit(solution)/shard_map/ppermute | solution.py:360
  97.2 1.4 %collective-permute-done.7 = f32[18,16,128]{2,1,0:T(8,128)S(1)} collective-permute-done((f32[18,16,128]{2,1,0:T(8,128)}, f32[18,16,128]{2,1,0:T(8,128)S(1)}, u32[]{:S(2)}, u32[]{:S(2)}) %collective-permute-start.7) | collective-permute-done | bytes 147488 | tf_op jit(solution)/shard_map/ppermute | solution.py:360
  98.6 2.1 %collective-permute-start.12 = (f32[18,16,128]{2,1,0:T(8,128)}, f32[18,16,128]{2,1,0:T(8,128)S(1)}, u32[]{:S(2)}, u32[]{:S(2)}) collective-permute-start(f32[18,16,128]{2,1,0:T(8,128)} %get-tuple-element.35), channel_id=1, source_target_pairs={{0,7},{1,6},{2,5},{3,4},{4,3},{5,2},{6,1},{7,0},{8,15},{9,14},{10,... | collective-permute-start | bytes 442376 | tf_op jit(solution)/shard_map/ppermute | solution.py:360
  100.8 7.5 %lag.2 = (f32[16,32,1024]{2,1,0:T(8,128)}, f32[16,32,1024]{2,1,0:T(8,128)}) custom-call(s32[1]{0:T(128)} %bitcast.me_ref, f32[288,128]{1,0:T(8,128)} %bitcast.17, f32[288,128]{1,0:T(8,128)} %bitcast.18, f32[288,128]{1,0:T(8,128)} %bitcast.19, f32[288,128]{1,0:T(8,128)} %bitcast.20, f32[288,128]{1,0:T(8,128)} %bitcast.21, f32[288,128]{1,0:T(8,128)} %bitcast.22, ...), custom_call_target="tpu_custom_call" | custom-call | bytes 18000000 | tf_op jit(solution)/shard_map/lag/pallas_call | solution.py:416
  109.2 8.3 %lag.3 = (f32[16,32,1024]{2,1,0:T(8,128)}, f32[16,32,1024]{2,1,0:T(8,128)}) custom-call(s32[1]{0:T(128)} %bitcast.me_ref, f32[288,128]{1,0:T(8,128)} %bitcast.25, f32[288,128]{1,0:T(8,128)} %bitcast.26, f32[288,128]{1,0:T(8,128)} %bitcast.27, f32[288,128]{1,0:T(8,128)} %bitcast.28, f32[288,128]{1,0:T(8,128)} %bitcast.29, f32[288,128]{1,0:T(8,128)} %bitcast.30, ...), custom_call_target="tpu_custom_call" | custom-call | bytes 18000000 | tf_op jit(solution)/shard_map/lag/pallas_call | solution.py:416
  (73 shorter events, 3.0 us)
Async XLA Ops:
  5.1 28.9 %copy-start.22 = (s32[4]{0:T(128)S(1)}, s32[4]{0:T(128)}, u32[]{:S(2)}) copy-start(s32[4]{0:T(128)} %param.9) | copy-start | bytes 52
  18.5 14.0 %collective-permute-start = (bf16[8,7,32,128]{3,2,1,0:T(8,128)(2,1)S(1)}, bf16[8,7,32,128]{3,2,1,0:T(8,128)(2,1)S(1)}, u32[]{:S(2)}, u32[]{:S(2)}) collective-permute-start(bf16[8,7,32,128]{3,2,1,0:T(8,128)(2,1)S(1)} %all_to_all.10.refs_1_.rest_4_.rest_0_), channel_id=1, source_target_pairs={{0,24},{8,0},{16,8},{24,16},{1,25},{9,1},{17,9},{25,17},{2,26},{10... | collective-permute-start | bytes 1376264 | tf_op jit(solution)/shard_map/ppermute | solution.py:376
  21.9 10.7 %all-to-all-start.1 = ((bf16[8,6,32,128]{3,2,1,0:T(8,128)(2,1)}), bf16[8,6,32,128]{3,2,1,0:T(8,128)(2,1)S(1)}, u32[]{:S(2)}, u32[]{:S(2)}) async-start(bf16[8,6,32,128]{3,2,1,0:T(8,128)(2,1)} %join.2), calls=%async_computation.1 | async-start | bytes 786432 | tf_op jit(solution)/shard_map/all_to_all | solution.py:371
  26.5 15.0 %collective-permute-start.4 = (bf16[8,7,32,128]{3,2,1,0:T(8,128)(2,1)}, bf16[8,7,32,128]{3,2,1,0:T(8,128)(2,1)S(1)}, u32[]{:S(2)}, u32[]{:S(2)}) collective-permute-start(bf16[8,7,32,128]{3,2,1,0:T(8,128)(2,1)} %copy-done), channel_id=1, source_target_pairs={{0,8},{8,16},{16,24},{24,0},{1,9},{9,17},{17,25},{25,1},{2,10},{10... | collective-permute-start | bytes 1376264 | tf_op jit(solution)/shard_map/ppermute | solution.py:375
  34.1 15.9 %collective-permute-start.1 = (bf16[8,6,32,128]{3,2,1,0:T(8,128)(2,1)}, bf16[8,6,32,128]{3,2,1,0:T(8,128)(2,1)S(1)}, u32[]{:S(2)}, u32[]{:S(2)}) collective-permute-start(bf16[8,6,32,128]{3,2,1,0:T(8,128)(2,1)} %join.3.rest_0_), channel_id=1, source_target_pairs={{0,8},{8,16},{16,24},{24,0},{1,9},{9,17},{17,25},{25,1},{2,10},{10... | collective-permute-start | bytes 1179656 | tf_op jit(solution)/shard_map/ppermute | solution.py:375
  41.4 18.3 %copy-start.2 = (bf16[8,7,32,128]{3,2,1,0:T(8,128)(2,1)}, bf16[8,7,32,128]{3,2,1,0:T(8,128)(2,1)S(1)}, u32[]{:S(2)}) copy-start(bf16[8,7,32,128]{3,2,1,0:T(8,128)(2,1)S(1)} %collective-permute-done.4.rest_5_.rest_1_) | copy-start | bytes 1376260
  41.4 18.3 %collective-permute-start.5 = (bf16[8,7,32,128]{3,2,1,0:T(8,128)(2,1)S(1)}, bf16[8,7,32,128]{3,2,1,0:T(8,128)(2,1)S(1)}, u32[]{:S(2)}, u32[]{:S(2)}) collective-permute-start(bf16[8,7,32,128]{3,2,1,0:T(8,128)(2,1)S(1)} %collective-permute-done.4.rest_5_.rest_1_), channel_id=1, source_target_pairs={{0,8},{8,16},{16,24},{24,0},{1,9},{9,17},{17,25},{25,1},{2,10},{10... | collective-permute-start | bytes 1376264 | tf_op jit(solution)/shard_map/ppermute | solution.py:377
  43.3 29.4 %collective-permute-start.3 = (bf16[8,6,32,128]{3,2,1,0:T(8,128)(2,1)}, bf16[8,6,32,128]{3,2,1,0:T(8,128)(2,1)S(1)}, u32[]{:S(2)}, u32[]{:S(2)}) collective-permute-start(bf16[8,6,32,128]{3,2,1,0:T(8,128)(2,1)} %join.3.rest_0_), channel_id=1, source_target_pairs={{0,24},{8,0},{16,8},{24,16},{1,25},{9,1},{17,9},{25,17},{2,26},{10... | collective-permute-start | bytes 1179656 | tf_op jit(solution)/shard_map/ppermute | solution.py:376
  49.9 28.8 %copy-start.5 = (bf16[8,6,32,128]{3,2,1,0:T(8,128)(2,1)}, bf16[8,6,32,128]{3,2,1,0:T(8,128)(2,1)S(1)}, u32[]{:S(2)}) copy-start(bf16[8,6,32,128]{3,2,1,0:T(8,128)(2,1)S(1)} %collective-permute-done.1.rest_1_) | copy-start | bytes 1179652
  49.9 26.7 %collective-permute-start.2 = (bf16[8,6,32,128]{3,2,1,0:T(8,128)(2,1)S(1)}, bf16[8,6,32,128]{3,2,1,0:T(8,128)(2,1)S(1)}, u32[]{:S(2)}, u32[]{:S(2)}) collective-permute-start(bf16[8,6,32,128]{3,2,1,0:T(8,128)(2,1)S(1)} %collective-permute-done.1.rest_1_), channel_id=1, source_target_pairs={{0,8},{8,16},{16,24},{24,0},{1,9},{9,17},{17,25},{25,1},{2,10},{10... | collective-permute-start | bytes 1179656 | tf_op jit(solution)/shard_map/ppermute | solution.py:377
  67.5 18.0 %copy-start.24 = (f32[18,16,128]{2,1,0:T(8,128)S(1)}, f32[18,16,128]{2,1,0:T(8,128)}, u32[]{:S(2)}) copy-start(f32[18,16,128]{2,1,0:T(8,128)} %get-tuple-element.42) | copy-start | bytes 442372
  67.5 19.7 %copy-start.23 = (f32[18,16,128]{2,1,0:T(8,128)S(1)}, f32[18,16,128]{2,1,0:T(8,128)}, u32[]{:S(2)}) copy-start(f32[18,16,128]{2,1,0:T(8,128)} %get-tuple-element.43) | copy-start | bytes 442372
  67.6 18.0 %collective-permute-start.13 = (f32[18,16,128]{2,1,0:T(8,128)}, f32[18,16,128]{2,1,0:T(8,128)S(1)}, u32[]{:S(2)}, u32[]{:S(2)}) collective-permute-start(f32[18,16,128]{2,1,0:T(8,128)} %get-tuple-element.37), channel_id=1, source_target_pairs={{0,1},{1,0},{2,3},{3,2},{4,5},{5,4},{6,7},{7,6},{8,9},{9,8},{10,11... | collective-permute-start | bytes 442376 | tf_op jit(solution)/shard_map/ppermute | solution.py:360
  71.0 16.2 %collective-permute-start.14 = (f32[18,16,128]{2,1,0:T(8,128)}, f32[18,16,128]{2,1,0:T(8,128)S(1)}, u32[]{:S(2)}, u32[]{:S(2)}) collective-permute-start(f32[18,16,128]{2,1,0:T(8,128)} %get-tuple-element.38), channel_id=1, source_target_pairs={{0,2},{1,3},{2,0},{3,1},{4,6},{5,7},{6,4},{7,5},{8,10},{9,11},{10,... | collective-permute-start | bytes 442376 | tf_op jit(solution)/shard_map/ppermute | solution.py:360
  71.3 17.6 %collective-permute-start.15 = (f32[18,16,128]{2,1,0:T(8,128)}, f32[18,16,128]{2,1,0:T(8,128)S(1)}, u32[]{:S(2)}, u32[]{:S(2)}) collective-permute-start(f32[18,16,128]{2,1,0:T(8,128)} %get-tuple-element.39), channel_id=1, source_target_pairs={{0,3},{1,2},{2,1},{3,0},{4,7},{5,6},{6,5},{7,4},{8,11},{9,10},{10,... | collective-permute-start | bytes 442376 | tf_op jit(solution)/shard_map/ppermute | solution.py:360
  72.7 16.1 %collective-permute-start.16 = (f32[18,16,128]{2,1,0:T(8,128)}, f32[18,16,128]{2,1,0:T(8,128)S(1)}, u32[]{:S(2)}, u32[]{:S(2)}) collective-permute-start(f32[18,16,128]{2,1,0:T(8,128)} %get-tuple-element.40), channel_id=1, source_target_pairs={{0,4},{1,5},{2,6},{3,7},{4,0},{5,1},{6,2},{7,3},{8,12},{9,13},{10,... | collective-permute-start | bytes 442376 | tf_op jit(solution)/shard_map/ppermute | solution.py:360
  76.6 13.0 %collective-permute-start.17 = (f32[18,16,128]{2,1,0:T(8,128)}, f32[18,16,128]{2,1,0:T(8,128)S(1)}, u32[]{:S(2)}, u32[]{:S(2)}) collective-permute-start(f32[18,16,128]{2,1,0:T(8,128)} %get-tuple-element.41), channel_id=1, source_target_pairs={{0,5},{1,4},{2,7},{3,6},{4,1},{5,0},{6,3},{7,2},{8,13},{9,12},{10,... | collective-permute-start | bytes 442376 | tf_op jit(solution)/shard_map/ppermute | solution.py:360
  85.6 15.2 %copy-start.8 = (f32[18,16,128]{2,1,0:T(8,128)}, f32[18,16,128]{2,1,0:T(8,128)S(1)}, u32[]{:S(2)}) copy-start(f32[18,16,128]{2,1,0:T(8,128)S(1)} %collective-permute-done.13) | copy-start | bytes 442372
  85.6 5.8 %collective-permute-start.18 = (f32[18,16,128]{2,1,0:T(8,128)S(1)}, f32[18,16,128]{2,1,0:T(8,128)S(1)}, u32[]{:S(2)}, u32[]{:S(2)}) collective-permute-start(f32[18,16,128]{2,1,0:T(8,128)S(1)} %copy-done.24), channel_id=1, source_target_pairs={{0,6},{1,7},{2,4},{3,5},{4,2},{5,3},{6,0},{7,1},{8,14},{9,15},{10,... | collective-permute-start | bytes 442376 | tf_op jit(solution)/shard_map/ppermute | solution.py:360
  87.2 13.5 %copy-start.9 = (f32[18,16,128]{2,1,0:T(8,128)}, f32[18,16,128]{2,1,0:T(8,128)S(1)}, u32[]{:S(2)}) copy-start(f32[18,16,128]{2,1,0:T(8,128)S(1)} %collective-permute-done.14) | copy-start | bytes 442372
  87.2 9.1 %collective-permute-start.19 = (f32[18,16,128]{2,1,0:T(8,128)S(1)}, f32[18,16,128]{2,1,0:T(8,128)S(1)}, u32[]{:S(2)}, u32[]{:S(2)}) collective-permute-start(f32[18,16,128]{2,1,0:T(8,128)S(1)} %copy-done.23), channel_id=1, source_target_pairs={{0,7},{1,6},{2,5},{3,4},{4,3},{5,2},{6,1},{7,0},{8,15},{9,14},{10,... | collective-permute-start | bytes 442376 | tf_op jit(solution)/shard_map/ppermute | solution.py:360
  88.8 11.9 %copy-start.10 = (f32[18,16,128]{2,1,0:T(8,128)}, f32[18,16,128]{2,1,0:T(8,128)S(1)}, u32[]{:S(2)}) copy-start(f32[18,16,128]{2,1,0:T(8,128)S(1)} %collective-permute-done.15) | copy-start | bytes 442372
  88.8 8.1 %collective-permute-start.6 = (f32[18,16,128]{2,1,0:T(8,128)}, f32[18,16,128]{2,1,0:T(8,128)S(1)}, u32[]{:S(2)}, u32[]{:S(2)}) collective-permute-start(f32[18,16,128]{2,1,0:T(8,128)} %get-tuple-element.29), channel_id=1, source_target_pairs={{0,1},{1,0},{2,3},{3,2},{4,5},{5,4},{6,7},{7,6},{8,9},{9,8},{10,11... | collective-permute-start | bytes 442376 | tf_op jit(solution)/shard_map/ppermute | solution.py:360
  88.8 11.9 %copy-start.11 = (f32[18,16,128]{2,1,0:T(8,128)}, f32[18,16,128]{2,1,0:T(8,128)S(1)}, u32[]{:S(2)}) copy-start(f32[18,16,128]{2,1,0:T(8,128)S(1)} %collective-permute-done.16) | copy-start | bytes 442372
  88.8 9.8 %collective-permute-start.7 = (f32[18,16,128]{2,1,0:T(8,128)}, f32[18,16,128]{2,1,0:T(8,128)S(1)}, u32[]{:S(2)}, u32[]{:S(2)}) collective-permute-start(f32[18,16,128]{2,1,0:T(8,128)} %get-tuple-element.30), channel_id=1, source_target_pairs={{0,2},{1,3},{2,0},{3,1},{4,6},{5,7},{6,4},{7,5},{8,10},{9,11},{10,... | collective-permute-start | bytes 442376 | tf_op jit(solution)/shard_map/ppermute | solution.py:360
  89.6 11.2 %copy-start.12 = (f32[18,16,128]{2,1,0:T(8,128)}, f32[18,16,128]{2,1,0:T(8,128)S(1)}, u32[]{:S(2)}) copy-start(f32[18,16,128]{2,1,0:T(8,128)S(1)} %collective-permute-done.17) | copy-start | bytes 442372
  89.6 18.7 %collective-permute-start.8 = (f32[18,16,128]{2,1,0:T(8,128)}, f32[18,16,128]{2,1,0:T(8,128)S(1)}, u32[]{:S(2)}, u32[]{:S(2)}) collective-permute-start(f32[18,16,128]{2,1,0:T(8,128)} %get-tuple-element.31), channel_id=1, source_target_pairs={{0,3},{1,2},{2,1},{3,0},{4,7},{5,6},{6,5},{7,4},{8,11},{9,10},{10,... | collective-permute-start | bytes 442376 | tf_op jit(solution)/shard_map/ppermute | solution.py:360
  91.4 16.9 %collective-permute-start.9 = (f32[18,16,128]{2,1,0:T(8,128)}, f32[18,16,128]{2,1,0:T(8,128)S(1)}, u32[]{:S(2)}, u32[]{:S(2)}) collective-permute-start(f32[18,16,128]{2,1,0:T(8,128)} %get-tuple-element.32), channel_id=1, source_target_pairs={{0,4},{1,5},{2,6},{3,7},{4,0},{5,1},{6,2},{7,3},{8,12},{9,13},{10,... | collective-permute-start | bytes 442376 | tf_op jit(solution)/shard_map/ppermute | solution.py:360
  96.3 12.0 %collective-permute-start.10 = (f32[18,16,128]{2,1,0:T(8,128)}, f32[18,16,128]{2,1,0:T(8,128)S(1)}, u32[]{:S(2)}, u32[]{:S(2)}) collective-permute-start(f32[18,16,128]{2,1,0:T(8,128)} %get-tuple-element.33), channel_id=1, source_target_pairs={{0,5},{1,4},{2,7},{3,6},{4,1},{5,0},{6,3},{7,2},{8,13},{9,12},{10,... | collective-permute-start | bytes 442376 | tf_op jit(solution)/shard_map/ppermute | solution.py:360
  97.0 11.4 %copy-start.15 = (f32[18,16,128]{2,1,0:T(8,128)}, f32[18,16,128]{2,1,0:T(8,128)S(1)}, u32[]{:S(2)}) copy-start(f32[18,16,128]{2,1,0:T(8,128)S(1)} %collective-permute-done.6) | copy-start | bytes 442372
  97.0 11.4 %collective-permute-start.11 = (f32[18,16,128]{2,1,0:T(8,128)}, f32[18,16,128]{2,1,0:T(8,128)S(1)}, u32[]{:S(2)}, u32[]{:S(2)}) collective-permute-start(f32[18,16,128]{2,1,0:T(8,128)} %get-tuple-element.34), channel_id=1, source_target_pairs={{0,6},{1,7},{2,4},{3,5},{4,2},{5,3},{6,0},{7,1},{8,14},{9,15},{10,... | collective-permute-start | bytes 442376 | tf_op jit(solution)/shard_map/ppermute | solution.py:360
  98.6 9.7 %collective-permute-start.12 = (f32[18,16,128]{2,1,0:T(8,128)}, f32[18,16,128]{2,1,0:T(8,128)S(1)}, u32[]{:S(2)}, u32[]{:S(2)}) collective-permute-start(f32[18,16,128]{2,1,0:T(8,128)} %get-tuple-element.35), channel_id=1, source_target_pairs={{0,7},{1,6},{2,5},{3,4},{4,3},{5,2},{6,1},{7,0},{8,15},{9,14},{10,... | collective-permute-start | bytes 442376 | tf_op jit(solution)/shard_map/ppermute | solution.py:360
  (14 other events, 40.8 us)

commit v4 on v3

--- a/solution.py
+++ b/solution.py
@@ -21,11 +21,11 @@
 ROWS = 3
 PACK = 4
 CHUNKS = (1 / 2, 1 / 2)
-W_IN = 1
+W_IN = 0
 W_Z = 1
 W_X = 1
 W_O = 0
-VMEM = 60 * 1024 * 1024
+VMEM = 24 * 1024 * 1024
 
 
 def cost(micros):
@@ -120,7 +120,8 @@
     rows_out = outs[0].shape[1]
 
     def opened(ref, q, part):
-        return swap_blocks([ref[part * 8 + d, q].astype(jnp.float32) for d in range(8)], width)
+        moved = swap_blocks([ref[part * 8 + d, q] for d in range(8)], width)
+        return [block.astype(jnp.float32) for block in moved]
 
     scale_refs = list(scales) if own_first else list(scales) + [own_scale]
     for g, ref in enumerate(scale_refs):
@@ -195,7 +196,7 @@
                 out[q * ROWS + t] = packed[t, at, :]
         return carry
 
-    lax.fori_loop(0, slots, step, 0, unroll=2)
+    lax.fori_loop(0, slots, step, 0, unroll=3)
 
 
 def lag_kernel(slots, devs, rows_out, windows, freq, pieces, first, me_ref, *rest):
@@ -355,9 +356,9 @@
         )(token, *got, *heads)
 
     def send_back(outs):
-        back = [outs[0]]
-        for m in range(1, devs):
-            back.append(lax.ppermute(outs[m], "win", [(d, d ^ m) for d in range(devs)]))
+        back = [outs[0]] * devs
+        for m in range(devs - 1, 0, -1):
+            back[m] = lax.ppermute(outs[m], "win", [(d, d ^ m) for d in range(devs)])
         return back
 
     backs = [None] * count

time: 118 us -> 113 us (0.958)
  Pallas kernels: 34.2 us -> 24.3 us
  waiting for transfers between devices: 32 us -> 38.3 us
  starting transfers between devices: 31.9 us -> 30.2 us
  local copies, waits for them, and re-layouts: 3.12 us -> 4.39 us
    pallas_call x2, Pallas kernels: 13.9 us -> 9.1 us  [cross_call(): pl.pallas_call(functools.partial(cross_kernel, groups, own_first), grid=(...]
    pallas_call x2, Pallas kernels: 15.8 us -> 12 us  [body(): pl.pallas_call(functools.partial(lag_kernel, n, devs, rows_out, windows,...]
    ppermute x14, waiting for transfers between devices: 4.67 us -> 8.07 us  [send_back(): back[m] = lax.ppermute(outs[m], 'win', [(d, d ^ m) for d in range(devs)])]
    ppermute x2, waiting for transfers between devices: 10.7 us -> 13.3 us  [spread(): held[i] = [own, up, lax.ppermute(up, 'chan', ring), down]]
    ppermute x14, starting transfers between devices: 17.7 us -> 15.9 us  [send_back(): back[m] = lax.ppermute(outs[m], 'win', [(d, d ^ m) for d in range(devs)])]
    pallas_call x1, Pallas kernels: 4.49 us -> 3.2 us  [body(): pl.pallas_call(functools.partial(pack_kernel, sizes, devs), out_shape=[ja...]
    unnamed x50 -> x24, local copies, waits for them, and re-layouts: 3.12 us -> 4.39 us
  transfers between devices with their start and end apart: 21 -> 21, of which waited for: 8 -> 10; matrix products, arithmetic and copies ran while one was open for 2% -> 1% of each run, Pallas kernels for 18% -> 13%
where the time goes in v4:
time: 113 us; the launch traced here: 112 us
  waiting for transfers between devices  38.3 us (34%)
  starting transfers between devices  30.2 us (27%)
  Pallas kernels  24.3 us (22%)
  blocking collectives  13.1 us (12%)
  local copies, waits for them, and re-layouts  4.39 us (4%)
  other arithmetic  1.27 us (1%)
    ppermute x14, starting transfers between devices, send_back(): back[m] = lax.ppermute(outs[m], 'win', [(d, d ^ m) for d in range(devs)])  15.9 us
    ppermute x2, waiting for transfers between devices, spread(): held[i] = [own, up, lax.ppermute(up, 'chan', ring), down]  13.3 us
    all_to_all x1, blocking collectives, enter(): held[i] = [lax.all_to_all(block, 'win', 0, 0, tiled=True)]  13.1 us
    pallas_call x2, Pallas kernels, body(): pl.pallas_call(functools.partial(lag_kernel, n, devs, rows_out, windows,...  12 us
    ppermute x2, waiting for transfers between devices, spread(): up = lax.ppermute(own, 'chan', ring)  10.6 us
    pallas_call x2, Pallas kernels, cross_call(): pl.pallas_call(functools.partial(cross_kernel, groups, own_first), grid=(...  9.1 us
    ppermute x14, waiting for transfers between devices, send_back(): back[m] = lax.ppermute(outs[m], 'win', [(d, d ^ m) for d in range(devs)])  8.07 us
    ppermute x2, starting transfers between devices, spread(): down = lax.ppermute(own, 'chan', back_ring)  6.14 us
  transfers between devices with their start and end apart: 21, of which 10 were waited for; matrix products, arithmetic and copies ran while one was open for 1% of the time, Pallas kernels for 13%

profile of v4, /device:TPU:1, one launch (start us, length us, event | category | flops | bytes accessed | tf_op | source)
XLA Modules:
  0.0 112.3 jit_solution(16816465298082994076)
XLA Ops:
  0.6 1.1 %copy-done.9 = bf16[2,16,32,384]{3,2,1,0:T(8,128)(2,1)S(1)} copy-done((bf16[2,16,32,384]{3,2,1,0:T(8,128)(2,1)S(1)}, bf16[2,16,32,384]{3,2,1,0:T(8,128)(2,1)}, u32[]{:S(2)}) %copy-start.9) | copy-done | bytes 786456
  2.5 3.2 %pack.1 = (bf16[8,7,32,128]{3,2,1,0:T(8,128)(2,1)S(1)}, bf16[8,6,32,128]{3,2,1,0:T(8,128)(2,1)}) custom-call(bf16[2,16,32,384]{3,2,1,0:T(8,128)(2,1)S(1)} %copy-done.9, s32[16,32]{1,0:T(8,128)S(1)} %copy-done.10), custom_call_target="tpu_custom_call" | custom-call | bytes 15000000 | tf_op jit(solution)/shard_map/pack/pallas_call | solution.py:299
  5.7 13.1 %all_to_all.10.rest_4_.rest_0_ = bf16[8,7,32,128]{3,2,1,0:T(8,128)(2,1)S(1)} all-to-all(bf16[8,7,32,128]{3,2,1,0:T(8,128)(2,1)S(1)} %get-tuple-element.27), channel_id=1, replica_groups=mesh['chan'=4,'win'=8] {'win'}, dimensions={0} | all-to-all | bytes 917504 | tf_op jit(solution)/shard_map/all_to_all | solution.py:372
  18.7 3.3 %collective-permute-start = (bf16[8,7,32,128]{3,2,1,0:T(8,128)(2,1)S(1)}, bf16[8,7,32,128]{3,2,1,0:T(8,128)(2,1)S(1)}, u32[]{:S(2)}, u32[]{:S(2)}) collective-permute-start(bf16[8,7,32,128]{3,2,1,0:T(8,128)(2,1)S(1)} %all_to_all.10.rest_4_.rest_0_), channel_id=1, source_target_pairs={{0,24},{8,0},{16,8},{24,16},{1,25},{9,1},{17,9},{25,17},{2,26},{10... | collective-permute-start | bytes 1376264 | tf_op jit(solution)/shard_map/ppermute | solution.py:377
  22.1 4.6 %all-to-all-start = ((bf16[8,6,32,128]{3,2,1,0:T(8,128)(2,1)}), bf16[8,6,32,128]{3,2,1,0:T(8,128)(2,1)S(1)}, u32[]{:S(2)}, u32[]{:S(2)}) async-start(bf16[8,6,32,128]{3,2,1,0:T(8,128)(2,1)} %get-tuple-element.26), calls=%async_computation | async-start | bytes 786432 | tf_op jit(solution)/shard_map/all_to_all | solution.py:372
  26.7 6.0 %all-to-all-done.refs_0_ = bf16[8,6,32,128]{3,2,1,0:T(8,128)(2,1)S(1)} async-done(((bf16[8,6,32,128]{3,2,1,0:T(8,128)(2,1)}), bf16[8,6,32,128]{3,2,1,0:T(8,128)(2,1)S(1)}, u32[]{:S(2)}, u32[]{:S(2)}) %all-to-all-start) | async-done | bytes 393248 | tf_op jit(solution)/shard_map/all_to_all | solution.py:372
  33.5 0.8 copy-done
  34.9 6.7 %collective-permute-done.4.rest_5_.rest_1_ = bf16[8,7,32,128]{3,2,1,0:T(8,128)(2,1)S(1)} collective-permute-done((bf16[8,7,32,128]{3,2,1,0:T(8,128)(2,1)S(1)}, bf16[8,7,32,128]{3,2,1,0:T(8,128)(2,1)S(1)}, u32[]{:S(2)}, u32[]{:S(2)}) %collective-permute-start.4) | collective-permute-done | bytes 458784 | tf_op jit(solution)/shard_map/ppermute | solution.py:376
  41.6 1.7 %collective-permute-start.5 = (bf16[8,7,32,128]{3,2,1,0:T(8,128)(2,1)S(1)}, bf16[8,7,32,128]{3,2,1,0:T(8,128)(2,1)S(1)}, u32[]{:S(2)}, u32[]{:S(2)}) collective-permute-start(bf16[8,7,32,128]{3,2,1,0:T(8,128)(2,1)S(1)} %collective-permute-done.4.rest_5_.rest_1_), channel_id=1, source_target_pairs={{0,8},{8,16},{16,24},{24,0},{1,9},{9,17},{17,25},{25,1},{2,10},{10... | collective-permute-start | bytes 1376264 | tf_op jit(solution)/shard_map/ppermute | solution.py:378
  43.4 2.8 %collective-permute-start.3 = (bf16[8,6,32,128]{3,2,1,0:T(8,128)(2,1)}, bf16[8,6,32,128]{3,2,1,0:T(8,128)(2,1)S(1)}, u32[]{:S(2)}, u32[]{:S(2)}) collective-permute-start(bf16[8,6,32,128]{3,2,1,0:T(8,128)(2,1)} %join.1.rest_0_), channel_id=1, source_target_pairs={{0,24},{8,0},{16,8},{24,16},{1,25},{9,1},{17,9},{25,17},{2,26},{10... | collective-permute-start | bytes 1179656 | tf_op jit(solution)/shard_map/ppermute | solution.py:377
  46.2 3.9 %collective-permute-done.1.rest_1_ = bf16[8,6,32,128]{3,2,1,0:T(8,128)(2,1)S(1)} collective-permute-done((bf16[8,6,32,128]{3,2,1,0:T(8,128)(2,1)}, bf16[8,6,32,128]{3,2,1,0:T(8,128)(2,1)S(1)}, u32[]{:S(2)}, u32[]{:S(2)}) %collective-permute-start.1) | collective-permute-done | bytes 393248 | tf_op jit(solution)/shard_map/ppermute | solution.py:376
  50.1 1.8 %collective-permute-start.2 = (bf16[8,6,32,128]{3,2,1,0:T(8,128)(2,1)S(1)}, bf16[8,6,32,128]{3,2,1,0:T(8,128)(2,1)S(1)}, u32[]{:S(2)}, u32[]{:S(2)}) collective-permute-start(bf16[8,6,32,128]{3,2,1,0:T(8,128)(2,1)S(1)} %collective-permute-done.1.rest_1_), channel_id=1, source_target_pairs={{0,8},{8,16},{16,24},{24,0},{1,9},{9,17},{17,25},{25,1},{2,10},{10... | collective-permute-start | bytes 1179656 | tf_op jit(solution)/shard_map/ppermute | solution.py:378
  52.5 7.5 %collective-permute-done.5.rest_6_.rest_2_ = bf16[8,7,32,128]{3,2,1,0:T(8,128)(2,1)S(1)} collective-permute-done((bf16[8,7,32,128]{3,2,1,0:T(8,128)(2,1)S(1)}, bf16[8,7,32,128]{3,2,1,0:T(8,128)(2,1)S(1)}, u32[]{:S(2)}, u32[]{:S(2)}) %collective-permute-start.5) | collective-permute-done | bytes 458784 | tf_op jit(solution)/shard_map/ppermute | solution.py:378
  59.9 1.0 copy-done.1
  61.0 4.6 %cross.3 = (f32[18,16,128]{2,1,0:T(8,128)S(1)}, f32[18,16,128]{2,1,0:T(8,128)S(1)}, f32[18,16,128]{2,1,0:T(8,128)S(1)}, f32[18,16,128]{2,1,0:T(8,128)S(1)}, f32[...) custom-call(s32[8]{0:T(128)S(1)} %fusion.1.rows_ref, ...), custom_call_target="tpu_custom_call" | custom-call | bytes 24000000 | tf_op jit(solution)/shard_map/cross/pallas_call | solution.py:337
  65.6 3.5 %collective-permute-start.13 = (f32[18,16,128]{2,1,0:T(8,128)S(1)}, f32[18,16,128]{2,1,0:T(8,128)S(1)}, u32[]{:S(2)}, u32[]{:S(2)}) collective-permute-start(f32[18,16,128]{2,1,0:T(8,128)S(1)} %get-tuple-element.37), channel_id=1, source_target_pairs={{0,1},{1,0},{2,3},{3,2},{4,5},{5,4},{6,7},{7,6},{8,9},{9,8},{10,11... | collective-permute-start | bytes 442376 | tf_op jit(solution)/shard_map/ppermute | solution.py:361
  69.2 1.5 %collective-permute-start.15 = (f32[18,16,128]{2,1,0:T(8,128)S(1)}, f32[18,16,128]{2,1,0:T(8,128)S(1)}, u32[]{:S(2)}, u32[]{:S(2)}) collective-permute-start(f32[18,16,128]{2,1,0:T(8,128)S(1)} %get-tuple-element.39), channel_id=1, source_target_pairs={{0,3},{1,2},{2,1},{3,0},{4,7},{5,6},{6,5},{7,4},{8,11},{9,10},{10,... | collective-permute-start | bytes 442376 | tf_op jit(solution)/shard_map/ppermute | solution.py:361
  71.0 5.8 %collective-permute-done.2.rest_2_ = bf16[8,6,32,128]{3,2,1,0:T(8,128)(2,1)S(1)} collective-permute-done((bf16[8,6,32,128]{3,2,1,0:T(8,128)(2,1)S(1)}, bf16[8,6,32,128]{3,2,1,0:T(8,128)(2,1)S(1)}, u32[]{:S(2)}, u32[]{:S(2)}) %collective-permute-start.2) | collective-permute-done | bytes 393248 | tf_op jit(solution)/shard_map/ppermute | solution.py:378
  76.8 2.1 %collective-permute-start.17 = (f32[18,16,128]{2,1,0:T(8,128)S(1)}, f32[18,16,128]{2,1,0:T(8,128)S(1)}, u32[]{:S(2)}, u32[]{:S(2)}) collective-permute-start(f32[18,16,128]{2,1,0:T(8,128)S(1)} %get-tuple-element.41), channel_id=1, source_target_pairs={{0,5},{1,4},{2,7},{3,6},{4,1},{5,0},{6,3},{7,2},{8,13},{9,12},{10,... | collective-permute-start | bytes 442376 | tf_op jit(solution)/shard_map/ppermute | solution.py:361
  78.9 4.5 %cross.2 = (f32[18,16,128]{2,1,0:T(8,128)S(1)}, f32[18,16,128]{2,1,0:T(8,128)S(1)}, f32[18,16,128]{2,1,0:T(8,128)S(1)}, f32[18,16,128]{2,1,0:T(8,128)S(1)}, f32[...) custom-call(s32[8]{0:T(128)S(1)} %fusion.1.rows_ref, ...), custom_call_target="tpu_custom_call" | custom-call | bytes 24000000 | tf_op jit(solution)/shard_map/cross/pallas_call | solution.py:337
  83.5 1.6 %collective-permute-start.18 = (f32[18,16,128]{2,1,0:T(8,128)S(1)}, f32[18,16,128]{2,1,0:T(8,128)S(1)}, u32[]{:S(2)}, u32[]{:S(2)}) collective-permute-start(f32[18,16,128]{2,1,0:T(8,128)S(1)} %get-tuple-element.42), channel_id=1, source_target_pairs={{0,6},{1,7},{2,4},{3,5},{4,2},{5,3},{6,0},{7,1},{8,14},{9,15},{10,... | collective-permute-start | bytes 442376 | tf_op jit(solution)/shard_map/ppermute | solution.py:361
  85.1 0.8 collective-permute-start.19
  86.8 1.2 %collective-permute-start.8 = (f32[18,16,128]{2,1,0:T(8,128)S(1)}, f32[18,16,128]{2,1,0:T(8,128)S(1)}, u32[]{:S(2)}, u32[]{:S(2)}) collective-permute-start(f32[18,16,128]{2,1,0:T(8,128)S(1)} %get-tuple-element.31), channel_id=1, source_target_pairs={{0,3},{1,2},{2,1},{3,0},{4,7},{5,6},{6,5},{7,4},{8,11},{9,10},{10,... | collective-permute-start | bytes 442376 | tf_op jit(solution)/shard_map/ppermute | solution.py:361
  88.1 1.9 %collective-permute-done.18 = f32[18,16,128]{2,1,0:T(8,128)S(1)} collective-permute-done((f32[18,16,128]{2,1,0:T(8,128)S(1)}, f32[18,16,128]{2,1,0:T(8,128)S(1)}, u32[]{:S(2)}, u32[]{:S(2)}) %collective-permute-start.18) | collective-permute-done | bytes 147488 | tf_op jit(solution)/shard_map/ppermute | solution.py:361
  90.0 1.1 %collective-permute-start.9 = (f32[18,16,128]{2,1,0:T(8,128)S(1)}, f32[18,16,128]{2,1,0:T(8,128)S(1)}, u32[]{:S(2)}, u32[]{:S(2)}) collective-permute-start(f32[18,16,128]{2,1,0:T(8,128)S(1)} %get-tuple-element.32), channel_id=1, source_target_pairs={{0,4},{1,5},{2,6},{3,7},{4,0},{5,1},{6,2},{7,3},{8,12},{9,13},{10,... | collective-permute-start | bytes 442376 | tf_op jit(solution)/shard_map/ppermute | solution.py:361
  91.1 2.3 %collective-permute-done.19 = f32[18,16,128]{2,1,0:T(8,128)S(1)} collective-permute-done((f32[18,16,128]{2,1,0:T(8,128)S(1)}, f32[18,16,128]{2,1,0:T(8,128)S(1)}, u32[]{:S(2)}, u32[]{:S(2)}) %collective-permute-start.19) | collective-permute-done | bytes 147488 | tf_op jit(solution)/shard_map/ppermute | solution.py:361
  93.5 1.4 %collective-permute-start.10 = (f32[18,16,128]{2,1,0:T(8,128)S(1)}, f32[18,16,128]{2,1,0:T(8,128)S(1)}, u32[]{:S(2)}, u32[]{:S(2)}) collective-permute-start(f32[18,16,128]{2,1,0:T(8,128)S(1)} %get-tuple-element.33), channel_id=1, source_target_pairs={{0,5},{1,4},{2,7},{3,6},{4,1},{5,0},{6,3},{7,2},{8,13},{9,12},{10,... | collective-permute-start | bytes 442376 | tf_op jit(solution)/shard_map/ppermute | solution.py:361
  95.2 1.4 %collective-permute-done.7 = f32[18,16,128]{2,1,0:T(8,128)S(1)} collective-permute-done((f32[18,16,128]{2,1,0:T(8,128)S(1)}, f32[18,16,128]{2,1,0:T(8,128)S(1)}, u32[]{:S(2)}, u32[]{:S(2)}) %collective-permute-start.7) | collective-permute-done | bytes 147488 | tf_op jit(solution)/shard_map/ppermute | solution.py:361
  96.6 1.2 %collective-permute-start.12 = (f32[18,16,128]{2,1,0:T(8,128)S(1)}, f32[18,16,128]{2,1,0:T(8,128)S(1)}, u32[]{:S(2)}, u32[]{:S(2)}) collective-permute-start(f32[18,16,128]{2,1,0:T(8,128)S(1)} %get-tuple-element.35), channel_id=1, source_target_pairs={{0,7},{1,6},{2,5},{3,4},{4,3},{5,2},{6,1},{7,0},{8,15},{9,14},{10,... | collective-permute-start | bytes 442376 | tf_op jit(solution)/shard_map/ppermute | solution.py:361
  97.8 5.5 %lag.2 = (f32[16,32,1024]{2,1,0:T(8,128)S(1)}, f32[16,32,1024]{2,1,0:T(8,128)S(1)}) custom-call(s32[1]{0:T(128)} %bitcast.me_ref, f32[288,128]{1,0:T(8,128)S(1)} %bitcast.17, f32[288,128]{1,0:T(8,128)S(1)} %bitcast.18, f32[288,128]{1,0:T(8,128)S(1)} %bitcast.19, f32[288,128]{1,0:T(8,128)S(1)} %bitcast.20, f32[288,128]{1,0:T(8,128)S(1)} %bitcast.21, ...), custom_call_target="tpu_custom_call" | custom-call | bytes 18000000 | tf_op jit(solution)/shard_map/lag/pallas_call | solution.py:417
  103.4 2.4 %collective-permute-done.12 = f32[18,16,128]{2,1,0:T(8,128)S(1)} collective-permute-done((f32[18,16,128]{2,1,0:T(8,128)S(1)}, f32[18,16,128]{2,1,0:T(8,128)S(1)}, u32[]{:S(2)}, u32[]{:S(2)}) %collective-permute-start.12) | collective-permute-done | bytes 147488 | tf_op jit(solution)/shard_map/ppermute | solution.py:361
  105.8 6.4 %lag.3 = (f32[16,32,1024]{2,1,0:T(8,128)}, f32[16,32,1024]{2,1,0:T(8,128)}) custom-call(s32[1]{0:T(128)} %bitcast.me_ref, f32[288,128]{1,0:T(8,128)S(1)} %bitcast.25, f32[288,128]{1,0:T(8,128)S(1)} %bitcast.26, f32[288,128]{1,0:T(8,128)S(1)} %bitcast.27, f32[288,128]{1,0:T(8,128)S(1)} %bitcast.28, f32[288,128]{1,0:T(8,128)S(1)} %bitcast.29, ...), custom_call_target="tpu_custom_call" | custom-call | bytes 18000000 | tf_op jit(solution)/shard_map/lag/pallas_call | solution.py:417
  (46 shorter events, 4.5 us)
Async XLA Ops:
  0.6 1.1 %copy-start.9 = (bf16[2,16,32,384]{3,2,1,0:T(8,128)(2,1)S(1)}, bf16[2,16,32,384]{3,2,1,0:T(8,128)(2,1)}, u32[]{:S(2)}) copy-start(bf16[2,16,32,384]{3,2,1,0:T(8,128)(2,1)} %spectra_ref.1) | copy-start | bytes 2359300
  2.5 31.8 %copy-start.11 = (s32[4]{0:T(128)S(1)}, s32[4]{0:T(128)}, u32[]{:S(2)}) copy-start(s32[4]{0:T(128)} %param.9) | copy-start | bytes 52
  18.7 14.0 %collective-permute-start = (bf16[8,7,32,128]{3,2,1,0:T(8,128)(2,1)S(1)}, bf16[8,7,32,128]{3,2,1,0:T(8,128)(2,1)S(1)}, u32[]{:S(2)}, u32[]{:S(2)}) collective-permute-start(bf16[8,7,32,128]{3,2,1,0:T(8,128)(2,1)S(1)} %all_to_all.10.rest_4_.rest_0_), channel_id=1, source_target_pairs={{0,24},{8,0},{16,8},{24,16},{1,25},{9,1},{17,9},{25,17},{2,26},{10... | collective-permute-start | bytes 1376264 | tf_op jit(solution)/shard_map/ppermute | solution.py:377
  22.1 10.7 %all-to-all-start = ((bf16[8,6,32,128]{3,2,1,0:T(8,128)(2,1)}), bf16[8,6,32,128]{3,2,1,0:T(8,128)(2,1)S(1)}, u32[]{:S(2)}, u32[]{:S(2)}) async-start(bf16[8,6,32,128]{3,2,1,0:T(8,128)(2,1)} %get-tuple-element.26), calls=%async_computation | async-start | bytes 786432 | tf_op jit(solution)/shard_map/all_to_all | solution.py:372
  26.7 15.0 %collective-permute-start.4 = (bf16[8,7,32,128]{3,2,1,0:T(8,128)(2,1)S(1)}, bf16[8,7,32,128]{3,2,1,0:T(8,128)(2,1)S(1)}, u32[]{:S(2)}, u32[]{:S(2)}) collective-permute-start(bf16[8,7,32,128]{3,2,1,0:T(8,128)(2,1)S(1)} %all_to_all.10.rest_4_.rest_0_), channel_id=1, source_target_pairs={{0,8},{8,16},{16,24},{24,0},{1,9},{9,17},{17,25},{25,1},{2,10},{10... | collective-permute-start | bytes 1376264 | tf_op jit(solution)/shard_map/ppermute | solution.py:376
  32.7 0.7 copy-start.3
  33.5 0.8 copy-start
  34.2 15.9 %collective-permute-start.1 = (bf16[8,6,32,128]{3,2,1,0:T(8,128)(2,1)}, bf16[8,6,32,128]{3,2,1,0:T(8,128)(2,1)S(1)}, u32[]{:S(2)}, u32[]{:S(2)}) collective-permute-start(bf16[8,6,32,128]{3,2,1,0:T(8,128)(2,1)} %join.1.rest_0_), channel_id=1, source_target_pairs={{0,8},{8,16},{16,24},{24,0},{1,9},{9,17},{17,25},{25,1},{2,10},{10... | collective-permute-start | bytes 1179656 | tf_op jit(solution)/shard_map/ppermute | solution.py:376
  41.6 18.3 %collective-permute-start.5 = (bf16[8,7,32,128]{3,2,1,0:T(8,128)(2,1)S(1)}, bf16[8,7,32,128]{3,2,1,0:T(8,128)(2,1)S(1)}, u32[]{:S(2)}, u32[]{:S(2)}) collective-permute-start(bf16[8,7,32,128]{3,2,1,0:T(8,128)(2,1)S(1)} %collective-permute-done.4.rest_5_.rest_1_), channel_id=1, source_target_pairs={{0,8},{8,16},{16,24},{24,0},{1,9},{9,17},{17,25},{25,1},{2,10},{10... | collective-permute-start | bytes 1376264 | tf_op jit(solution)/shard_map/ppermute | solution.py:378
  43.4 27.6 %collective-permute-start.3 = (bf16[8,6,32,128]{3,2,1,0:T(8,128)(2,1)}, bf16[8,6,32,128]{3,2,1,0:T(8,128)(2,1)S(1)}, u32[]{:S(2)}, u32[]{:S(2)}) collective-permute-start(bf16[8,6,32,128]{3,2,1,0:T(8,128)(2,1)} %join.1.rest_0_), channel_id=1, source_target_pairs={{0,24},{8,0},{16,8},{24,16},{1,25},{9,1},{17,9},{25,17},{2,26},{10... | collective-permute-start | bytes 1179656 | tf_op jit(solution)/shard_map/ppermute | solution.py:377
  50.1 26.7 %collective-permute-start.2 = (bf16[8,6,32,128]{3,2,1,0:T(8,128)(2,1)S(1)}, bf16[8,6,32,128]{3,2,1,0:T(8,128)(2,1)S(1)}, u32[]{:S(2)}, u32[]{:S(2)}) collective-permute-start(bf16[8,6,32,128]{3,2,1,0:T(8,128)(2,1)S(1)} %collective-permute-done.1.rest_1_), channel_id=1, source_target_pairs={{0,8},{8,16},{16,24},{24,0},{1,9},{9,17},{17,25},{25,1},{2,10},{10... | collective-permute-start | bytes 1179656 | tf_op jit(solution)/shard_map/ppermute | solution.py:378
  59.9 1.0 copy-start.1
  61.0 17.9 %copy-start.2 = (bf16[8,7,32,128]{3,2,1,0:T(8,128)(2,1)S(1)}, bf16[8,7,32,128]{3,2,1,0:T(8,128)(2,1)}, u32[]{:S(2)}) copy-start(bf16[8,7,32,128]{3,2,1,0:T(8,128)(2,1)} %copy-done) | copy-start | bytes 1376260
  61.0 17.9 %copy-start.4 = (bf16[8,6,32,128]{3,2,1,0:T(8,128)(2,1)S(1)}, bf16[8,6,32,128]{3,2,1,0:T(8,128)(2,1)}, u32[]{:S(2)}) copy-start(bf16[8,6,32,128]{3,2,1,0:T(8,128)(2,1)} %join.1.rest_0_) | copy-start | bytes 1179652
  65.5 32.3 %copy-start.5 = (bf16[512,1024]{1,0:T(8,128)(2,1)S(1)}, bf16[512,1024]{1,0:T(8,128)(2,1)}, u32[]{:S(2)}) copy-start(bf16[512,1024]{1,0:T(8,128)(2,1)} %constant.61.clone.rest_9_) | copy-start | bytes 3145732
  65.5 32.2 %copy-start.6 = (bf16[512,1024]{1,0:T(8,128)(2,1)S(1)}, bf16[512,1024]{1,0:T(8,128)(2,1)}, u32[]{:S(2)}) copy-start(bf16[512,1024]{1,0:T(8,128)(2,1)} %constant.60.clone.rest_8_) | copy-start | bytes 3145732
  65.6 17.9 %collective-permute-start.13 = (f32[18,16,128]{2,1,0:T(8,128)S(1)}, f32[18,16,128]{2,1,0:T(8,128)S(1)}, u32[]{:S(2)}, u32[]{:S(2)}) collective-permute-start(f32[18,16,128]{2,1,0:T(8,128)S(1)} %get-tuple-element.37), channel_id=1, source_target_pairs={{0,1},{1,0},{2,3},{3,2},{4,5},{5,4},{6,7},{7,6},{8,9},{9,8},{10,11... | collective-permute-start | bytes 442376 | tf_op jit(solution)/shard_map/ppermute | solution.py:361
  69.0 16.1 %collective-permute-start.14 = (f32[18,16,128]{2,1,0:T(8,128)S(1)}, f32[18,16,128]{2,1,0:T(8,128)S(1)}, u32[]{:S(2)}, u32[]{:S(2)}) collective-permute-start(f32[18,16,128]{2,1,0:T(8,128)S(1)} %get-tuple-element.38), channel_id=1, source_target_pairs={{0,2},{1,3},{2,0},{3,1},{4,6},{5,7},{6,4},{7,5},{8,10},{9,11},{10,... | collective-permute-start | bytes 442376 | tf_op jit(solution)/shard_map/ppermute | solution.py:361
  69.2 16.7 %collective-permute-start.15 = (f32[18,16,128]{2,1,0:T(8,128)S(1)}, f32[18,16,128]{2,1,0:T(8,128)S(1)}, u32[]{:S(2)}, u32[]{:S(2)}) collective-permute-start(f32[18,16,128]{2,1,0:T(8,128)S(1)} %get-tuple-element.39), channel_id=1, source_target_pairs={{0,3},{1,2},{2,1},{3,0},{4,7},{5,6},{6,5},{7,4},{8,11},{9,10},{10,... | collective-permute-start | bytes 442376 | tf_op jit(solution)/shard_map/ppermute | solution.py:361
  71.0 15.3 %collective-permute-start.16 = (f32[18,16,128]{2,1,0:T(8,128)S(1)}, f32[18,16,128]{2,1,0:T(8,128)S(1)}, u32[]{:S(2)}, u32[]{:S(2)}) collective-permute-start(f32[18,16,128]{2,1,0:T(8,128)S(1)} %get-tuple-element.40), channel_id=1, source_target_pairs={{0,4},{1,5},{2,6},{3,7},{4,0},{5,1},{6,2},{7,3},{8,12},{9,13},{10,... | collective-permute-start | bytes 442376 | tf_op jit(solution)/shard_map/ppermute | solution.py:361
  76.8 10.0 %collective-permute-start.17 = (f32[18,16,128]{2,1,0:T(8,128)S(1)}, f32[18,16,128]{2,1,0:T(8,128)S(1)}, u32[]{:S(2)}, u32[]{:S(2)}) collective-permute-start(f32[18,16,128]{2,1,0:T(8,128)S(1)} %get-tuple-element.41), channel_id=1, source_target_pairs={{0,5},{1,4},{2,7},{3,6},{4,1},{5,0},{6,3},{7,2},{8,13},{9,12},{10,... | collective-permute-start | bytes 442376 | tf_op jit(solution)/shard_map/ppermute | solution.py:361
  83.4 22.4 %copy-start.7 = (bf16[512,1024]{1,0:T(8,128)(2,1)S(1)}, bf16[512,1024]{1,0:T(8,128)(2,1)}, u32[]{:S(2)}) copy-start(bf16[512,1024]{1,0:T(8,128)(2,1)} %constant.63.clone.rest_9_) | copy-start | bytes 3145732
  83.4 22.4 %copy-start.8 = (bf16[512,1024]{1,0:T(8,128)(2,1)S(1)}, bf16[512,1024]{1,0:T(8,128)(2,1)}, u32[]{:S(2)}) copy-start(bf16[512,1024]{1,0:T(8,128)(2,1)} %constant.62.clone.rest_8_) | copy-start | bytes 3145732
  83.5 6.5 %collective-permute-start.18 = (f32[18,16,128]{2,1,0:T(8,128)S(1)}, f32[18,16,128]{2,1,0:T(8,128)S(1)}, u32[]{:S(2)}, u32[]{:S(2)}) collective-permute-start(f32[18,16,128]{2,1,0:T(8,128)S(1)} %get-tuple-element.42), channel_id=1, source_target_pairs={{0,6},{1,7},{2,4},{3,5},{4,2},{5,3},{6,0},{7,1},{8,14},{9,15},{10,... | collective-permute-start | bytes 442376 | tf_op jit(solution)/shard_map/ppermute | solution.py:361
  85.1 8.4 %collective-permute-start.19 = (f32[18,16,128]{2,1,0:T(8,128)S(1)}, f32[18,16,128]{2,1,0:T(8,128)S(1)}, u32[]{:S(2)}, u32[]{:S(2)}) collective-permute-start(f32[18,16,128]{2,1,0:T(8,128)S(1)} %get-tuple-element.43), channel_id=1, source_target_pairs={{0,7},{1,6},{2,5},{3,4},{4,3},{5,2},{6,1},{7,0},{8,15},{9,14},{10,... | collective-permute-start | bytes 442376 | tf_op jit(solution)/shard_map/ppermute | solution.py:361
  85.9 8.9 %collective-permute-start.6 = (f32[18,16,128]{2,1,0:T(8,128)S(1)}, f32[18,16,128]{2,1,0:T(8,128)S(1)}, u32[]{:S(2)}, u32[]{:S(2)}) collective-permute-start(f32[18,16,128]{2,1,0:T(8,128)S(1)} %get-tuple-element.29), channel_id=1, source_target_pairs={{0,1},{1,0},{2,3},{3,2},{4,5},{5,4},{6,7},{7,6},{8,9},{9,8},{10,11... | collective-permute-start | bytes 442376 | tf_op jit(solution)/shard_map/ppermute | solution.py:361
  86.3 10.3 %collective-permute-start.7 = (f32[18,16,128]{2,1,0:T(8,128)S(1)}, f32[18,16,128]{2,1,0:T(8,128)S(1)}, u32[]{:S(2)}, u32[]{:S(2)}) collective-permute-start(f32[18,16,128]{2,1,0:T(8,128)S(1)} %get-tuple-element.30), channel_id=1, source_target_pairs={{0,2},{1,3},{2,0},{3,1},{4,6},{5,7},{6,4},{7,5},{8,10},{9,11},{10,... | collective-permute-start | bytes 442376 | tf_op jit(solution)/shard_map/ppermute | solution.py:361
  86.8 16.5 %collective-permute-start.8 = (f32[18,16,128]{2,1,0:T(8,128)S(1)}, f32[18,16,128]{2,1,0:T(8,128)S(1)}, u32[]{:S(2)}, u32[]{:S(2)}) collective-permute-start(f32[18,16,128]{2,1,0:T(8,128)S(1)} %get-tuple-element.31), channel_id=1, source_target_pairs={{0,3},{1,2},{2,1},{3,0},{4,7},{5,6},{6,5},{7,4},{8,11},{9,10},{10,... | collective-permute-start | bytes 442376 | tf_op jit(solution)/shard_map/ppermute | solution.py:361
  90.0 13.4 %collective-permute-start.9 = (f32[18,16,128]{2,1,0:T(8,128)S(1)}, f32[18,16,128]{2,1,0:T(8,128)S(1)}, u32[]{:S(2)}, u32[]{:S(2)}) collective-permute-start(f32[18,16,128]{2,1,0:T(8,128)S(1)} %get-tuple-element.32), channel_id=1, source_target_pairs={{0,4},{1,5},{2,6},{3,7},{4,0},{5,1},{6,2},{7,3},{8,12},{9,13},{10,... | collective-permute-start | bytes 442376 | tf_op jit(solution)/shard_map/ppermute | solution.py:361
  93.5 9.9 %collective-permute-start.10 = (f32[18,16,128]{2,1,0:T(8,128)S(1)}, f32[18,16,128]{2,1,0:T(8,128)S(1)}, u32[]{:S(2)}, u32[]{:S(2)}) collective-permute-start(f32[18,16,128]{2,1,0:T(8,128)S(1)} %get-tuple-element.33), channel_id=1, source_target_pairs={{0,5},{1,4},{2,7},{3,6},{4,1},{5,0},{6,3},{7,2},{8,13},{9,12},{10,... | collective-permute-start | bytes 442376 | tf_op jit(solution)/shard_map/ppermute | solution.py:361
  94.9 8.5 %collective-permute-start.11 = (f32[18,16,128]{2,1,0:T(8,128)S(1)}, f32[18,16,128]{2,1,0:T(8,128)S(1)}, u32[]{:S(2)}, u32[]{:S(2)}) collective-permute-start(f32[18,16,128]{2,1,0:T(8,128)S(1)} %get-tuple-element.34), channel_id=1, source_target_pairs={{0,6},{1,7},{2,4},{3,5},{4,2},{5,3},{6,0},{7,1},{8,14},{9,15},{10,... | collective-permute-start | bytes 442376 | tf_op jit(solution)/shard_map/ppermute | solution.py:361
  96.6 9.2 %collective-permute-start.12 = (f32[18,16,128]{2,1,0:T(8,128)S(1)}, f32[18,16,128]{2,1,0:T(8,128)S(1)}, u32[]{:S(2)}, u32[]{:S(2)}) collective-permute-start(f32[18,16,128]{2,1,0:T(8,128)S(1)} %get-tuple-element.35), channel_id=1, source_target_pairs={{0,7},{1,6},{2,5},{3,4},{4,3},{5,2},{6,1},{7,0},{8,15},{9,14},{10,... | collective-permute-start | bytes 442376 | tf_op jit(solution)/shard_map/ppermute | solution.py:361
  (1 other events, 0.7 us)

commit v5 on v4

--- a/solution.py
+++ b/solution.py
@@ -99,20 +99,22 @@
     return arrays
 
 
-def cross_kernel(groups, own_first, rows_ref, *rest):
+def cross_kernel(groups, own_first, first, rows_ref, *rest):
     blocks = rest[:groups]
     rest = rest[groups:]
     own = blocks[0]
     if not own_first:
         own, rest = rest[0], rest[1:]
-    scales = rest[:groups]
-    rest = rest[groups:]
-    own_scale = scales[0]
-    if not own_first:
-        own_scale, rest = rest[0], rest[1:]
-    devs, chans = own_scale.shape[0], own_scale.shape[2]
+    if first:
+        count = groups + (not own_first)
+        scale_refs, rest = rest[:count], rest[count:]
+    else:
+        (factor, cap, inv), rest = rest[:3], rest[3:]
+    devs, chans = own.shape[0], own.shape[2]
     outs, rest = rest[:devs], rest[devs:]
-    factor, cap, src_white, src_unit, recv_white, recv_unit, inv, packed = rest
+    if first:
+        (factor, cap, inv), rest = rest[:3], rest[3:]
+    src_white, src_unit, recv_white, recv_unit, packed = rest
     width = 128 // 8
     parts = devs // 8
     half = parts * 128
@@ -123,20 +125,20 @@
         moved = swap_blocks([ref[part * 8 + d, q] for d in range(8)], width)
         return [block.astype(jnp.float32) for block in moved]
 
-    scale_refs = list(scales) if own_first else list(scales) + [own_scale]
-    for g, ref in enumerate(scale_refs):
-        for part in range(parts):
-            got = opened(ref, 0, part)
-            value = got[0] + got[1] + got[2]
-            factor[pl.ds(g * chans, chans), pl.ds(part * 128, 128)] = value
-            cap[pl.ds(g * chans, chans), pl.ds(part * 128, 128)] = jnp.where(value > 0, 1.0 / phase_floor, 0.0)
-    masks = jnp.where(cap[...] > 0, 1.0, 0.0).astype(jnp.bfloat16)
-    mine = 0 if own_first else groups * chans
-    recv = jnp.concatenate([masks[mine : mine + chans]] * 4, axis=0)
-    counts = lax.dot_general(
-        masks[: groups * chans], recv, (((1,), (1,)), ((), ())), preferred_element_type=jnp.float32
-    )
-    inv[...] = 1.0 / jnp.maximum(counts, 1.0)
+    if first:
+        for g, ref in enumerate(scale_refs):
+            for part in range(parts):
+                got = opened(ref, 0, part)
+                value = got[0] + got[1] + got[2]
+                factor[pl.ds(g * chans, chans), pl.ds(part * 128, 128)] = value
+                cap[pl.ds(g * chans, chans), pl.ds(part * 128, 128)] = jnp.where(value > 0, 1.0 / phase_floor, 0.0)
+        masks = jnp.where(cap[...] > 0, 1.0, 0.0).astype(jnp.bfloat16)
+        mine = 0 if own_first else groups * chans
+        recv = jnp.concatenate([masks[mine : mine + chans]] * 4, axis=0)
+        counts = lax.dot_general(
+            masks[: groups * chans], recv, (((1,), (1,)), ((), ())), preferred_element_type=jnp.float32
+        )
+        inv[...] = 1.0 / jnp.maximum(counts, 1.0)
     data_refs = list(blocks) if own_first else list(blocks) + [own]
 
     def step(q, carry):
@@ -326,34 +328,48 @@
     ring = [(i, (i + 1) % stations) for i in range(stations)]
     count = len(sizes)
 
+    shared = []
+
     def cross_call(i, token, got, heads):
         n = sizes[i]
         rows = groups * chans if own_first else (groups + 1) * chans
         half = win_dev * devs
         last = sizes[0]
-        whole = pl.BlockSpec((devs, n + (i == 0), chans, 128), lambda s: (0, 0, 0, 0))
-        tail = pl.BlockSpec((devs, 1, chans, 128), lambda s: (0, last, 0, 0))
+        first = i == 0
+        whole = pl.BlockSpec((devs, n + first, chans, 128), lambda s: (0, 0, 0, 0))
         shape = (n * ROWS, rows_out, 128)
-        return pl.pallas_call(
-            functools.partial(cross_kernel, groups, own_first),
+        flat = lambda s: (0, 0)
+        tables = [(rows, half), (rows, half), (groups * chans, 128)]
+        table_specs = [pl.BlockSpec(t, flat) for t in tables]
+        out_specs = [pl.BlockSpec(shape, lambda s: (0, 0, 0))] * devs
+        out_shape = [jax.ShapeDtypeStruct(shape, jnp.float32)] * devs
+        if first:
+            extra = list(heads)
+            extra_specs = [pl.BlockSpec((devs, 1, chans, 128), lambda s: (0, last, 0, 0))] * len(heads)
+            out_specs = out_specs + table_specs
+            out_shape = out_shape + [jax.ShapeDtypeStruct(t, jnp.float32) for t in tables]
+        else:
+            extra, extra_specs = list(shared), table_specs
+        result = pl.pallas_call(
+            functools.partial(cross_kernel, groups, own_first, first),
             grid=(1,),
-            in_specs=[pl.BlockSpec(memory_space=pltpu.SMEM)] + [whole] * len(got) + [tail] * len(got),
-            out_specs=[pl.BlockSpec(shape, lambda s: (0, 0, 0))] * devs,
-            out_shape=[jax.ShapeDtypeStruct(shape, jnp.float32)] * devs,
+            in_specs=[pl.BlockSpec(memory_space=pltpu.SMEM)] + [whole] * len(got) + extra_specs,
+            out_specs=out_specs,
+            out_shape=out_shape,
             scratch_shapes=[
-                pltpu.VMEM((rows, half), jnp.float32),
-                pltpu.VMEM((rows, half), jnp.float32),
                 pltpu.VMEM((PACK, groups * chans, 2 * half), jnp.bfloat16),
                 pltpu.VMEM((PACK, groups * chans, 2 * half), jnp.bfloat16),
                 pltpu.VMEM((PACK, 4 * chans, 2 * half), jnp.bfloat16),
                 pltpu.VMEM((PACK, 8 * chans, 2 * half), jnp.bfloat16),
-                pltpu.VMEM((groups * chans, 128), jnp.float32),
                 pltpu.VMEM((ROWS, groups * chans, 128), jnp.float32),
             ],
             compiler_params=params,
-            cost_estimate=cost(2 + n),
+            cost_estimate=cost(1 + first + n),
             name="cross",
-        )(token, *got, *heads)
+        )(token, *got, *extra)
+        if first:
+            shared.extend(result[devs:])
+        return result[:devs]
 
     def send_back(outs):
         back = [outs[0]] * devs

time: 113 us -> 113 us (level)
    unnamed x24 -> x22, local copies, waits for them, and re-layouts: 4.39 us -> 4.38 us
where the time goes in v5:
time: 113 us; the launch traced here: 112 us
  waiting for transfers between devices  38.2 us (34%)
  starting transfers between devices  30.2 us (27%)
  Pallas kernels  23.9 us (21%)
  blocking collectives  13.1 us (12%)
  local copies, waits for them, and re-layouts  4.38 us (4%)
  other arithmetic  1.37 us (1%)
    ppermute x14, starting transfers between devices, send_back(): back[m] = lax.ppermute(outs[m], 'win', [(d, d ^ m) for d in range(devs)])  15.9 us
    ppermute x2, waiting for transfers between devices, spread(): held[i] = [own, up, lax.ppermute(up, 'chan', ring), down]  13.2 us
    all_to_all x1, blocking collectives, enter(): held[i] = [lax.all_to_all(block, 'win', 0, 0, tiled=True)]  13.1 us
    pallas_call x2, Pallas kernels, body(): pl.pallas_call(functools.partial(lag_kernel, n, devs, rows_out, windows,...  12 us
    ppermute x2, waiting for transfers between devices, spread(): up = lax.ppermute(own, 'chan', ring)  10.6 us
    pallas_call x2, Pallas kernels, cross_call(): pl.pallas_call(functools.partial(cross_kernel, groups, own_first, first),...  8.7 us
    ppermute x14, waiting for transfers between devices, send_back(): back[m] = lax.ppermute(outs[m], 'win', [(d, d ^ m) for d in range(devs)])  8.1 us
    ppermute x2, starting transfers between devices, spread(): down = lax.ppermute(own, 'chan', back_ring)  6.14 us
  transfers between devices with their start and end apart: 21, of which 10 were waited for; matrix products, arithmetic and copies ran while one was open for 1% of the time, Pallas kernels for 13%

profile of v5, /device:TPU:1, one launch (start us, length us, event | category | flops | bytes accessed | tf_op | source)
XLA Modules:
  0.0 111.9 jit_solution(13845321401457885001)
XLA Ops:
  0.6 1.1 %copy-done.8 = bf16[2,16,32,384]{3,2,1,0:T(8,128)(2,1)S(1)} copy-done((bf16[2,16,32,384]{3,2,1,0:T(8,128)(2,1)S(1)}, bf16[2,16,32,384]{3,2,1,0:T(8,128)(2,1)}, u32[]{:S(2)}) %copy-start.8) | copy-done | bytes 786456
  2.5 3.2 %pack.1 = (bf16[8,7,32,128]{3,2,1,0:T(8,128)(2,1)S(1)}, bf16[8,6,32,128]{3,2,1,0:T(8,128)(2,1)}) custom-call(bf16[2,16,32,384]{3,2,1,0:T(8,128)(2,1)S(1)} %copy-done.8, s32[16,32]{1,0:T(8,128)S(1)} %copy-done.9), custom_call_target="tpu_custom_call" | custom-call | bytes 15000000 | tf_op jit(solution)/shard_map/pack/pallas_call | solution.py:301
  5.7 13.1 %all_to_all.10.rest_0_.rest_4_ = bf16[8,7,32,128]{3,2,1,0:T(8,128)(2,1)S(1)} all-to-all(bf16[8,7,32,128]{3,2,1,0:T(8,128)(2,1)S(1)} %get-tuple-element.30), channel_id=1, replica_groups=mesh['chan'=4,'win'=8] {'win'}, dimensions={0} | all-to-all | bytes 917504 | tf_op jit(solution)/shard_map/all_to_all | solution.py:388
  18.7 3.3 %collective-permute-start = (bf16[8,7,32,128]{3,2,1,0:T(8,128)(2,1)S(1)}, bf16[8,7,32,128]{3,2,1,0:T(8,128)(2,1)S(1)}, u32[]{:S(2)}, u32[]{:S(2)}) collective-permute-start(bf16[8,7,32,128]{3,2,1,0:T(8,128)(2,1)S(1)} %all_to_all.10.rest_0_.rest_4_), channel_id=1, source_target_pairs={{0,24},{8,0},{16,8},{24,16},{1,25},{9,1},{17,9},{25,17},{2,26},{10... | collective-permute-start | bytes 1376264 | tf_op jit(solution)/shard_map/ppermute | solution.py:393
  22.1 4.6 %all-to-all-start = ((bf16[8,6,32,128]{3,2,1,0:T(8,128)(2,1)}), bf16[8,6,32,128]{3,2,1,0:T(8,128)(2,1)S(1)}, u32[]{:S(2)}, u32[]{:S(2)}) async-start(bf16[8,6,32,128]{3,2,1,0:T(8,128)(2,1)} %get-tuple-element.29), calls=%async_computation | async-start | bytes 786432 | tf_op jit(solution)/shard_map/all_to_all | solution.py:388
  26.7 6.0 %all-to-all-done.refs_0_ = bf16[8,6,32,128]{3,2,1,0:T(8,128)(2,1)S(1)} async-done(((bf16[8,6,32,128]{3,2,1,0:T(8,128)(2,1)}), bf16[8,6,32,128]{3,2,1,0:T(8,128)(2,1)S(1)}, u32[]{:S(2)}, u32[]{:S(2)}) %all-to-all-start) | async-done | bytes 393248 | tf_op jit(solution)/shard_map/all_to_all | solution.py:388
  33.5 0.8 copy-done
  35.0 6.7 %collective-permute-done.4.rest_1_.rest_5_ = bf16[8,7,32,128]{3,2,1,0:T(8,128)(2,1)S(1)} collective-permute-done((bf16[8,7,32,128]{3,2,1,0:T(8,128)(2,1)S(1)}, bf16[8,7,32,128]{3,2,1,0:T(8,128)(2,1)S(1)}, u32[]{:S(2)}, u32[]{:S(2)}) %collective-permute-start.4) | collective-permute-done | bytes 458784 | tf_op jit(solution)/shard_map/ppermute | solution.py:392
  41.6 1.7 %collective-permute-start.5 = (bf16[8,7,32,128]{3,2,1,0:T(8,128)(2,1)S(1)}, bf16[8,7,32,128]{3,2,1,0:T(8,128)(2,1)S(1)}, u32[]{:S(2)}, u32[]{:S(2)}) collective-permute-start(bf16[8,7,32,128]{3,2,1,0:T(8,128)(2,1)S(1)} %collective-permute-done.4.rest_1_.rest_5_), channel_id=1, source_target_pairs={{0,8},{8,16},{16,24},{24,0},{1,9},{9,17},{17,25},{25,1},{2,10},{10... | collective-permute-start | bytes 1376264 | tf_op jit(solution)/shard_map/ppermute | solution.py:394
  43.4 2.8 %collective-permute-start.3 = (bf16[8,6,32,128]{3,2,1,0:T(8,128)(2,1)}, bf16[8,6,32,128]{3,2,1,0:T(8,128)(2,1)S(1)}, u32[]{:S(2)}, u32[]{:S(2)}) collective-permute-start(bf16[8,6,32,128]{3,2,1,0:T(8,128)(2,1)} %join.1.rest_0_), channel_id=1, source_target_pairs={{0,24},{8,0},{16,8},{24,16},{1,25},{9,1},{17,9},{25,17},{2,26},{10... | collective-permute-start | bytes 1179656 | tf_op jit(solution)/shard_map/ppermute | solution.py:393
  46.2 3.9 %collective-permute-done.1.rest_1_ = bf16[8,6,32,128]{3,2,1,0:T(8,128)(2,1)S(1)} collective-permute-done((bf16[8,6,32,128]{3,2,1,0:T(8,128)(2,1)}, bf16[8,6,32,128]{3,2,1,0:T(8,128)(2,1)S(1)}, u32[]{:S(2)}, u32[]{:S(2)}) %collective-permute-start.1) | collective-permute-done | bytes 393248 | tf_op jit(solution)/shard_map/ppermute | solution.py:392
  50.1 1.8 %collective-permute-start.2 = (bf16[8,6,32,128]{3,2,1,0:T(8,128)(2,1)S(1)}, bf16[8,6,32,128]{3,2,1,0:T(8,128)(2,1)S(1)}, u32[]{:S(2)}, u32[]{:S(2)}) collective-permute-start(bf16[8,6,32,128]{3,2,1,0:T(8,128)(2,1)S(1)} %collective-permute-done.1.rest_1_), channel_id=1, source_target_pairs={{0,8},{8,16},{16,24},{24,0},{1,9},{9,17},{17,25},{25,1},{2,10},{10... | collective-permute-start | bytes 1179656 | tf_op jit(solution)/shard_map/ppermute | solution.py:394
  52.5 7.4 %collective-permute-done.5.rest_2_.rest_6_ = bf16[8,7,32,128]{3,2,1,0:T(8,128)(2,1)S(1)} collective-permute-done((bf16[8,7,32,128]{3,2,1,0:T(8,128)(2,1)S(1)}, bf16[8,7,32,128]{3,2,1,0:T(8,128)(2,1)S(1)}, u32[]{:S(2)}, u32[]{:S(2)}) %collective-permute-start.5) | collective-permute-done | bytes 458784 | tf_op jit(solution)/shard_map/ppermute | solution.py:394
  59.9 1.0 copy-done.1
  61.0 4.5 %cross.2 = (f32[18,16,128]{2,1,0:T(8,128)S(1)}, f32[18,16,128]{2,1,0:T(8,128)S(1)}, f32[18,16,128]{2,1,0:T(8,128)S(1)}, f32[18,16,128]{2,1,0:T(8,128)S(1)}, f32[...) custom-call(s32[8]{0:T(128)S(1)} %fusion.1.rows_ref, ...), custom_call_target="tpu_custom_call" | custom-call | bytes 24000000 | tf_op jit(solution)/shard_map/cross/pallas_call | solution.py:353
  65.5 3.5 %collective-permute-start.13 = (f32[18,16,128]{2,1,0:T(8,128)S(1)}, f32[18,16,128]{2,1,0:T(8,128)S(1)}, u32[]{:S(2)}, u32[]{:S(2)}) collective-permute-start(f32[18,16,128]{2,1,0:T(8,128)S(1)} %get-tuple-element.43), channel_id=1, source_target_pairs={{0,1},{1,0},{2,3},{3,2},{4,5},{5,4},{6,7},{7,6},{8,9},{9,8},{10,11... | collective-permute-start | bytes 442376 | tf_op jit(solution)/shard_map/ppermute | solution.py:377
  69.2 1.5 %collective-permute-start.15 = (f32[18,16,128]{2,1,0:T(8,128)S(1)}, f32[18,16,128]{2,1,0:T(8,128)S(1)}, u32[]{:S(2)}, u32[]{:S(2)}) collective-permute-start(f32[18,16,128]{2,1,0:T(8,128)S(1)} %get-tuple-element.45), channel_id=1, source_target_pairs={{0,3},{1,2},{2,1},{3,0},{4,7},{5,6},{6,5},{7,4},{8,11},{9,10},{10,... | collective-permute-start | bytes 442376 | tf_op jit(solution)/shard_map/ppermute | solution.py:377
  71.0 5.8 %collective-permute-done.2.rest_2_ = bf16[8,6,32,128]{3,2,1,0:T(8,128)(2,1)S(1)} collective-permute-done((bf16[8,6,32,128]{3,2,1,0:T(8,128)(2,1)S(1)}, bf16[8,6,32,128]{3,2,1,0:T(8,128)(2,1)S(1)}, u32[]{:S(2)}, u32[]{:S(2)}) %collective-permute-start.2) | collective-permute-done | bytes 393248 | tf_op jit(solution)/shard_map/ppermute | solution.py:394
  76.8 2.1 %collective-permute-start.17 = (f32[18,16,128]{2,1,0:T(8,128)S(1)}, f32[18,16,128]{2,1,0:T(8,128)S(1)}, u32[]{:S(2)}, u32[]{:S(2)}) collective-permute-start(f32[18,16,128]{2,1,0:T(8,128)S(1)} %get-tuple-element.47), channel_id=1, source_target_pairs={{0,5},{1,4},{2,7},{3,6},{4,1},{5,0},{6,3},{7,2},{8,13},{9,12},{10,... | collective-permute-start | bytes 442376 | tf_op jit(solution)/shard_map/ppermute | solution.py:377
  78.9 4.2 %cross.3 = (f32[18,16,128]{2,1,0:T(8,128)S(1)}, f32[18,16,128]{2,1,0:T(8,128)S(1)}, f32[18,16,128]{2,1,0:T(8,128)S(1)}, f32[18,16,128]{2,1,0:T(8,128)S(1)}, f32[...) custom-call(s32[8]{0:T(128)S(1)} %fusion.1.rows_ref, ...), custom_call_target="tpu_custom_call" | custom-call | bytes 21000000 | tf_op jit(solution)/shard_map/cross/pallas_call | solution.py:353
  83.1 1.6 %collective-permute-start.18 = (f32[18,16,128]{2,1,0:T(8,128)S(1)}, f32[18,16,128]{2,1,0:T(8,128)S(1)}, u32[]{:S(2)}, u32[]{:S(2)}) collective-permute-start(f32[18,16,128]{2,1,0:T(8,128)S(1)} %get-tuple-element.48), channel_id=1, source_target_pairs={{0,6},{1,7},{2,4},{3,5},{4,2},{5,3},{6,0},{7,1},{8,14},{9,15},{10,... | collective-permute-start | bytes 442376 | tf_op jit(solution)/shard_map/ppermute | solution.py:377
  84.7 0.8 collective-permute-start.19
  86.5 1.2 %collective-permute-start.8 = (f32[18,16,128]{2,1,0:T(8,128)S(1)}, f32[18,16,128]{2,1,0:T(8,128)S(1)}, u32[]{:S(2)}, u32[]{:S(2)}) collective-permute-start(f32[18,16,128]{2,1,0:T(8,128)S(1)} %get-tuple-element.37), channel_id=1, source_target_pairs={{0,3},{1,2},{2,1},{3,0},{4,7},{5,6},{6,5},{7,4},{8,11},{9,10},{10,... | collective-permute-start | bytes 442376 | tf_op jit(solution)/shard_map/ppermute | solution.py:377
  87.7 1.9 %collective-permute-done.18 = f32[18,16,128]{2,1,0:T(8,128)S(1)} collective-permute-done((f32[18,16,128]{2,1,0:T(8,128)S(1)}, f32[18,16,128]{2,1,0:T(8,128)S(1)}, u32[]{:S(2)}, u32[]{:S(2)}) %collective-permute-start.18) | collective-permute-done | bytes 147488 | tf_op jit(solution)/shard_map/ppermute | solution.py:377
  89.6 1.1 %collective-permute-start.9 = (f32[18,16,128]{2,1,0:T(8,128)S(1)}, f32[18,16,128]{2,1,0:T(8,128)S(1)}, u32[]{:S(2)}, u32[]{:S(2)}) collective-permute-start(f32[18,16,128]{2,1,0:T(8,128)S(1)} %get-tuple-element.38), channel_id=1, source_target_pairs={{0,4},{1,5},{2,6},{3,7},{4,0},{5,1},{6,2},{7,3},{8,12},{9,13},{10,... | collective-permute-start | bytes 442376 | tf_op jit(solution)/shard_map/ppermute | solution.py:377
  90.7 2.3 %collective-permute-done.19 = f32[18,16,128]{2,1,0:T(8,128)S(1)} collective-permute-done((f32[18,16,128]{2,1,0:T(8,128)S(1)}, f32[18,16,128]{2,1,0:T(8,128)S(1)}, u32[]{:S(2)}, u32[]{:S(2)}) %collective-permute-start.19) | collective-permute-done | bytes 147488 | tf_op jit(solution)/shard_map/ppermute | solution.py:377
  93.1 1.4 %collective-permute-start.10 = (f32[18,16,128]{2,1,0:T(8,128)S(1)}, f32[18,16,128]{2,1,0:T(8,128)S(1)}, u32[]{:S(2)}, u32[]{:S(2)}) collective-permute-start(f32[18,16,128]{2,1,0:T(8,128)S(1)} %get-tuple-element.39), channel_id=1, source_target_pairs={{0,5},{1,4},{2,7},{3,6},{4,1},{5,0},{6,3},{7,2},{8,13},{9,12},{10,... | collective-permute-start | bytes 442376 | tf_op jit(solution)/shard_map/ppermute | solution.py:377
  94.8 1.4 %collective-permute-done.7 = f32[18,16,128]{2,1,0:T(8,128)S(1)} collective-permute-done((f32[18,16,128]{2,1,0:T(8,128)S(1)}, f32[18,16,128]{2,1,0:T(8,128)S(1)}, u32[]{:S(2)}, u32[]{:S(2)}) %collective-permute-start.7) | collective-permute-done | bytes 147488 | tf_op jit(solution)/shard_map/ppermute | solution.py:377
  96.2 1.2 %collective-permute-start.12 = (f32[18,16,128]{2,1,0:T(8,128)S(1)}, f32[18,16,128]{2,1,0:T(8,128)S(1)}, u32[]{:S(2)}, u32[]{:S(2)}) collective-permute-start(f32[18,16,128]{2,1,0:T(8,128)S(1)} %get-tuple-element.41), channel_id=1, source_target_pairs={{0,7},{1,6},{2,5},{3,4},{4,3},{5,2},{6,1},{7,0},{8,15},{9,14},{10,... | collective-permute-start | bytes 442376 | tf_op jit(solution)/shard_map/ppermute | solution.py:377
  97.4 5.5 %lag.2 = (f32[16,32,1024]{2,1,0:T(8,128)S(1)}, f32[16,32,1024]{2,1,0:T(8,128)S(1)}) custom-call(s32[1]{0:T(128)} %bitcast.me_ref, f32[288,128]{1,0:T(8,128)S(1)} %bitcast.17, f32[288,128]{1,0:T(8,128)S(1)} %bitcast.18, f32[288,128]{1,0:T(8,128)S(1)} %bitcast.19, f32[288,128]{1,0:T(8,128)S(1)} %bitcast.20, f32[288,128]{1,0:T(8,128)S(1)} %bitcast.21, ...), custom_call_target="tpu_custom_call" | custom-call | bytes 18000000 | tf_op jit(solution)/shard_map/lag/pallas_call | solution.py:433
  102.9 2.5 %collective-permute-done.12 = f32[18,16,128]{2,1,0:T(8,128)S(1)} collective-permute-done((f32[18,16,128]{2,1,0:T(8,128)S(1)}, f32[18,16,128]{2,1,0:T(8,128)S(1)}, u32[]{:S(2)}, u32[]{:S(2)}) %collective-permute-start.12) | collective-permute-done | bytes 147488 | tf_op jit(solution)/shard_map/ppermute | solution.py:377
  105.4 6.5 %lag.3 = (f32[16,32,1024]{2,1,0:T(8,128)}, f32[16,32,1024]{2,1,0:T(8,128)}) custom-call(s32[1]{0:T(128)} %bitcast.me_ref, f32[288,128]{1,0:T(8,128)S(1)} %bitcast.25, f32[288,128]{1,0:T(8,128)S(1)} %bitcast.26, f32[288,128]{1,0:T(8,128)S(1)} %bitcast.27, f32[288,128]{1,0:T(8,128)S(1)} %bitcast.28, f32[288,128]{1,0:T(8,128)S(1)} %bitcast.29, ...), custom_call_target="tpu_custom_call" | custom-call | bytes 18000000 | tf_op jit(solution)/shard_map/lag/pallas_call | solution.py:433
  (44 shorter events, 4.7 us)
Async XLA Ops:
  0.6 1.1 %copy-start.8 = (bf16[2,16,32,384]{3,2,1,0:T(8,128)(2,1)S(1)}, bf16[2,16,32,384]{3,2,1,0:T(8,128)(2,1)}, u32[]{:S(2)}) copy-start(bf16[2,16,32,384]{3,2,1,0:T(8,128)(2,1)} %spectra_ref.1) | copy-start | bytes 2359300
  1.8 0.7 copy-start.9
  2.5 31.8 %copy-start.10 = (s32[4]{0:T(128)S(1)}, s32[4]{0:T(128)}, u32[]{:S(2)}) copy-start(s32[4]{0:T(128)} %param.9) | copy-start | bytes 52
  18.7 14.0 %collective-permute-start = (bf16[8,7,32,128]{3,2,1,0:T(8,128)(2,1)S(1)}, bf16[8,7,32,128]{3,2,1,0:T(8,128)(2,1)S(1)}, u32[]{:S(2)}, u32[]{:S(2)}) collective-permute-start(bf16[8,7,32,128]{3,2,1,0:T(8,128)(2,1)S(1)} %all_to_all.10.rest_0_.rest_4_), channel_id=1, source_target_pairs={{0,24},{8,0},{16,8},{24,16},{1,25},{9,1},{17,9},{25,17},{2,26},{10... | collective-permute-start | bytes 1376264 | tf_op jit(solution)/shard_map/ppermute | solution.py:393
  22.1 10.7 %all-to-all-start = ((bf16[8,6,32,128]{3,2,1,0:T(8,128)(2,1)}), bf16[8,6,32,128]{3,2,1,0:T(8,128)(2,1)S(1)}, u32[]{:S(2)}, u32[]{:S(2)}) async-start(bf16[8,6,32,128]{3,2,1,0:T(8,128)(2,1)} %get-tuple-element.29), calls=%async_computation | async-start | bytes 786432 | tf_op jit(solution)/shard_map/all_to_all | solution.py:388
  26.7 15.0 %collective-permute-start.4 = (bf16[8,7,32,128]{3,2,1,0:T(8,128)(2,1)S(1)}, bf16[8,7,32,128]{3,2,1,0:T(8,128)(2,1)S(1)}, u32[]{:S(2)}, u32[]{:S(2)}) collective-permute-start(bf16[8,7,32,128]{3,2,1,0:T(8,128)(2,1)S(1)} %all_to_all.10.rest_0_.rest_4_), channel_id=1, source_target_pairs={{0,8},{8,16},{16,24},{24,0},{1,9},{9,17},{17,25},{25,1},{2,10},{10... | collective-permute-start | bytes 1376264 | tf_op jit(solution)/shard_map/ppermute | solution.py:392
  32.7 0.7 copy-start.2
  33.5 0.8 copy-start
  34.2 15.9 %collective-permute-start.1 = (bf16[8,6,32,128]{3,2,1,0:T(8,128)(2,1)}, bf16[8,6,32,128]{3,2,1,0:T(8,128)(2,1)S(1)}, u32[]{:S(2)}, u32[]{:S(2)}) collective-permute-start(bf16[8,6,32,128]{3,2,1,0:T(8,128)(2,1)} %join.1.rest_0_), channel_id=1, source_target_pairs={{0,8},{8,16},{16,24},{24,0},{1,9},{9,17},{17,25},{25,1},{2,10},{10... | collective-permute-start | bytes 1179656 | tf_op jit(solution)/shard_map/ppermute | solution.py:392
  41.6 18.3 %collective-permute-start.5 = (bf16[8,7,32,128]{3,2,1,0:T(8,128)(2,1)S(1)}, bf16[8,7,32,128]{3,2,1,0:T(8,128)(2,1)S(1)}, u32[]{:S(2)}, u32[]{:S(2)}) collective-permute-start(bf16[8,7,32,128]{3,2,1,0:T(8,128)(2,1)S(1)} %collective-permute-done.4.rest_1_.rest_5_), channel_id=1, source_target_pairs={{0,8},{8,16},{16,24},{24,0},{1,9},{9,17},{17,25},{25,1},{2,10},{10... | collective-permute-start | bytes 1376264 | tf_op jit(solution)/shard_map/ppermute | solution.py:394
  43.4 27.6 %collective-permute-start.3 = (bf16[8,6,32,128]{3,2,1,0:T(8,128)(2,1)}, bf16[8,6,32,128]{3,2,1,0:T(8,128)(2,1)S(1)}, u32[]{:S(2)}, u32[]{:S(2)}) collective-permute-start(bf16[8,6,32,128]{3,2,1,0:T(8,128)(2,1)} %join.1.rest_0_), channel_id=1, source_target_pairs={{0,24},{8,0},{16,8},{24,16},{1,25},{9,1},{17,9},{25,17},{2,26},{10... | collective-permute-start | bytes 1179656 | tf_op jit(solution)/shard_map/ppermute | solution.py:393
  50.1 26.7 %collective-permute-start.2 = (bf16[8,6,32,128]{3,2,1,0:T(8,128)(2,1)S(1)}, bf16[8,6,32,128]{3,2,1,0:T(8,128)(2,1)S(1)}, u32[]{:S(2)}, u32[]{:S(2)}) collective-permute-start(bf16[8,6,32,128]{3,2,1,0:T(8,128)(2,1)S(1)} %collective-permute-done.1.rest_1_), channel_id=1, source_target_pairs={{0,8},{8,16},{16,24},{24,0},{1,9},{9,17},{17,25},{25,1},{2,10},{10... | collective-permute-start | bytes 1179656 | tf_op jit(solution)/shard_map/ppermute | solution.py:394
  59.9 1.0 copy-start.1
  61.0 17.9 %copy-start.3 = (bf16[8,6,32,128]{3,2,1,0:T(8,128)(2,1)S(1)}, bf16[8,6,32,128]{3,2,1,0:T(8,128)(2,1)}, u32[]{:S(2)}) copy-start(bf16[8,6,32,128]{3,2,1,0:T(8,128)(2,1)} %join.1.rest_0_) | copy-start | bytes 1179652
  61.0 36.4 %copy-start.4 = (bf16[512,1024]{1,0:T(8,128)(2,1)S(1)}, bf16[512,1024]{1,0:T(8,128)(2,1)}, u32[]{:S(2)}) copy-start(bf16[512,1024]{1,0:T(8,128)(2,1)} %constant.61.clone.rest_9_) | copy-start | bytes 3145732
  61.0 36.4 %copy-start.5 = (bf16[512,1024]{1,0:T(8,128)(2,1)S(1)}, bf16[512,1024]{1,0:T(8,128)(2,1)}, u32[]{:S(2)}) copy-start(bf16[512,1024]{1,0:T(8,128)(2,1)} %constant.60.clone.rest_8_) | copy-start | bytes 3145732
  65.5 17.5 %collective-permute-start.13 = (f32[18,16,128]{2,1,0:T(8,128)S(1)}, f32[18,16,128]{2,1,0:T(8,128)S(1)}, u32[]{:S(2)}, u32[]{:S(2)}) collective-permute-start(f32[18,16,128]{2,1,0:T(8,128)S(1)} %get-tuple-element.43), channel_id=1, source_target_pairs={{0,1},{1,0},{2,3},{3,2},{4,5},{5,4},{6,7},{7,6},{8,9},{9,8},{10,11... | collective-permute-start | bytes 442376 | tf_op jit(solution)/shard_map/ppermute | solution.py:377
  69.0 15.7 %collective-permute-start.14 = (f32[18,16,128]{2,1,0:T(8,128)S(1)}, f32[18,16,128]{2,1,0:T(8,128)S(1)}, u32[]{:S(2)}, u32[]{:S(2)}) collective-permute-start(f32[18,16,128]{2,1,0:T(8,128)S(1)} %get-tuple-element.44), channel_id=1, source_target_pairs={{0,2},{1,3},{2,0},{3,1},{4,6},{5,7},{6,4},{7,5},{8,10},{9,11},{10,... | collective-permute-start | bytes 442376 | tf_op jit(solution)/shard_map/ppermute | solution.py:377
  69.2 16.3 %collective-permute-start.15 = (f32[18,16,128]{2,1,0:T(8,128)S(1)}, f32[18,16,128]{2,1,0:T(8,128)S(1)}, u32[]{:S(2)}, u32[]{:S(2)}) collective-permute-start(f32[18,16,128]{2,1,0:T(8,128)S(1)} %get-tuple-element.45), channel_id=1, source_target_pairs={{0,3},{1,2},{2,1},{3,0},{4,7},{5,6},{6,5},{7,4},{8,11},{9,10},{10,... | collective-permute-start | bytes 442376 | tf_op jit(solution)/shard_map/ppermute | solution.py:377
  71.0 14.9 %collective-permute-start.16 = (f32[18,16,128]{2,1,0:T(8,128)S(1)}, f32[18,16,128]{2,1,0:T(8,128)S(1)}, u32[]{:S(2)}, u32[]{:S(2)}) collective-permute-start(f32[18,16,128]{2,1,0:T(8,128)S(1)} %get-tuple-element.46), channel_id=1, source_target_pairs={{0,4},{1,5},{2,6},{3,7},{4,0},{5,1},{6,2},{7,3},{8,12},{9,13},{10,... | collective-permute-start | bytes 442376 | tf_op jit(solution)/shard_map/ppermute | solution.py:377
  76.8 9.7 %collective-permute-start.17 = (f32[18,16,128]{2,1,0:T(8,128)S(1)}, f32[18,16,128]{2,1,0:T(8,128)S(1)}, u32[]{:S(2)}, u32[]{:S(2)}) collective-permute-start(f32[18,16,128]{2,1,0:T(8,128)S(1)} %get-tuple-element.47), channel_id=1, source_target_pairs={{0,5},{1,4},{2,7},{3,6},{4,1},{5,0},{6,3},{7,2},{8,13},{9,12},{10,... | collective-permute-start | bytes 442376 | tf_op jit(solution)/shard_map/ppermute | solution.py:377
  83.0 22.4 %copy-start.6 = (bf16[512,1024]{1,0:T(8,128)(2,1)S(1)}, bf16[512,1024]{1,0:T(8,128)(2,1)}, u32[]{:S(2)}) copy-start(bf16[512,1024]{1,0:T(8,128)(2,1)} %constant.63.clone.rest_9_) | copy-start | bytes 3145732
  83.0 22.4 %copy-start.7 = (bf16[512,1024]{1,0:T(8,128)(2,1)S(1)}, bf16[512,1024]{1,0:T(8,128)(2,1)}, u32[]{:S(2)}) copy-start(bf16[512,1024]{1,0:T(8,128)(2,1)} %constant.62.clone.rest_8_) | copy-start | bytes 3145732
  83.1 6.5 %collective-permute-start.18 = (f32[18,16,128]{2,1,0:T(8,128)S(1)}, f32[18,16,128]{2,1,0:T(8,128)S(1)}, u32[]{:S(2)}, u32[]{:S(2)}) collective-permute-start(f32[18,16,128]{2,1,0:T(8,128)S(1)} %get-tuple-element.48), channel_id=1, source_target_pairs={{0,6},{1,7},{2,4},{3,5},{4,2},{5,3},{6,0},{7,1},{8,14},{9,15},{10,... | collective-permute-start | bytes 442376 | tf_op jit(solution)/shard_map/ppermute | solution.py:377
  84.7 8.4 %collective-permute-start.19 = (f32[18,16,128]{2,1,0:T(8,128)S(1)}, f32[18,16,128]{2,1,0:T(8,128)S(1)}, u32[]{:S(2)}, u32[]{:S(2)}) collective-permute-start(f32[18,16,128]{2,1,0:T(8,128)S(1)} %get-tuple-element.49), channel_id=1, source_target_pairs={{0,7},{1,6},{2,5},{3,4},{4,3},{5,2},{6,1},{7,0},{8,15},{9,14},{10,... | collective-permute-start | bytes 442376 | tf_op jit(solution)/shard_map/ppermute | solution.py:377
  85.5 8.9 %collective-permute-start.6 = (f32[18,16,128]{2,1,0:T(8,128)S(1)}, f32[18,16,128]{2,1,0:T(8,128)S(1)}, u32[]{:S(2)}, u32[]{:S(2)}) collective-permute-start(f32[18,16,128]{2,1,0:T(8,128)S(1)} %get-tuple-element.35), channel_id=1, source_target_pairs={{0,1},{1,0},{2,3},{3,2},{4,5},{5,4},{6,7},{7,6},{8,9},{9,8},{10,11... | collective-permute-start | bytes 442376 | tf_op jit(solution)/shard_map/ppermute | solution.py:377
  85.9 10.3 %collective-permute-start.7 = (f32[18,16,128]{2,1,0:T(8,128)S(1)}, f32[18,16,128]{2,1,0:T(8,128)S(1)}, u32[]{:S(2)}, u32[]{:S(2)}) collective-permute-start(f32[18,16,128]{2,1,0:T(8,128)S(1)} %get-tuple-element.36), channel_id=1, source_target_pairs={{0,2},{1,3},{2,0},{3,1},{4,6},{5,7},{6,4},{7,5},{8,10},{9,11},{10,... | collective-permute-start | bytes 442376 | tf_op jit(solution)/shard_map/ppermute | solution.py:377
  86.5 16.4 %collective-permute-start.8 = (f32[18,16,128]{2,1,0:T(8,128)S(1)}, f32[18,16,128]{2,1,0:T(8,128)S(1)}, u32[]{:S(2)}, u32[]{:S(2)}) collective-permute-start(f32[18,16,128]{2,1,0:T(8,128)S(1)} %get-tuple-element.37), channel_id=1, source_target_pairs={{0,3},{1,2},{2,1},{3,0},{4,7},{5,6},{6,5},{7,4},{8,11},{9,10},{10,... | collective-permute-start | bytes 442376 | tf_op jit(solution)/shard_map/ppermute | solution.py:377
  89.6 13.3 %collective-permute-start.9 = (f32[18,16,128]{2,1,0:T(8,128)S(1)}, f32[18,16,128]{2,1,0:T(8,128)S(1)}, u32[]{:S(2)}, u32[]{:S(2)}) collective-permute-start(f32[18,16,128]{2,1,0:T(8,128)S(1)} %get-tuple-element.38), channel_id=1, source_target_pairs={{0,4},{1,5},{2,6},{3,7},{4,0},{5,1},{6,2},{7,3},{8,12},{9,13},{10,... | collective-permute-start | bytes 442376 | tf_op jit(solution)/shard_map/ppermute | solution.py:377
  93.1 9.8 %collective-permute-start.10 = (f32[18,16,128]{2,1,0:T(8,128)S(1)}, f32[18,16,128]{2,1,0:T(8,128)S(1)}, u32[]{:S(2)}, u32[]{:S(2)}) collective-permute-start(f32[18,16,128]{2,1,0:T(8,128)S(1)} %get-tuple-element.39), channel_id=1, source_target_pairs={{0,5},{1,4},{2,7},{3,6},{4,1},{5,0},{6,3},{7,2},{8,13},{9,12},{10,... | collective-permute-start | bytes 442376 | tf_op jit(solution)/shard_map/ppermute | solution.py:377
  94.5 8.4 %collective-permute-start.11 = (f32[18,16,128]{2,1,0:T(8,128)S(1)}, f32[18,16,128]{2,1,0:T(8,128)S(1)}, u32[]{:S(2)}, u32[]{:S(2)}) collective-permute-start(f32[18,16,128]{2,1,0:T(8,128)S(1)} %get-tuple-element.40), channel_id=1, source_target_pairs={{0,6},{1,7},{2,4},{3,5},{4,2},{5,3},{6,0},{7,1},{8,14},{9,15},{10,... | collective-permute-start | bytes 442376 | tf_op jit(solution)/shard_map/ppermute | solution.py:377
  96.2 9.2 %collective-permute-start.12 = (f32[18,16,128]{2,1,0:T(8,128)S(1)}, f32[18,16,128]{2,1,0:T(8,128)S(1)}, u32[]{:S(2)}, u32[]{:S(2)}) collective-permute-start(f32[18,16,128]{2,1,0:T(8,128)S(1)} %get-tuple-element.41), channel_id=1, source_target_pairs={{0,7},{1,6},{2,5},{3,4},{4,3},{5,2},{6,1},{7,0},{8,15},{9,14},{10,... | collective-permute-start | bytes 442376 | tf_op jit(solution)/shard_map/ppermute | solution.py:377

commit v6 on v5

--- a/solution.py
+++ b/solution.py
@@ -25,7 +25,7 @@
 W_Z = 1
 W_X = 1
 W_O = 0
-VMEM = 24 * 1024 * 1024
+VMEM = 36 * 1024 * 1024
 
 
 def cost(micros):
@@ -421,7 +421,7 @@
         for i in range(count):
             backs[i] = send_back(cross_call(i, row_table, gathered[i], gathered[0]))
 
-    tile = 256
+    tile = 512
     result = []
     whole_out = jax.ShapeDtypeStruct((rows_out, chans, LAGS), jnp.float32)
     out_spec = pl.BlockSpec((rows_out, chans, tile), lambda s: (0, 0, s))

time: 113 us -> 112 us (level)
  transfers between devices with their start and end apart: 21 -> 21, of which waited for: 10 -> 10; matrix products, arithmetic and copies ran while one was open for 1% -> 1% of each run, Pallas kernels for 13% -> 12%
where the time goes in v6:
time: 112 us
  waiting for transfers between devices  38.8 us (35%)
  starting transfers between devices  30.2 us (27%)
  Pallas kernels  23.1 us (21%)
  blocking collectives  13.1 us (12%)
  local copies, waits for them, and re-layouts  4.38 us (4%)
  other arithmetic  1.37 us (1%)
    ppermute x14, starting transfers between devices, send_back(): back[m] = lax.ppermute(outs[m], 'win', [(d, d ^ m) for d in range(devs)])  15.9 us
    ppermute x2, waiting for transfers between devices, spread(): held[i] = [own, up, lax.ppermute(up, 'chan', ring), down]  13.2 us
    all_to_all x1, blocking collectives, enter(): held[i] = [lax.all_to_all(block, 'win', 0, 0, tiled=True)]  13.1 us
    pallas_call x2, Pallas kernels, body(): pl.pallas_call(functools.partial(lag_kernel, n, devs, rows_out, windows,...  11.2 us
    ppermute x2, waiting for transfers between devices, spread(): up = lax.ppermute(own, 'chan', ring)  10.6 us
    pallas_call x2, Pallas kernels, cross_call(): pl.pallas_call(functools.partial(cross_kernel, groups, own_first, first),...  8.69 us
    ppermute x14, waiting for transfers between devices, send_back(): back[m] = lax.ppermute(outs[m], 'win', [(d, d ^ m) for d in range(devs)])  8.65 us
    ppermute x2, starting transfers between devices, spread(): down = lax.ppermute(own, 'chan', back_ring)  6.14 us
  transfers between devices with their start and end apart: 21, of which 10 were waited for; matrix products, arithmetic and copies ran while one was open for 1% of the time, Pallas kernels for 12%

profile of v6, /device:TPU:1, one launch (start us, length us, event | category | flops | bytes accessed | tf_op | source)
XLA Modules:
  0.0 111.6 jit_solution(14976214241621968335)
XLA Ops:
  0.6 1.1 %copy-done.8 = bf16[2,16,32,384]{3,2,1,0:T(8,128)(2,1)S(1)} copy-done((bf16[2,16,32,384]{3,2,1,0:T(8,128)(2,1)S(1)}, bf16[2,16,32,384]{3,2,1,0:T(8,128)(2,1)}, u32[]{:S(2)}) %copy-start.8) | copy-done | bytes 786456
  2.5 3.2 %pack.1 = (bf16[8,7,32,128]{3,2,1,0:T(8,128)(2,1)S(1)}, bf16[8,6,32,128]{3,2,1,0:T(8,128)(2,1)}) custom-call(bf16[2,16,32,384]{3,2,1,0:T(8,128)(2,1)S(1)} %copy-done.8, s32[16,32]{1,0:T(8,128)S(1)} %copy-done.9), custom_call_target="tpu_custom_call" | custom-call | bytes 15000000 | tf_op jit(solution)/shard_map/pack/pallas_call | solution.py:301
  5.7 13.1 %all_to_all.10.rest_0_.rest_4_ = bf16[8,7,32,128]{3,2,1,0:T(8,128)(2,1)S(1)} all-to-all(bf16[8,7,32,128]{3,2,1,0:T(8,128)(2,1)S(1)} %get-tuple-element.30), channel_id=1, replica_groups=mesh['chan'=4,'win'=8] {'win'}, dimensions={0} | all-to-all | bytes 917504 | tf_op jit(solution)/shard_map/all_to_all | solution.py:388
  18.7 3.3 %collective-permute-start = (bf16[8,7,32,128]{3,2,1,0:T(8,128)(2,1)S(1)}, bf16[8,7,32,128]{3,2,1,0:T(8,128)(2,1)S(1)}, u32[]{:S(2)}, u32[]{:S(2)}) collective-permute-start(bf16[8,7,32,128]{3,2,1,0:T(8,128)(2,1)S(1)} %all_to_all.10.rest_0_.rest_4_), channel_id=1, source_target_pairs={{0,24},{8,0},{16,8},{24,16},{1,25},{9,1},{17,9},{25,17},{2,26},{10... | collective-permute-start | bytes 1376264 | tf_op jit(solution)/shard_map/ppermute | solution.py:393
  22.1 4.6 %all-to-all-start = ((bf16[8,6,32,128]{3,2,1,0:T(8,128)(2,1)}), bf16[8,6,32,128]{3,2,1,0:T(8,128)(2,1)S(1)}, u32[]{:S(2)}, u32[]{:S(2)}) async-start(bf16[8,6,32,128]{3,2,1,0:T(8,128)(2,1)} %get-tuple-element.29), calls=%async_computation | async-start | bytes 786432 | tf_op jit(solution)/shard_map/all_to_all | solution.py:388
  26.7 6.0 %all-to-all-done.refs_0_ = bf16[8,6,32,128]{3,2,1,0:T(8,128)(2,1)S(1)} async-done(((bf16[8,6,32,128]{3,2,1,0:T(8,128)(2,1)}), bf16[8,6,32,128]{3,2,1,0:T(8,128)(2,1)S(1)}, u32[]{:S(2)}, u32[]{:S(2)}) %all-to-all-start) | async-done | bytes 393248 | tf_op jit(solution)/shard_map/all_to_all | solution.py:388
  33.5 0.8 copy-done
  35.0 6.7 %collective-permute-done.4.rest_1_.rest_5_ = bf16[8,7,32,128]{3,2,1,0:T(8,128)(2,1)S(1)} collective-permute-done((bf16[8,7,32,128]{3,2,1,0:T(8,128)(2,1)S(1)}, bf16[8,7,32,128]{3,2,1,0:T(8,128)(2,1)S(1)}, u32[]{:S(2)}, u32[]{:S(2)}) %collective-permute-start.4) | collective-permute-done | bytes 458784 | tf_op jit(solution)/shard_map/ppermute | solution.py:392
  41.6 1.7 %collective-permute-start.5 = (bf16[8,7,32,128]{3,2,1,0:T(8,128)(2,1)S(1)}, bf16[8,7,32,128]{3,2,1,0:T(8,128)(2,1)S(1)}, u32[]{:S(2)}, u32[]{:S(2)}) collective-permute-start(bf16[8,7,32,128]{3,2,1,0:T(8,128)(2,1)S(1)} %collective-permute-done.4.rest_1_.rest_5_), channel_id=1, source_target_pairs={{0,8},{8,16},{16,24},{24,0},{1,9},{9,17},{17,25},{25,1},{2,10},{10... | collective-permute-start | bytes 1376264 | tf_op jit(solution)/shard_map/ppermute | solution.py:394
  43.4 2.8 %collective-permute-start.3 = (bf16[8,6,32,128]{3,2,1,0:T(8,128)(2,1)}, bf16[8,6,32,128]{3,2,1,0:T(8,128)(2,1)S(1)}, u32[]{:S(2)}, u32[]{:S(2)}) collective-permute-start(bf16[8,6,32,128]{3,2,1,0:T(8,128)(2,1)} %join.1.rest_0_), channel_id=1, source_target_pairs={{0,24},{8,0},{16,8},{24,16},{1,25},{9,1},{17,9},{25,17},{2,26},{10... | collective-permute-start | bytes 1179656 | tf_op jit(solution)/shard_map/ppermute | solution.py:393
  46.2 3.9 %collective-permute-done.1.rest_1_ = bf16[8,6,32,128]{3,2,1,0:T(8,128)(2,1)S(1)} collective-permute-done((bf16[8,6,32,128]{3,2,1,0:T(8,128)(2,1)}, bf16[8,6,32,128]{3,2,1,0:T(8,128)(2,1)S(1)}, u32[]{:S(2)}, u32[]{:S(2)}) %collective-permute-start.1) | collective-permute-done | bytes 393248 | tf_op jit(solution)/shard_map/ppermute | solution.py:392
  50.1 1.8 %collective-permute-start.2 = (bf16[8,6,32,128]{3,2,1,0:T(8,128)(2,1)S(1)}, bf16[8,6,32,128]{3,2,1,0:T(8,128)(2,1)S(1)}, u32[]{:S(2)}, u32[]{:S(2)}) collective-permute-start(bf16[8,6,32,128]{3,2,1,0:T(8,128)(2,1)S(1)} %collective-permute-done.1.rest_1_), channel_id=1, source_target_pairs={{0,8},{8,16},{16,24},{24,0},{1,9},{9,17},{17,25},{25,1},{2,10},{10... | collective-permute-start | bytes 1179656 | tf_op jit(solution)/shard_map/ppermute | solution.py:394
  52.5 7.4 %collective-permute-done.5.rest_2_.rest_6_ = bf16[8,7,32,128]{3,2,1,0:T(8,128)(2,1)S(1)} collective-permute-done((bf16[8,7,32,128]{3,2,1,0:T(8,128)(2,1)S(1)}, bf16[8,7,32,128]{3,2,1,0:T(8,128)(2,1)S(1)}, u32[]{:S(2)}, u32[]{:S(2)}) %collective-permute-start.5) | collective-permute-done | bytes 458784 | tf_op jit(solution)/shard_map/ppermute | solution.py:394
  59.9 1.0 copy-done.1
  61.0 4.5 %cross.2 = (f32[18,16,128]{2,1,0:T(8,128)S(1)}, f32[18,16,128]{2,1,0:T(8,128)S(1)}, f32[18,16,128]{2,1,0:T(8,128)S(1)}, f32[18,16,128]{2,1,0:T(8,128)S(1)}, f32[...) custom-call(s32[8]{0:T(128)S(1)} %fusion.1.rows_ref, ...), custom_call_target="tpu_custom_call" | custom-call | bytes 24000000 | tf_op jit(solution)/shard_map/cross/pallas_call | solution.py:353
  65.5 3.5 %collective-permute-start.13 = (f32[18,16,128]{2,1,0:T(8,128)S(1)}, f32[18,16,128]{2,1,0:T(8,128)S(1)}, u32[]{:S(2)}, u32[]{:S(2)}) collective-permute-start(f32[18,16,128]{2,1,0:T(8,128)S(1)} %get-tuple-element.43), channel_id=1, source_target_pairs={{0,1},{1,0},{2,3},{3,2},{4,5},{5,4},{6,7},{7,6},{8,9},{9,8},{10,11... | collective-permute-start | bytes 442376 | tf_op jit(solution)/shard_map/ppermute | solution.py:377
  69.2 1.5 %collective-permute-start.15 = (f32[18,16,128]{2,1,0:T(8,128)S(1)}, f32[18,16,128]{2,1,0:T(8,128)S(1)}, u32[]{:S(2)}, u32[]{:S(2)}) collective-permute-start(f32[18,16,128]{2,1,0:T(8,128)S(1)} %get-tuple-element.45), channel_id=1, source_target_pairs={{0,3},{1,2},{2,1},{3,0},{4,7},{5,6},{6,5},{7,4},{8,11},{9,10},{10,... | collective-permute-start | bytes 442376 | tf_op jit(solution)/shard_map/ppermute | solution.py:377
  71.0 5.8 %collective-permute-done.2.rest_2_ = bf16[8,6,32,128]{3,2,1,0:T(8,128)(2,1)S(1)} collective-permute-done((bf16[8,6,32,128]{3,2,1,0:T(8,128)(2,1)S(1)}, bf16[8,6,32,128]{3,2,1,0:T(8,128)(2,1)S(1)}, u32[]{:S(2)}, u32[]{:S(2)}) %collective-permute-start.2) | collective-permute-done | bytes 393248 | tf_op jit(solution)/shard_map/ppermute | solution.py:394
  76.8 2.1 %collective-permute-start.17 = (f32[18,16,128]{2,1,0:T(8,128)S(1)}, f32[18,16,128]{2,1,0:T(8,128)S(1)}, u32[]{:S(2)}, u32[]{:S(2)}) collective-permute-start(f32[18,16,128]{2,1,0:T(8,128)S(1)} %get-tuple-element.47), channel_id=1, source_target_pairs={{0,5},{1,4},{2,7},{3,6},{4,1},{5,0},{6,3},{7,2},{8,13},{9,12},{10,... | collective-permute-start | bytes 442376 | tf_op jit(solution)/shard_map/ppermute | solution.py:377
  78.9 4.2 %cross.3 = (f32[18,16,128]{2,1,0:T(8,128)S(1)}, f32[18,16,128]{2,1,0:T(8,128)S(1)}, f32[18,16,128]{2,1,0:T(8,128)S(1)}, f32[18,16,128]{2,1,0:T(8,128)S(1)}, f32[...) custom-call(s32[8]{0:T(128)S(1)} %fusion.1.rows_ref, ...), custom_call_target="tpu_custom_call" | custom-call | bytes 21000000 | tf_op jit(solution)/shard_map/cross/pallas_call | solution.py:353
  83.1 1.6 %collective-permute-start.18 = (f32[18,16,128]{2,1,0:T(8,128)S(1)}, f32[18,16,128]{2,1,0:T(8,128)S(1)}, u32[]{:S(2)}, u32[]{:S(2)}) collective-permute-start(f32[18,16,128]{2,1,0:T(8,128)S(1)} %get-tuple-element.48), channel_id=1, source_target_pairs={{0,6},{1,7},{2,4},{3,5},{4,2},{5,3},{6,0},{7,1},{8,14},{9,15},{10,... | collective-permute-start | bytes 442376 | tf_op jit(solution)/shard_map/ppermute | solution.py:377
  84.7 0.8 collective-permute-start.19
  86.4 1.2 %collective-permute-start.8 = (f32[18,16,128]{2,1,0:T(8,128)S(1)}, f32[18,16,128]{2,1,0:T(8,128)S(1)}, u32[]{:S(2)}, u32[]{:S(2)}) collective-permute-start(f32[18,16,128]{2,1,0:T(8,128)S(1)} %get-tuple-element.37), channel_id=1, source_target_pairs={{0,3},{1,2},{2,1},{3,0},{4,7},{5,6},{6,5},{7,4},{8,11},{9,10},{10,... | collective-permute-start | bytes 442376 | tf_op jit(solution)/shard_map/ppermute | solution.py:377
  87.7 1.9 %collective-permute-done.18 = f32[18,16,128]{2,1,0:T(8,128)S(1)} collective-permute-done((f32[18,16,128]{2,1,0:T(8,128)S(1)}, f32[18,16,128]{2,1,0:T(8,128)S(1)}, u32[]{:S(2)}, u32[]{:S(2)}) %collective-permute-start.18) | collective-permute-done | bytes 147488 | tf_op jit(solution)/shard_map/ppermute | solution.py:377
  89.6 1.2 %collective-permute-start.9 = (f32[18,16,128]{2,1,0:T(8,128)S(1)}, f32[18,16,128]{2,1,0:T(8,128)S(1)}, u32[]{:S(2)}, u32[]{:S(2)}) collective-permute-start(f32[18,16,128]{2,1,0:T(8,128)S(1)} %get-tuple-element.38), channel_id=1, source_target_pairs={{0,4},{1,5},{2,6},{3,7},{4,0},{5,1},{6,2},{7,3},{8,12},{9,13},{10,... | collective-permute-start | bytes 442376 | tf_op jit(solution)/shard_map/ppermute | solution.py:377
  90.7 2.3 %collective-permute-done.19 = f32[18,16,128]{2,1,0:T(8,128)S(1)} collective-permute-done((f32[18,16,128]{2,1,0:T(8,128)S(1)}, f32[18,16,128]{2,1,0:T(8,128)S(1)}, u32[]{:S(2)}, u32[]{:S(2)}) %collective-permute-start.19) | collective-permute-done | bytes 147488 | tf_op jit(solution)/shard_map/ppermute | solution.py:377
  93.1 1.4 %collective-permute-start.10 = (f32[18,16,128]{2,1,0:T(8,128)S(1)}, f32[18,16,128]{2,1,0:T(8,128)S(1)}, u32[]{:S(2)}, u32[]{:S(2)}) collective-permute-start(f32[18,16,128]{2,1,0:T(8,128)S(1)} %get-tuple-element.39), channel_id=1, source_target_pairs={{0,5},{1,4},{2,7},{3,6},{4,1},{5,0},{6,3},{7,2},{8,13},{9,12},{10,... | collective-permute-start | bytes 442376 | tf_op jit(solution)/shard_map/ppermute | solution.py:377
  94.8 1.4 %collective-permute-done.7 = f32[18,16,128]{2,1,0:T(8,128)S(1)} collective-permute-done((f32[18,16,128]{2,1,0:T(8,128)S(1)}, f32[18,16,128]{2,1,0:T(8,128)S(1)}, u32[]{:S(2)}, u32[]{:S(2)}) %collective-permute-start.7) | collective-permute-done | bytes 147488 | tf_op jit(solution)/shard_map/ppermute | solution.py:377
  96.2 1.2 %collective-permute-start.12 = (f32[18,16,128]{2,1,0:T(8,128)S(1)}, f32[18,16,128]{2,1,0:T(8,128)S(1)}, u32[]{:S(2)}, u32[]{:S(2)}) collective-permute-start(f32[18,16,128]{2,1,0:T(8,128)S(1)} %get-tuple-element.41), channel_id=1, source_target_pairs={{0,7},{1,6},{2,5},{3,4},{4,3},{5,2},{6,1},{7,0},{8,15},{9,14},{10,... | collective-permute-start | bytes 442376 | tf_op jit(solution)/shard_map/ppermute | solution.py:377
  97.4 4.9 %lag.2 = (f32[16,32,1024]{2,1,0:T(8,128)S(1)}, f32[16,32,1024]{2,1,0:T(8,128)S(1)}) custom-call(s32[1]{0:T(128)} %bitcast.me_ref, f32[288,128]{1,0:T(8,128)S(1)} %bitcast.17, f32[288,128]{1,0:T(8,128)S(1)} %bitcast.18, f32[288,128]{1,0:T(8,128)S(1)} %bitcast.19, f32[288,128]{1,0:T(8,128)S(1)} %bitcast.20, f32[288,128]{1,0:T(8,128)S(1)} %bitcast.21, ...), custom_call_target="tpu_custom_call" | custom-call | bytes 18000000 | tf_op jit(solution)/shard_map/lag/pallas_call | solution.py:433
  102.4 3.0 %collective-permute-done.12 = f32[18,16,128]{2,1,0:T(8,128)S(1)} collective-permute-done((f32[18,16,128]{2,1,0:T(8,128)S(1)}, f32[18,16,128]{2,1,0:T(8,128)S(1)}, u32[]{:S(2)}, u32[]{:S(2)}) %collective-permute-start.12) | collective-permute-done | bytes 147488 | tf_op jit(solution)/shard_map/ppermute | solution.py:377
  105.4 6.2 %lag.3 = (f32[16,32,1024]{2,1,0:T(8,128)}, f32[16,32,1024]{2,1,0:T(8,128)}) custom-call(s32[1]{0:T(128)} %bitcast.me_ref, f32[288,128]{1,0:T(8,128)S(1)} %bitcast.25, f32[288,128]{1,0:T(8,128)S(1)} %bitcast.26, f32[288,128]{1,0:T(8,128)S(1)} %bitcast.27, f32[288,128]{1,0:T(8,128)S(1)} %bitcast.28, f32[288,128]{1,0:T(8,128)S(1)} %bitcast.29, ...), custom_call_target="tpu_custom_call" | custom-call | bytes 18000000 | tf_op jit(solution)/shard_map/lag/pallas_call | solution.py:433
  (44 shorter events, 4.6 us)
Async XLA Ops:
  0.6 1.1 %copy-start.8 = (bf16[2,16,32,384]{3,2,1,0:T(8,128)(2,1)S(1)}, bf16[2,16,32,384]{3,2,1,0:T(8,128)(2,1)}, u32[]{:S(2)}) copy-start(bf16[2,16,32,384]{3,2,1,0:T(8,128)(2,1)} %spectra_ref.1) | copy-start | bytes 2359300
  1.8 0.7 copy-start.9
  2.5 31.8 %copy-start.10 = (s32[4]{0:T(128)S(1)}, s32[4]{0:T(128)}, u32[]{:S(2)}) copy-start(s32[4]{0:T(128)} %param.9) | copy-start | bytes 52
  18.7 14.0 %collective-permute-start = (bf16[8,7,32,128]{3,2,1,0:T(8,128)(2,1)S(1)}, bf16[8,7,32,128]{3,2,1,0:T(8,128)(2,1)S(1)}, u32[]{:S(2)}, u32[]{:S(2)}) collective-permute-start(bf16[8,7,32,128]{3,2,1,0:T(8,128)(2,1)S(1)} %all_to_all.10.rest_0_.rest_4_), channel_id=1, source_target_pairs={{0,24},{8,0},{16,8},{24,16},{1,25},{9,1},{17,9},{25,17},{2,26},{10... | collective-permute-start | bytes 1376264 | tf_op jit(solution)/shard_map/ppermute | solution.py:393
  22.1 10.7 %all-to-all-start = ((bf16[8,6,32,128]{3,2,1,0:T(8,128)(2,1)}), bf16[8,6,32,128]{3,2,1,0:T(8,128)(2,1)S(1)}, u32[]{:S(2)}, u32[]{:S(2)}) async-start(bf16[8,6,32,128]{3,2,1,0:T(8,128)(2,1)} %get-tuple-element.29), calls=%async_computation | async-start | bytes 786432 | tf_op jit(solution)/shard_map/all_to_all | solution.py:388
  26.7 15.0 %collective-permute-start.4 = (bf16[8,7,32,128]{3,2,1,0:T(8,128)(2,1)S(1)}, bf16[8,7,32,128]{3,2,1,0:T(8,128)(2,1)S(1)}, u32[]{:S(2)}, u32[]{:S(2)}) collective-permute-start(bf16[8,7,32,128]{3,2,1,0:T(8,128)(2,1)S(1)} %all_to_all.10.rest_0_.rest_4_), channel_id=1, source_target_pairs={{0,8},{8,16},{16,24},{24,0},{1,9},{9,17},{17,25},{25,1},{2,10},{10... | collective-permute-start | bytes 1376264 | tf_op jit(solution)/shard_map/ppermute | solution.py:392
  32.7 0.7 copy-start.2
  33.5 0.8 copy-start
  34.2 15.9 %collective-permute-start.1 = (bf16[8,6,32,128]{3,2,1,0:T(8,128)(2,1)}, bf16[8,6,32,128]{3,2,1,0:T(8,128)(2,1)S(1)}, u32[]{:S(2)}, u32[]{:S(2)}) collective-permute-start(bf16[8,6,32,128]{3,2,1,0:T(8,128)(2,1)} %join.1.rest_0_), channel_id=1, source_target_pairs={{0,8},{8,16},{16,24},{24,0},{1,9},{9,17},{17,25},{25,1},{2,10},{10... | collective-permute-start | bytes 1179656 | tf_op jit(solution)/shard_map/ppermute | solution.py:392
  41.6 18.3 %collective-permute-start.5 = (bf16[8,7,32,128]{3,2,1,0:T(8,128)(2,1)S(1)}, bf16[8,7,32,128]{3,2,1,0:T(8,128)(2,1)S(1)}, u32[]{:S(2)}, u32[]{:S(2)}) collective-permute-start(bf16[8,7,32,128]{3,2,1,0:T(8,128)(2,1)S(1)} %collective-permute-done.4.rest_1_.rest_5_), channel_id=1, source_target_pairs={{0,8},{8,16},{16,24},{24,0},{1,9},{9,17},{17,25},{25,1},{2,10},{10... | collective-permute-start | bytes 1376264 | tf_op jit(solution)/shard_map/ppermute | solution.py:394
  43.4 27.6 %collective-permute-start.3 = (bf16[8,6,32,128]{3,2,1,0:T(8,128)(2,1)}, bf16[8,6,32,128]{3,2,1,0:T(8,128)(2,1)S(1)}, u32[]{:S(2)}, u32[]{:S(2)}) collective-permute-start(bf16[8,6,32,128]{3,2,1,0:T(8,128)(2,1)} %join.1.rest_0_), channel_id=1, source_target_pairs={{0,24},{8,0},{16,8},{24,16},{1,25},{9,1},{17,9},{25,17},{2,26},{10... | collective-permute-start | bytes 1179656 | tf_op jit(solution)/shard_map/ppermute | solution.py:393
  50.1 26.7 %collective-permute-start.2 = (bf16[8,6,32,128]{3,2,1,0:T(8,128)(2,1)S(1)}, bf16[8,6,32,128]{3,2,1,0:T(8,128)(2,1)S(1)}, u32[]{:S(2)}, u32[]{:S(2)}) collective-permute-start(bf16[8,6,32,128]{3,2,1,0:T(8,128)(2,1)S(1)} %collective-permute-done.1.rest_1_), channel_id=1, source_target_pairs={{0,8},{8,16},{16,24},{24,0},{1,9},{9,17},{17,25},{25,1},{2,10},{10... | collective-permute-start | bytes 1179656 | tf_op jit(solution)/shard_map/ppermute | solution.py:394
  59.9 1.0 copy-start.1
  61.0 17.9 %copy-start.3 = (bf16[8,6,32,128]{3,2,1,0:T(8,128)(2,1)S(1)}, bf16[8,6,32,128]{3,2,1,0:T(8,128)(2,1)}, u32[]{:S(2)}) copy-start(bf16[8,6,32,128]{3,2,1,0:T(8,128)(2,1)} %join.1.rest_0_) | copy-start | bytes 1179652
  61.0 36.4 %copy-start.4 = (bf16[512,1024]{1,0:T(8,128)(2,1)S(1)}, bf16[512,1024]{1,0:T(8,128)(2,1)}, u32[]{:S(2)}) copy-start(bf16[512,1024]{1,0:T(8,128)(2,1)} %constant.61.clone.rest_9_) | copy-start | bytes 3145732
  61.0 36.4 %copy-start.5 = (bf16[512,1024]{1,0:T(8,128)(2,1)S(1)}, bf16[512,1024]{1,0:T(8,128)(2,1)}, u32[]{:S(2)}) copy-start(bf16[512,1024]{1,0:T(8,128)(2,1)} %constant.60.clone.rest_8_) | copy-start | bytes 3145732
  65.5 17.5 %collective-permute-start.13 = (f32[18,16,128]{2,1,0:T(8,128)S(1)}, f32[18,16,128]{2,1,0:T(8,128)S(1)}, u32[]{:S(2)}, u32[]{:S(2)}) collective-permute-start(f32[18,16,128]{2,1,0:T(8,128)S(1)} %get-tuple-element.43), channel_id=1, source_target_pairs={{0,1},{1,0},{2,3},{3,2},{4,5},{5,4},{6,7},{7,6},{8,9},{9,8},{10,11... | collective-permute-start | bytes 442376 | tf_op jit(solution)/shard_map/ppermute | solution.py:377
  69.0 15.7 %collective-permute-start.14 = (f32[18,16,128]{2,1,0:T(8,128)S(1)}, f32[18,16,128]{2,1,0:T(8,128)S(1)}, u32[]{:S(2)}, u32[]{:S(2)}) collective-permute-start(f32[18,16,128]{2,1,0:T(8,128)S(1)} %get-tuple-element.44), channel_id=1, source_target_pairs={{0,2},{1,3},{2,0},{3,1},{4,6},{5,7},{6,4},{7,5},{8,10},{9,11},{10,... | collective-permute-start | bytes 442376 | tf_op jit(solution)/shard_map/ppermute | solution.py:377
  69.2 16.3 %collective-permute-start.15 = (f32[18,16,128]{2,1,0:T(8,128)S(1)}, f32[18,16,128]{2,1,0:T(8,128)S(1)}, u32[]{:S(2)}, u32[]{:S(2)}) collective-permute-start(f32[18,16,128]{2,1,0:T(8,128)S(1)} %get-tuple-element.45), channel_id=1, source_target_pairs={{0,3},{1,2},{2,1},{3,0},{4,7},{5,6},{6,5},{7,4},{8,11},{9,10},{10,... | collective-permute-start | bytes 442376 | tf_op jit(solution)/shard_map/ppermute | solution.py:377
  71.0 14.9 %collective-permute-start.16 = (f32[18,16,128]{2,1,0:T(8,128)S(1)}, f32[18,16,128]{2,1,0:T(8,128)S(1)}, u32[]{:S(2)}, u32[]{:S(2)}) collective-permute-start(f32[18,16,128]{2,1,0:T(8,128)S(1)} %get-tuple-element.46), channel_id=1, source_target_pairs={{0,4},{1,5},{2,6},{3,7},{4,0},{5,1},{6,2},{7,3},{8,12},{9,13},{10,... | collective-permute-start | bytes 442376 | tf_op jit(solution)/shard_map/ppermute | solution.py:377
  76.8 9.6 %collective-permute-start.17 = (f32[18,16,128]{2,1,0:T(8,128)S(1)}, f32[18,16,128]{2,1,0:T(8,128)S(1)}, u32[]{:S(2)}, u32[]{:S(2)}) collective-permute-start(f32[18,16,128]{2,1,0:T(8,128)S(1)} %get-tuple-element.47), channel_id=1, source_target_pairs={{0,5},{1,4},{2,7},{3,6},{4,1},{5,0},{6,3},{7,2},{8,13},{9,12},{10,... | collective-permute-start | bytes 442376 | tf_op jit(solution)/shard_map/ppermute | solution.py:377
  83.0 22.4 %copy-start.6 = (bf16[512,1024]{1,0:T(8,128)(2,1)S(1)}, bf16[512,1024]{1,0:T(8,128)(2,1)}, u32[]{:S(2)}) copy-start(bf16[512,1024]{1,0:T(8,128)(2,1)} %constant.63.clone.rest_9_) | copy-start | bytes 3145732
  83.0 22.4 %copy-start.7 = (bf16[512,1024]{1,0:T(8,128)(2,1)S(1)}, bf16[512,1024]{1,0:T(8,128)(2,1)}, u32[]{:S(2)}) copy-start(bf16[512,1024]{1,0:T(8,128)(2,1)} %constant.62.clone.rest_8_) | copy-start | bytes 3145732
  83.1 6.5 %collective-permute-start.18 = (f32[18,16,128]{2,1,0:T(8,128)S(1)}, f32[18,16,128]{2,1,0:T(8,128)S(1)}, u32[]{:S(2)}, u32[]{:S(2)}) collective-permute-start(f32[18,16,128]{2,1,0:T(8,128)S(1)} %get-tuple-element.48), channel_id=1, source_target_pairs={{0,6},{1,7},{2,4},{3,5},{4,2},{5,3},{6,0},{7,1},{8,14},{9,15},{10,... | collective-permute-start | bytes 442376 | tf_op jit(solution)/shard_map/ppermute | solution.py:377
  84.7 8.4 %collective-permute-start.19 = (f32[18,16,128]{2,1,0:T(8,128)S(1)}, f32[18,16,128]{2,1,0:T(8,128)S(1)}, u32[]{:S(2)}, u32[]{:S(2)}) collective-permute-start(f32[18,16,128]{2,1,0:T(8,128)S(1)} %get-tuple-element.49), channel_id=1, source_target_pairs={{0,7},{1,6},{2,5},{3,4},{4,3},{5,2},{6,1},{7,0},{8,15},{9,14},{10,... | collective-permute-start | bytes 442376 | tf_op jit(solution)/shard_map/ppermute | solution.py:377
  85.5 9.0 %collective-permute-start.6 = (f32[18,16,128]{2,1,0:T(8,128)S(1)}, f32[18,16,128]{2,1,0:T(8,128)S(1)}, u32[]{:S(2)}, u32[]{:S(2)}) collective-permute-start(f32[18,16,128]{2,1,0:T(8,128)S(1)} %get-tuple-element.35), channel_id=1, source_target_pairs={{0,1},{1,0},{2,3},{3,2},{4,5},{5,4},{6,7},{7,6},{8,9},{9,8},{10,11... | collective-permute-start | bytes 442376 | tf_op jit(solution)/shard_map/ppermute | solution.py:377
  85.9 10.3 %collective-permute-start.7 = (f32[18,16,128]{2,1,0:T(8,128)S(1)}, f32[18,16,128]{2,1,0:T(8,128)S(1)}, u32[]{:S(2)}, u32[]{:S(2)}) collective-permute-start(f32[18,16,128]{2,1,0:T(8,128)S(1)} %get-tuple-element.36), channel_id=1, source_target_pairs={{0,2},{1,3},{2,0},{3,1},{4,6},{5,7},{6,4},{7,5},{8,10},{9,11},{10,... | collective-permute-start | bytes 442376 | tf_op jit(solution)/shard_map/ppermute | solution.py:377
  86.4 15.9 %collective-permute-start.8 = (f32[18,16,128]{2,1,0:T(8,128)S(1)}, f32[18,16,128]{2,1,0:T(8,128)S(1)}, u32[]{:S(2)}, u32[]{:S(2)}) collective-permute-start(f32[18,16,128]{2,1,0:T(8,128)S(1)} %get-tuple-element.37), channel_id=1, source_target_pairs={{0,3},{1,2},{2,1},{3,0},{4,7},{5,6},{6,5},{7,4},{8,11},{9,10},{10,... | collective-permute-start | bytes 442376 | tf_op jit(solution)/shard_map/ppermute | solution.py:377
  89.6 12.8 %collective-permute-start.9 = (f32[18,16,128]{2,1,0:T(8,128)S(1)}, f32[18,16,128]{2,1,0:T(8,128)S(1)}, u32[]{:S(2)}, u32[]{:S(2)}) collective-permute-start(f32[18,16,128]{2,1,0:T(8,128)S(1)} %get-tuple-element.38), channel_id=1, source_target_pairs={{0,4},{1,5},{2,6},{3,7},{4,0},{5,1},{6,2},{7,3},{8,12},{9,13},{10,... | collective-permute-start | bytes 442376 | tf_op jit(solution)/shard_map/ppermute | solution.py:377
  93.1 9.3 %collective-permute-start.10 = (f32[18,16,128]{2,1,0:T(8,128)S(1)}, f32[18,16,128]{2,1,0:T(8,128)S(1)}, u32[]{:S(2)}, u32[]{:S(2)}) collective-permute-start(f32[18,16,128]{2,1,0:T(8,128)S(1)} %get-tuple-element.39), channel_id=1, source_target_pairs={{0,5},{1,4},{2,7},{3,6},{4,1},{5,0},{6,3},{7,2},{8,13},{9,12},{10,... | collective-permute-start | bytes 442376 | tf_op jit(solution)/shard_map/ppermute | solution.py:377
  94.5 7.9 %collective-permute-start.11 = (f32[18,16,128]{2,1,0:T(8,128)S(1)}, f32[18,16,128]{2,1,0:T(8,128)S(1)}, u32[]{:S(2)}, u32[]{:S(2)}) collective-permute-start(f32[18,16,128]{2,1,0:T(8,128)S(1)} %get-tuple-element.40), channel_id=1, source_target_pairs={{0,6},{1,7},{2,4},{3,5},{4,2},{5,3},{6,0},{7,1},{8,14},{9,15},{10,... | collective-permute-start | bytes 442376 | tf_op jit(solution)/shard_map/ppermute | solution.py:377
  96.2 9.2 %collective-permute-start.12 = (f32[18,16,128]{2,1,0:T(8,128)S(1)}, f32[18,16,128]{2,1,0:T(8,128)S(1)}, u32[]{:S(2)}, u32[]{:S(2)}) collective-permute-start(f32[18,16,128]{2,1,0:T(8,128)S(1)} %get-tuple-element.41), channel_id=1, source_target_pairs={{0,7},{1,6},{2,5},{3,4},{4,3},{5,2},{6,1},{7,0},{8,15},{9,14},{10,... | collective-permute-start | bytes 442376 | tf_op jit(solution)/shard_map/ppermute | solution.py:377
